TPU v7x, 32 devices: a whole 2x2x4 slice. The times are simulated.
32 devices in a mesh: row: 8 (over z, core), col: 4 (over y, x).
Axes of the slice: x: 2, y: 2, z: 4, core: 2. Of those that a mesh axis runs over, the one named last changes fastest.
Arguments:
- raw_amps: float32 [2048, 3072], P('row', 'col'), may hold values from -24 to 24
- integrals: float32 [3072, 2048], P('row', 'col'), may hold values from -0.109375 to 0.109375
- occ_energy: float32 [256], replicated, may hold values from -2 to -0.5
- vir_energy: float32 [2048], replicated, may hold values from 0.5 to 3
- occ_pairs: int32 [2048, 2], P('row'), may hold values from 0 to 255
- vir_pairs: int32 [3072, 2], replicated, may hold values from 0 to 2047
- pair_order: int32 [3072], replicated, may hold values from 0 to 3071, each once
Outputs:
- residual: float32 [2048, 2048], P('row', 'col')
Inputs may be any that keep to these rules, and one draw needn't show every extreme that they name: `pair_order`: each column index appears exactly once.
All inputs are finite; a program needn't handle non-finite values.
Results may differ from a plain program's by a relative error of at most 0.000068.
Values sent between devices are 32-bit elements; how exact they have to be, the bound alone decides.
No kernel may reach another device: no remote copies, remote signals or barrier semaphores. Data moves between devices by JAX's collectives and lax.ppermute only.
A program may use at most 64 MiB of HBM per device.

v0:
```python
import jax
import jax.numpy as jnp
from jax import lax
from jax.sharding import PartitionSpec as P


def on_device(raw_amps, integrals, occ_energy, vir_energy, occ_pairs, vir_pairs, pair_order):
    width = raw_amps.shape[1]
    col_start = lax.axis_index("col") * width
    local_pairs = lax.dynamic_slice_in_dim(vir_pairs, col_start, width, 0)
    occ_sum = occ_energy[occ_pairs[:, 0]] + occ_energy[occ_pairs[:, 1]]
    vir_sum = vir_energy[local_pairs[:, 0]] + vir_energy[local_pairs[:, 1]]
    scaled = raw_amps / (vir_sum[None, :] - occ_sum[:, None])
    gathered = lax.all_gather(scaled, "col", axis=1, tiled=True)
    ordered = jnp.take(gathered, pair_order, axis=1)
    return jnp.dot(
        ordered,
        lax.all_gather(integrals, "row", axis=0, tiled=True),
        preferred_element_type=jnp.float32,
        precision=lax.Precision.HIGHEST,
    )


def solution(mesh):
    placed = (P("row", "col"), P("row", "col"), P(), P(), P("row", None), P(), P())
    return jax.shard_map(
        on_device, mesh=mesh, in_specs=placed, out_specs=P("row", "col"), check_vma=False
    )
```

profile of v0, /device:TPU:0, one launch (start us, length us, event | category | flops | bytes accessed | tf_op | source)
XLA Modules:
  0.0 151.5 jit_solution(18051002545509406550)
XLA Ops:
  6.5 0.0 copy-start
  6.5 0.0 all-gather.3.cloned.1.call-start
  6.5 0.9 fusion.6
  7.4 0.0 copy-done
  7.4 4.5 %gather_fusion = f32[768]{0:T(1024)S(1)} fusion(f32[2048]{0:T(1024)S(1)} %copy-done, s32[1024]{0:T(1024)S(1)} %get-tuple-element.10), kind=kCustom, calls=%fused_computation | custom fusion | bytes 9216 | tf_op jit(solution)/shard_map/gather | solution.py:12
  11.9 0.0 copy-start.4
  11.9 0.0 copy-start.1
  11.9 0.0 copy-start.2
  11.9 4.5 %gather_fusion.1 = f32[768]{0:T(1024)S(1)} fusion(f32[2048]{0:T(1024)S(1)} %copy-done, s32[1024]{0:T(1024)S(1)} %get-tuple-element.9), kind=kCustom, calls=%fused_computation.1 | custom fusion | bytes 9216 | tf_op jit(solution)/shard_map/gather | solution.py:12
  16.4 0.0 copy-done.4
  16.5 0.0 copy-done.1
  16.5 1.9 %gather_fusion.2 = f32[256]{0:T(256)S(1)} fusion(f32[256]{0:T(256)S(1)} %copy-done.1, s32[1024]{0:T(1024)S(1)} %pad_clamp_fusion.1), kind=kCustom, calls=%fused_computation.2 | custom fusion | bytes 3072 | tf_op jit(solution)/shard_map/gather | solution.py:11
  18.4 0.0 copy-start.3
  18.4 1.9 %gather_fusion.3 = f32[256]{0:T(256)S(1)} fusion(f32[256]{0:T(256)S(1)} %copy-done.1, s32[1024]{0:T(1024)S(1)} %pad_clamp_fusion), kind=kCustom, calls=%fused_computation.3 | custom fusion | bytes 3072 | tf_op jit(solution)/shard_map/gather | solution.py:11
  20.4 0.0 copy-done.2
  20.4 0.3 copy.9
  20.7 1.1 subtract_divide_fusion
  21.7 0.0 all-gather.3.cloned.1.call-update
  21.8 0.0 all-gather.5.cloned.1.call-start
  21.8 0.7 all-gather.5.cloned.1.call-update
  22.5 0.0 copy-done.3
  22.6 46.0 %all-gather.3.cloned.1.call-done = f32[256,3072]{0,1:T(8,128)} async-done(((f32[256,768]{0,1:T(8,128)}), f32[256,3072]{0,1:T(8,128)}) %all-gather.3.cloned.1.call-update) | async-done | bytes 3145744 | tf_op jit(solution)/shard_map/all_gather | solution.py:14
  68.6 11.7 %gather_fusion.4 = f32[3072,256]{1,0:T(8,128)S(1)} fusion(f32[256,3072]{0,1:T(8,128)} %all-gather.3.cloned.1.call-done, s32[3072]{0:T(1024)S(1)} %fusion.4), kind=kCustom, calls=%fused_computation.4 | custom fusion | bytes 6303744 | tf_op jit(solution)/shard_map/jit(_take)/gather | solution.py:15
  80.3 54.7 %all-gather.5.cloned.1.call-done = f32[3072,512]{1,0:T(8,128)} async-done(((f32[384,512]{1,0:T(8,128)}), f32[3072,512]{1,0:T(8,128)}) %all-gather.5.cloned.1.call-update) | async-done | bytes 6291472 | tf_op jit(solution)/shard_map/all_gather | solution.py:18
  135.0 9.6 %fusion = f32[256,512]{1,0:T(8,128)} fusion(f32[3072,512]{1,0:T(8,128)} %all-gather.5.cloned.1.call-done, f32[3072,256]{1,0:T(8,128)S(1)} %gather_fusion.4, pred[3072]{0:T(1024)(128)(4,1)S(1)} %compare_and_fusion), kind=kOutput, calls=%fused_computation.5 | convolution fusion | flops 4832624640 | bytes 9964544 | tf_op jit(solution)/shard_map/dot_general | solution.py:16
  (8 shorter events, 0.0 us)
Async XLA Ops:
  6.5 0.9 copy-start
  6.5 62.1 %all-gather.3.cloned.1.call-start = ((), (), s32[]{:S(2)}) async-start(), calls=%async_computation | async-start | bytes 3932160 | tf_op jit(solution)/shard_map/all_gather | solution.py:14
  11.9 4.5 %copy-start.4 = (s32[256,2]{0,1:T(2,128)S(1)}, s32[256,2]{0,1:T(2,128)}, u32[]{:S(2)}) copy-start(s32[256,2]{0,1:T(2,128)} %param.11) | copy-start | bytes 6148
  11.9 4.5 %copy-start.1 = (f32[256]{0:T(256)S(1)}, f32[256]{0:T(256)}, u32[]{:S(2)}) copy-start(f32[256]{0:T(256)} %param.9) | copy-start | bytes 3076
  11.9 8.5 %copy-start.2 = (f32[256,768]{1,0:T(8,128)S(1)}, f32[256,768]{1,0:T(8,128)}, u32[]{:S(2)}) copy-start(f32[256,768]{1,0:T(8,128)} %param.7) | copy-start | bytes 2359300
  18.4 4.1 %copy-start.3 = (s32[3072]{0:T(1024)S(1)}, s32[3072]{0:T(1024)}, u32[]{:S(2)}) copy-start(s32[3072]{0:T(1024)} %param.13) | copy-start | bytes 36868
  21.8 113.3 %all-gather.5.cloned.1.call-start = ((), (), s32[]{:S(2)}) async-start(), calls=%async_computation.1 | async-start | bytes 7077888 | tf_op jit(solution)/shard_map/all_gather | solution.py:18
Sparse Core Ops, SparseCore 0:
  21.9 46.6 all-gather.2
  70.2 64.7 all-gather.4
where the time goes:
time: 152 us; the launch traced here: 151 us
  waiting for transfers between devices  101 us (66%)
  local copies, waits for them, and re-layouts  24.8 us (16%)
  between operations  13.6 us (9%)
  matrix products  9.6 us (6%)
  other arithmetic  1.96 us (1%)
    all_gather x1, waiting for transfers between devices, on_device(): lax.all_gather(integrals, 'row', axis=0, tiled=True)  54.7 us
    all_gather x1, waiting for transfers between devices, on_device(): gathered = lax.all_gather(scaled, 'col', axis=1, tiled=True)  46 us
    gather x1, local copies, waits for them, and re-layouts, on_device(): ordered = jnp.take(gathered, pair_order, axis=1)  11.7 us
    dot_general x1, matrix products, on_device(): jnp.dot(ordered, lax.all_gather(integrals, 'row', axis=0, tiled=True), pr...  9.6 us
    gather x2, local copies, waits for them, and re-layouts, on_device(): vir_sum = vir_energy[local_pairs[:, 0]] + vir_energy[local_pairs[:, 1]]  8.93 us
    gather x2, local copies, waits for them, and re-layouts, on_device(): occ_sum = occ_energy[occ_pairs[:, 0]] + occ_energy[occ_pairs[:, 1]]  3.89 us
  transfers between devices with their start and end apart: 2, of which 2 were waited for; matrix products, arithmetic and copies ran while one was open for 8% of the time, Pallas kernels for 0%

commit v1 on v0

v1 whole, which is shorter than its diff:
```python
import functools

import jax
import jax.numpy as jnp
from jax import lax
from jax.experimental import pallas as pl
from jax.experimental.pallas import tpu as pltpu
from jax.sharding import PartitionSpec as P

LANES = 128
VMEM = pl.BlockSpec(memory_space=pltpu.VMEM)
SMEM = pl.BlockSpec(memory_space=pltpu.SMEM)
ANY = pl.BlockSpec(memory_space=pl.ANY)
PARAMS = pltpu.CompilerParams(vmem_limit_bytes=40 * 2**20)


def split(x):
    high = x.astype(jnp.bfloat16)
    return high, (x - high.astype(jnp.float32)).astype(jnp.bfloat16)


def look_up(energy, pairs, sums, column):
    tiles = energy.shape[0]
    for tile in range(tiles):
        column[pl.ds(tile * LANES, LANES), :] = jnp.broadcast_to(energy[tile : tile + 1, :], (LANES, LANES)).T
    width = 2 * LANES

    @pl.loop(0, pairs.shape[1] // width)
    def _(step):
        here = pl.ds(pl.multiple_of(step * width, width), width)
        first = jnp.broadcast_to(pairs[0:1, here], (8, width))
        second = jnp.broadcast_to(pairs[1:2, here], (8, width))
        sublane = lax.broadcasted_iota(jnp.int32, (8, width), 0)

        def add(group, total):
            value = column[pl.ds(pl.multiple_of(group * 8, 8), 8), :]
            value = jnp.concatenate([value, value], axis=1)
            index = sublane + group * 8
            return total + (jnp.where(index == first, value, 0.0) + jnp.where(index == second, value, 0.0))

        total = lax.fori_loop(0, tiles * (LANES // 8), add, jnp.zeros((8, width), jnp.float32), unroll=16)
        sums[0:1, here] = jnp.sum(total, axis=0, keepdims=True)


def energy_kernel(occ, vir, occ_pairs, vir_pairs, occ_sum, vir_sum, column):
    look_up(occ, occ_pairs, occ_sum, column)
    look_up(vir, vir_pairs, vir_sum, column)


def energy_sums(occ_energy, vir_energy, occ_pairs, vir_pairs):
    return pl.pallas_call(
        energy_kernel,
        name="energy_sums",
        out_shape=(
            jax.ShapeDtypeStruct((1, occ_pairs.shape[0]), jnp.float32),
            jax.ShapeDtypeStruct((1, vir_pairs.shape[0]), jnp.float32),
        ),
        scratch_shapes=[pltpu.VMEM((max(vir_energy.shape[0], occ_energy.shape[0]), LANES), jnp.float32)],
        compiler_params=PARAMS,
    )(occ_energy.reshape(-1, LANES), vir_energy.reshape(-1, LANES), occ_pairs.T, vir_pairs.T)


def divide_transposed(raw, occ_sum, vir_sum, vir_start, out, out_start):
    rows, width = raw.shape
    step = 2 * LANES if width % (2 * LANES) == 0 else LANES
    for start in range(0, width, step):
        vir = vir_sum[0:1, pl.ds(pl.multiple_of(vir_start + start, LANES), step)]
        vir = jnp.broadcast_to(vir, (LANES, step)).T
        vir = jnp.concatenate([vir] * (rows // LANES), axis=1)
        out[pl.ds(out_start + start, step), :] = raw[:, start : start + step].T / (vir - occ_sum[0:1, :])


def divide_kernel(count, starts, occ_sum, vir_sum, *refs):
    out = refs[count]
    width = refs[0].shape[1]
    for block in range(count):
        divide_transposed(refs[block], occ_sum, vir_sum, starts[block], out, block * width)


def divided(starts, occ_sum, vir_sum, *blocks):
    rows, width = blocks[0].shape
    return pl.pallas_call(
        functools.partial(divide_kernel, len(blocks)),
        name="divided",
        in_specs=[SMEM] + [VMEM] * (2 + len(blocks)),
        out_shape=jax.ShapeDtypeStruct((width * len(blocks), rows), jnp.float32),
        compiler_params=PARAMS,
    )(starts, occ_sum, vir_sum, *blocks)


def order_kernel(chunk, row_of, starts, bases, occ_sum, vir_sum, done, raw, high, low, held, rows, sem):
    size = done.shape[0]
    copy = pltpu.make_async_copy(done, held.at[pl.ds(0, size)], sem)
    copy.start()
    divide_transposed(raw, occ_sum, vir_sum, starts[starts.shape[0] - 1], held, size)
    copy.wait()
    per_block = high.shape[0] // bases.shape[0] // chunk

    @pl.loop(0, high.shape[0] // chunk)
    def _(step):
        base = bases[step // per_block] + (step % per_block) * chunk
        for row in range(chunk):
            rows[pl.ds(row, 1), :] = held[pl.ds(row_of[base + row], 1), :]
        here = pl.ds(pl.multiple_of(step * chunk, chunk), chunk)
        high[here, :], low[here, :] = split(rows[...])


def in_order(row_of, starts, bases, occ_sum, vir_sum, done, raw):
    pairs, rows = row_of.shape[0], raw.shape[0]
    chunk = LANES
    return pl.pallas_call(
        functools.partial(order_kernel, chunk),
        name="in_order",
        in_specs=[SMEM, SMEM, SMEM, VMEM, VMEM, ANY, VMEM],
        out_shape=(jax.ShapeDtypeStruct((pairs, rows), jnp.bfloat16),) * 2,
        scratch_shapes=[
            pltpu.VMEM((pairs, rows), jnp.float32),
            pltpu.VMEM((chunk, rows), jnp.float32),
            pltpu.SemaphoreType.DMA,
        ],
        compiler_params=PARAMS,
    )(row_of, starts, bases, occ_sum, vir_sum, done, raw)


def product(high, low, block):
    dot = functools.partial(
        lax.dot_general, dimension_numbers=(((0,), (0,)), ((), ())), preferred_element_type=jnp.float32
    )
    block_high, block_low = split(block)
    return dot(high, block_high) + (dot(high, block_low) + dot(low, block_high))


def product_kernel(count, has_total, high, low, *refs):
    blocks, refs = refs[:count], refs[count:]
    out, held, sems = refs[-3:]
    copies = [pltpu.make_async_copy(blocks[i], held.at[i], sems.at[i]) for i in range(count)]
    for copy in copies:
        copy.start()
    depth = held.shape[1]
    if has_total:
        out[...] = refs[0][...]
    else:
        out[...] = jnp.zeros_like(out)
    for i in range(count):
        copies[i].wait()
        here = pl.ds(i * depth, depth)
        out[...] += product(high[here, :], low[here, :], held[i])


def summed(high, low, part, blocks, total=None):
    depth, columns = blocks[0].shape
    count, rows = len(blocks), high.shape[1]
    ours = pl.BlockSpec((depth * count, rows), lambda i: (part, 0))
    whole = pl.BlockSpec((rows, columns), lambda i: (0, 0))
    return pl.pallas_call(
        functools.partial(product_kernel, count, total is not None),
        name="summed",
        grid=(1,),
        in_specs=[ours, ours] + [ANY] * count + ([whole] if total is not None else []),
        out_specs=whole,
        out_shape=jax.ShapeDtypeStruct((rows, columns), jnp.float32),
        scratch_shapes=[pltpu.VMEM((count, depth, columns), jnp.float32), pltpu.SemaphoreType.DMA((count,))],
        compiler_params=PARAMS,
    )(high, low, *blocks, *([total] if total is not None else []))


def four_chips_each(raw_amps, integrals, occ_energy, vir_energy, occ_pairs, vir_pairs, pair_order):
    row, col = lax.axis_index("row"), lax.axis_index("col")
    chip, core = row // 2, row % 2
    width, depth = raw_amps.shape[1], integrals.shape[0]

    def between_chips(block, pairs):
        return lax.ppermute(block, "row", [(2 * a + c, 2 * b + c) for a, b in pairs for c in range(2)])

    def other_core(block):
        return lax.ppermute(block, "row", [(i, i ^ 1) for i in range(8)])

    next_chip = between_chips(integrals, [(0, 1), (1, 0), (2, 3), (3, 2)])
    second_chip = between_chips(integrals, [(0, 2), (2, 0), (1, 3), (3, 1)])
    raw = [raw_amps] + [lax.ppermute(raw_amps, "col", [(i, i ^ m) for i in range(4)]) for m in (1, 2, 3)]
    far = between_chips(second_chip, [(1, 0), (2, 3)])
    middle = between_chips(integrals, [(1, 2), (2, 1)])
    third_chip = jnp.where((chip == 0) | (chip == 3), far, middle)

    occ_sum, vir_sum = energy_sums(occ_energy, vir_energy, occ_pairs, vir_pairs)
    starts = (col ^ jnp.arange(4, dtype=jnp.int32)) * width
    row_of = ((pair_order // width) ^ col) * width + pair_order % width
    bases = jnp.stack([((chip ^ m) * 2 + (core ^ s)) * depth for m in range(4) for s in range(2)])
    done = divided(starts[:3], occ_sum, vir_sum, *raw[:3])
    high, low = in_order(row_of, starts, bases, occ_sum, vir_sum, done, raw[3])

    blocks = []
    for block in (integrals, next_chip, second_chip):
        blocks += [block, other_core(block)]
    total = summed(high, low, 0, blocks)
    return summed(high, low, 3, [third_chip, other_core(third_chip)], total)


def any_mesh(raw_amps, integrals, occ_energy, vir_energy, occ_pairs, vir_pairs, pair_order):
    occ_sum, vir_sum = energy_sums(occ_energy, vir_energy, occ_pairs, vir_pairs)
    raw = lax.all_gather(raw_amps, "col", axis=1, tiled=True)
    half = raw.shape[1] // 2
    starts = jnp.arange(2, dtype=jnp.int32) * half
    done = divided(starts[:1], occ_sum, vir_sum, raw[:, :half])
    bases = jnp.zeros(1, jnp.int32)
    high, low = in_order(pair_order, starts, bases, occ_sum, vir_sum, done, raw[:, half:])
    return summed(high, low, 0, [lax.all_gather(integrals, "row", axis=0, tiled=True)])


def solution(mesh):
    placed = (P("row", "col"), P("row", "col"), P(), P(), P("row", None), P(), P())
    on_device = four_chips_each if (mesh.shape["row"], mesh.shape["col"]) == (8, 4) else any_mesh
    return jax.shard_map(
        on_device, mesh=mesh, in_specs=placed, out_specs=P("row", "col"), check_vma=False
    )
```

time: 152 us -> 104 us (0.68)
  the two profiles are of different devices: /device:TPU:0 before, /device:TPU:17 now
where the time goes in v1:
time: 104 us
  waiting for transfers between devices  55.5 us (53%)
  Pallas kernels  23.7 us (23%)
  starting transfers between devices  21 us (20%)
  local copies, waits for them, and re-layouts  2.13 us (2%)
  other arithmetic  1.3 us (1%)
    ppermute x4, waiting for transfers between devices, between_chips(): lax.ppermute(block, 'row', [(2 * a + c, 2 * b + c) for a, b in pairs for...  38.2 us
    ppermute x3, waiting for transfers between devices, four_chips_each(): lax.ppermute(raw_amps, 'col', [(i, i ^ m) for i in range(4)])  17.2 us
    ppermute x4, starting transfers between devices, between_chips(): lax.ppermute(block, 'row', [(2 * a + c, 2 * b + c) for a, b in pairs for...  12.2 us
    pallas_call x1, Pallas kernels, in_order(): pl.pallas_call(functools.partial(order_kernel, chunk), name='in_order', i...  8.03 us
    pallas_call x1, Pallas kernels, energy_sums(): pl.pallas_call(energy_kernel, name='energy_sums', out_shape=(jax.ShapeDty...  7.08 us
    pallas_call x2, Pallas kernels, summed(): pl.pallas_call(functools.partial(product_kernel, count, total is not None...  6.48 us
    ppermute x4, starting transfers between devices, other_core(): return lax.ppermute(block, 'row', [(i, i ^ 1) for i in range(8)])  5.13 us
    ppermute x3, starting transfers between devices, four_chips_each(): lax.ppermute(raw_amps, 'col', [(i, i ^ m) for i in range(4)])  3.62 us
  transfers between devices with their start and end apart: 11, of which 4 were waited for; matrix products, arithmetic and copies ran while one was open for 1% of the time, Pallas kernels for 20%

profile of v1, /device:TPU:17, one launch (start us, length us, event | category | flops | bytes accessed | tf_op | source)
XLA Modules:
  0.0 103.8 jit_solution(1365310578519628934)
XLA Ops:
  0.0 0.1 collective-permute-start.3
  0.1 1.3 %collective-permute-start = (f32[256,768]{1,0:T(8,128)}, f32[256,768]{1,0:T(8,128)S(1)}, u32[]{:S(2)}, u32[]{:S(2)}) collective-permute-start(f32[256,768]{1,0:T(8,128)} %refs_0_.2), channel_id=1, source_target_pairs={{0,1},{1,0},{2,3},{3,2},{4,5},{5,4},{6,7},{7,6},{8,9},{9,8},{10,11... | collective-permute-start | bytes 2359304 | tf_op jit(solution)/shard_map/ppermute | solution.py:180
  1.4 1.3 %collective-permute-start.8 = (f32[384,512]{1,0:T(8,128)}, f32[384,512]{1,0:T(8,128)S(1)}, u32[]{:S(2)}, u32[]{:S(2)}) collective-permute-start(f32[384,512]{1,0:T(8,128)} %refs_0_.3), channel_id=1, source_target_pairs={{0,8},{4,12},{8,0},{12,4},{16,24},{20,28},{24,16},{28,20},{1,9},{5... | collective-permute-start | bytes 2359304 | tf_op jit(solution)/shard_map/ppermute | solution.py:173
  2.7 3.2 %collective-permute-start.5 = (f32[384,512]{1,0:T(8,128)}, f32[384,512]{1,0:T(8,128)}, u32[]{:S(2)}, u32[]{:S(2)}) collective-permute-start(f32[384,512]{1,0:T(8,128)} %refs_0_.3), channel_id=1, source_target_pairs={{8,16},{12,20},{16,8},{20,12},{9,17},{13,21},{17,9},{21,13},{10,18... | collective-permute-start | bytes 2359304 | tf_op jit(solution)/shard_map/ppermute | solution.py:173
  5.9 28.0 %collective-permute-done.3.refs_4_ = f32[384,512]{1,0:T(8,128)S(1)} collective-permute-done((f32[384,512]{1,0:T(8,128)}, f32[384,512]{1,0:T(8,128)S(1)}, u32[]{:S(2)}, u32[]{:S(2)}) %collective-permute-start.3) | collective-permute-done | bytes 786464 | tf_op jit(solution)/shard_map/ppermute | solution.py:173
  33.9 7.7 %collective-permute-start.4 = (f32[384,512]{1,0:T(8,128)S(1)}, f32[384,512]{1,0:T(8,128)}, u32[]{:S(2)}, u32[]{:S(2)}) collective-permute-start(f32[384,512]{1,0:T(8,128)S(1)} %collective-permute-done.3.refs_4_), channel_id=1, source_target_pairs={{8,0},{12,4},{16,24},{20,28},{9,1},{13,5},{17,25},{21,29},{10,2},{... | collective-permute-start | bytes 2359304 | tf_op jit(solution)/shard_map/ppermute | solution.py:173
  41.6 1.2 %collective-permute-start.1 = (f32[256,768]{1,0:T(8,128)}, f32[256,768]{1,0:T(8,128)}, u32[]{:S(2)}, u32[]{:S(2)}) collective-permute-start(f32[256,768]{1,0:T(8,128)} %refs_0_.2), channel_id=1, source_target_pairs={{0,2},{1,3},{2,0},{3,1},{4,6},{5,7},{6,4},{7,5},{8,10},{9,11},{10,... | collective-permute-start | bytes 2359304 | tf_op jit(solution)/shard_map/ppermute | solution.py:180
  42.8 0.0 collective-permute-done.refs_1_
  42.8 0.9 copy-done.2
  43.7 1.1 %collective-permute-start.2 = (f32[256,768]{1,0:T(8,128)}, f32[256,768]{1,0:T(8,128)}, u32[]{:S(2)}, u32[]{:S(2)}) collective-permute-start(f32[256,768]{1,0:T(8,128)} %refs_0_.2), channel_id=1, source_target_pairs={{0,3},{1,2},{2,1},{3,0},{4,7},{5,6},{6,5},{7,4},{8,11},{9,10},{10,... | collective-permute-start | bytes 2359304 | tf_op jit(solution)/shard_map/ppermute | solution.py:180
  44.8 0.0 collective-permute-done.8.refs_2_
  44.8 1.4 %collective-permute-start.7 = (f32[384,512]{1,0:T(8,128)}, f32[384,512]{1,0:T(8,128)}, u32[]{:S(2)}, u32[]{:S(2)}) collective-permute-start(f32[384,512]{1,0:T(8,128)} %refs_0_.3), channel_id=1, source_target_pairs={{0,4},{4,0},{8,12},{12,8},{16,20},{20,16},{24,28},{28,24},{1,5},{5... | collective-permute-start | bytes 2359304 | tf_op jit(solution)/shard_map/ppermute | solution.py:176
  46.2 8.3 %collective-permute-done.5 = f32[384,512]{1,0:T(8,128)} collective-permute-done((f32[384,512]{1,0:T(8,128)}, f32[384,512]{1,0:T(8,128)}, u32[]{:S(2)}, u32[]{:S(2)}) %collective-permute-start.5) | collective-permute-done | bytes 786464 | tf_op jit(solution)/shard_map/ppermute | solution.py:173
  54.5 0.5 collective-permute-start.10
  55.0 1.9 %collective-permute-done.4 = f32[384,512]{1,0:T(8,128)} collective-permute-done((f32[384,512]{1,0:T(8,128)S(1)}, f32[384,512]{1,0:T(8,128)}, u32[]{:S(2)}, u32[]{:S(2)}) %collective-permute-start.4) | collective-permute-done | bytes 786464 | tf_op jit(solution)/shard_map/ppermute | solution.py:173
  57.0 1.4 %collective-permute-start.9 = (f32[384,512]{1,0:T(8,128)S(1)}, f32[384,512]{1,0:T(8,128)}, u32[]{:S(2)}, u32[]{:S(2)}) collective-permute-start(f32[384,512]{1,0:T(8,128)S(1)} %collective-permute-done.8.refs_2_), channel_id=1, source_target_pairs={{0,4},{4,0},{8,12},{12,8},{16,20},{20,16},{24,28},{28,24},{1,5},{5... | collective-permute-start | bytes 2359304 | tf_op jit(solution)/shard_map/ppermute | solution.py:176
  58.4 1.3 %broadcast_select_fusion.refs_0_ = f32[384,512]{1,0:T(8,128)S(1)} fusion(f32[384,512]{1,0:T(8,128)} %collective-permute-done.4, f32[384,512]{1,0:T(8,128)} %collective-permute-done.5, pred[]{:T(512)S(6)} %or.3), kind=kLoop, calls=%fused_computation | loop fusion | flops 196608 | bytes 2359297 | tf_op jit(solution)/shard_map/jit(_where)/select_n | solution.py:183
  59.7 17.2 %collective-permute-done.1.refs_2_ = f32[256,768]{1,0:T(8,128)} collective-permute-done((f32[256,768]{1,0:T(8,128)}, f32[256,768]{1,0:T(8,128)}, u32[]{:S(2)}, u32[]{:S(2)}) %collective-permute-start.1) | collective-permute-done | bytes 786464 | tf_op jit(solution)/shard_map/ppermute | solution.py:180
  76.9 1.8 %collective-permute-start.6 = (f32[384,512]{1,0:T(8,128)S(1)}, f32[384,512]{1,0:T(8,128)}, u32[]{:S(2)}, u32[]{:S(2)}) collective-permute-start(f32[384,512]{1,0:T(8,128)S(1)} %broadcast_select_fusion.refs_0_), channel_id=1, source_target_pairs={{0,4},{4,0},{8,12},{12,8},{16,20},{20,16},{24,28},{28,24},{1,5},{5... | collective-permute-start | bytes 2359304 | tf_op jit(solution)/shard_map/ppermute | solution.py:176
  78.7 7.1 %energy_sums.1 = (f32[1,256]{1,0:T(1,128)S(1)}, f32[1,3072]{1,0:T(1,128)S(1)}) custom-call(f32[2,128]{1,0:T(2,128)S(1)} %bitcast.17, f32[16,128]{1,0:T(8,128)S(1)} %bitcast.14, s32[2,256]{1,0:T(2,128)S(1)} %bitcast.15, s32[2,3072]{1,0:T(2,128)S(1)} %bitcast.13), custom_call_target="tpu_custom_call" | custom-call | tf_op jit(solution)/shard_map/energy_sums/pallas_call | solution.py:51
  85.8 0.1 stack.35.bases
  85.9 1.1 %copy-done.3 = f32[256,768]{1,0:T(8,128)S(1)} copy-done((f32[256,768]{1,0:T(8,128)S(1)}, f32[256,768]{1,0:T(8,128)}, u32[]{:S(2)}) %copy-start.3) | copy-done | bytes 786456
  87.1 2.1 %divided.1.done = f32[2304,256]{1,0:T(8,128)S(1)} custom-call(s32[3]{0:T(128)S(1)} %bitcast.16, f32[1,256]{1,0:T(1,128)S(1)} %get-tuple-element.9.occ_sum, f32[1,3072]{1,0:T(1,128)S(1)} %get-tuple-element.10.vir_sum, f32[256,768]{1,0:T(8,128)S(1)} %copy-done, f32[256,768]{1,0:T(8,128)S(1)} %copy-done.3, f32[256,768]{1,0:T(8,128)} %collective-permute-done.1.refs_2_), custom_call_target="tpu_custom_call" | custom-call | tf_op jit(solution)/shard_map/divided/pallas_call | solution.py:82
  89.2 0.0 copy-start.1
  89.2 0.0 collective-permute-done.2.raw
  89.2 8.0 %in_order.1 = (bf16[3072,256]{1,0:T(8,128)(2,1)S(1)}, bf16[3072,256]{1,0:T(8,128)(2,1)S(1)}) custom-call(s32[3072]{0:T(1024)S(1)} %fusion.2.row_of, s32[4]{0:T(128)S(1)} %xor_multiply_fusion.starts, s32[8]{0:T(128)S(1)} %stack.35.bases, f32[1,256]{1,0:T(1,128)S(1)} %get-tuple-element.9.occ_sum, f32[1,3072]{1,0:T(1,128)S(1)} %get-tuple-element.10.vir_sum, ...), custom_call_target="tpu_custom_call" | custom-call | tf_op jit(solution)/shard_map/in_order/pallas_call | solution.py:111
  97.2 0.0 collective-permute-done.7.refs_1_
  97.3 0.0 collective-permute-done.10.refs_5_
  97.3 0.0 collective-permute-done.9.refs_3_
  97.3 3.9 %summed.2.refs_2_ = f32[256,512]{1,0:T(8,128)S(1)} custom-call(bf16[3072,256]{1,0:T(8,128)(2,1)S(1)} %get-tuple-element.11.high, bf16[3072,256]{1,0:T(8,128)(2,1)S(1)} %get-tuple-element.12.low, f32[384,512]{1,0:T(8,128)S(1)} %copy-done.1, f32[384,512]{1,0:T(8,128)} %collective-permute-done.7.refs_1_, f32[384,512]{1,0:T(8,128)S(1)} %collective-permute-done.8.refs_2_, ...), custom_call_target="tpu_custom_call" | custom-call | tf_op jit(solution)/shard_map/summed/pallas_call | solution.py:155
  101.2 0.0 collective-permute-done.6.refs_1_
  101.2 2.6 %summed.3 = f32[256,512]{1,0:T(8,128)} custom-call(bf16[3072,256]{1,0:T(8,128)(2,1)S(1)} %get-tuple-element.11.high, bf16[3072,256]{1,0:T(8,128)(2,1)S(1)} %get-tuple-element.12.low, f32[384,512]{1,0:T(8,128)S(1)} %broadcast_select_fusion.refs_0_, f32[384,512]{1,0:T(8,128)} %collective-permute-done.6.refs_1_, f32[256,512]{1,0:T(8,128)S(1)} %summed.2.refs_2_), custom_call_target="tpu_custom_call" | custom-call | tf_op jit(solution)/shard_map/summed/pallas_call | solution.py:155
  (17 shorter events, 0.1 us)
Async XLA Ops:
  0.0 85.9 %copy-start = (f32[256,768]{1,0:T(8,128)S(1)}, f32[256,768]{1,0:T(8,128)}, u32[]{:S(2)}) copy-start(f32[256,768]{1,0:T(8,128)} %refs_0_.2) | copy-start | bytes 2359300
  0.0 78.7 %copy-start.6 = (s32[256,2]{0,1:T(2,128)S(1)}, s32[256,2]{0,1:T(2,128)}, u32[]{:S(2)}) copy-start(s32[256,2]{0,1:T(2,128)} %param.11) | copy-start | bytes 6148
  0.0 78.7 %copy-start.4 = (s32[3072,2]{0,1:T(2,128)S(1)}, s32[3072,2]{0,1:T(2,128)}, u32[]{:S(2)}) copy-start(s32[3072,2]{0,1:T(2,128)} %param.12) | copy-start | bytes 73732
  0.0 78.7 %copy-start.7 = (f32[256]{0:T(256)S(1)}, f32[256]{0:T(256)}, u32[]{:S(2)}) copy-start(f32[256]{0:T(256)} %param.9) | copy-start | bytes 3076
  0.0 78.7 %copy-start.5 = (f32[2048]{0:T(1024)S(1)}, f32[2048]{0:T(1024)}, u32[]{:S(2)}) copy-start(f32[2048]{0:T(1024)} %param.10) | copy-start | bytes 24580
  0.0 85.8 %copy-start.8 = (s32[3072]{0:T(1024)S(1)}, s32[3072]{0:T(1024)}, u32[]{:S(2)}) copy-start(s32[3072]{0:T(1024)} %param.13) | copy-start | bytes 36868
  0.0 33.8 %collective-permute-start.3 = (f32[384,512]{1,0:T(8,128)}, f32[384,512]{1,0:T(8,128)S(1)}, u32[]{:S(2)}, u32[]{:S(2)}) collective-permute-start(f32[384,512]{1,0:T(8,128)} %refs_0_.3), channel_id=1, source_target_pairs={{0,16},{4,20},{16,0},{20,4},{8,24},{12,28},{24,8},{28,12},{1,17},{... | collective-permute-start | bytes 2359304 | tf_op jit(solution)/shard_map/ppermute | solution.py:173
  0.1 42.7 %collective-permute-start = (f32[256,768]{1,0:T(8,128)}, f32[256,768]{1,0:T(8,128)S(1)}, u32[]{:S(2)}, u32[]{:S(2)}) collective-permute-start(f32[256,768]{1,0:T(8,128)} %refs_0_.2), channel_id=1, source_target_pairs={{0,1},{1,0},{2,3},{3,2},{4,5},{5,4},{6,7},{7,6},{8,9},{9,8},{10,11... | collective-permute-start | bytes 2359304 | tf_op jit(solution)/shard_map/ppermute | solution.py:180
  1.4 43.4 %collective-permute-start.8 = (f32[384,512]{1,0:T(8,128)}, f32[384,512]{1,0:T(8,128)S(1)}, u32[]{:S(2)}, u32[]{:S(2)}) collective-permute-start(f32[384,512]{1,0:T(8,128)} %refs_0_.3), channel_id=1, source_target_pairs={{0,8},{4,12},{8,0},{12,4},{16,24},{20,28},{24,16},{28,20},{1,9},{5... | collective-permute-start | bytes 2359304 | tf_op jit(solution)/shard_map/ppermute | solution.py:173
  2.7 51.8 %collective-permute-start.5 = (f32[384,512]{1,0:T(8,128)}, f32[384,512]{1,0:T(8,128)}, u32[]{:S(2)}, u32[]{:S(2)}) collective-permute-start(f32[384,512]{1,0:T(8,128)} %refs_0_.3), channel_id=1, source_target_pairs={{8,16},{12,20},{16,8},{20,12},{9,17},{13,21},{17,9},{21,13},{10,18... | collective-permute-start | bytes 2359304 | tf_op jit(solution)/shard_map/ppermute | solution.py:173
  33.9 23.1 %collective-permute-start.4 = (f32[384,512]{1,0:T(8,128)S(1)}, f32[384,512]{1,0:T(8,128)}, u32[]{:S(2)}, u32[]{:S(2)}) collective-permute-start(f32[384,512]{1,0:T(8,128)S(1)} %collective-permute-done.3.refs_4_), channel_id=1, source_target_pairs={{8,0},{12,4},{16,24},{20,28},{9,1},{13,5},{17,25},{21,29},{10,2},{... | collective-permute-start | bytes 2359304 | tf_op jit(solution)/shard_map/ppermute | solution.py:173
  41.6 35.4 %collective-permute-start.1 = (f32[256,768]{1,0:T(8,128)}, f32[256,768]{1,0:T(8,128)}, u32[]{:S(2)}, u32[]{:S(2)}) collective-permute-start(f32[256,768]{1,0:T(8,128)} %refs_0_.2), channel_id=1, source_target_pairs={{0,2},{1,3},{2,0},{3,1},{4,6},{5,7},{6,4},{7,5},{8,10},{9,11},{10,... | collective-permute-start | bytes 2359304 | tf_op jit(solution)/shard_map/ppermute | solution.py:180
  42.8 0.9 copy-start.2
  43.7 45.5 %collective-permute-start.2 = (f32[256,768]{1,0:T(8,128)}, f32[256,768]{1,0:T(8,128)}, u32[]{:S(2)}, u32[]{:S(2)}) collective-permute-start(f32[256,768]{1,0:T(8,128)} %refs_0_.2), channel_id=1, source_target_pairs={{0,3},{1,2},{2,1},{3,0},{4,7},{5,6},{6,5},{7,4},{8,11},{9,10},{10,... | collective-permute-start | bytes 2359304 | tf_op jit(solution)/shard_map/ppermute | solution.py:180
  44.8 52.4 %collective-permute-start.7 = (f32[384,512]{1,0:T(8,128)}, f32[384,512]{1,0:T(8,128)}, u32[]{:S(2)}, u32[]{:S(2)}) collective-permute-start(f32[384,512]{1,0:T(8,128)} %refs_0_.3), channel_id=1, source_target_pairs={{0,4},{4,0},{8,12},{12,8},{16,20},{20,16},{24,28},{28,24},{1,5},{5... | collective-permute-start | bytes 2359304 | tf_op jit(solution)/shard_map/ppermute | solution.py:176
  54.5 42.7 %collective-permute-start.10 = (f32[384,512]{1,0:T(8,128)S(1)}, f32[384,512]{1,0:T(8,128)}, u32[]{:S(2)}, u32[]{:S(2)}) collective-permute-start(f32[384,512]{1,0:T(8,128)S(1)} %collective-permute-done.3.refs_4_), channel_id=1, source_target_pairs={{0,4},{4,0},{8,12},{12,8},{16,20},{20,16},{24,28},{28,24},{1,5},{5... | collective-permute-start | bytes 2359304 | tf_op jit(solution)/shard_map/ppermute | solution.py:176
  57.0 40.3 %collective-permute-start.9 = (f32[384,512]{1,0:T(8,128)S(1)}, f32[384,512]{1,0:T(8,128)}, u32[]{:S(2)}, u32[]{:S(2)}) collective-permute-start(f32[384,512]{1,0:T(8,128)S(1)} %collective-permute-done.8.refs_2_), channel_id=1, source_target_pairs={{0,4},{4,0},{8,12},{12,8},{16,20},{20,16},{24,28},{28,24},{1,5},{5... | collective-permute-start | bytes 2359304 | tf_op jit(solution)/shard_map/ppermute | solution.py:176
  76.9 24.2 %collective-permute-start.6 = (f32[384,512]{1,0:T(8,128)S(1)}, f32[384,512]{1,0:T(8,128)}, u32[]{:S(2)}, u32[]{:S(2)}) collective-permute-start(f32[384,512]{1,0:T(8,128)S(1)} %broadcast_select_fusion.refs_0_), channel_id=1, source_target_pairs={{0,4},{4,0},{8,12},{12,8},{16,20},{20,16},{24,28},{28,24},{1,5},{5... | collective-permute-start | bytes 2359304 | tf_op jit(solution)/shard_map/ppermute | solution.py:176
  85.9 1.1 %copy-start.3 = (f32[256,768]{1,0:T(8,128)S(1)}, f32[256,768]{1,0:T(8,128)}, u32[]{:S(2)}) copy-start(f32[256,768]{1,0:T(8,128)} %copy-done.2) | copy-start | bytes 2359300
  89.2 8.1 %copy-start.1 = (f32[384,512]{1,0:T(8,128)S(1)}, f32[384,512]{1,0:T(8,128)}, u32[]{:S(2)}) copy-start(f32[384,512]{1,0:T(8,128)} %refs_0_.3) | copy-start | bytes 2359300

commit v2 on v1

v2 whole, which is shorter than its diff:
```python
import functools

import jax
import jax.numpy as jnp
from jax import lax
from jax.experimental import pallas as pl
from jax.experimental.pallas import tpu as pltpu
from jax.sharding import PartitionSpec as P

LANES = 128
VMEM = pl.BlockSpec(memory_space=pltpu.VMEM)
SMEM = pl.BlockSpec(memory_space=pltpu.SMEM)
ANY = pl.BlockSpec(memory_space=pl.ANY)
PARAMS = pltpu.CompilerParams(vmem_limit_bytes=40 * 2**20)


def split(x):
    high = x.astype(jnp.bfloat16)
    return high, (x - high.astype(jnp.float32)).astype(jnp.bfloat16)


def look_up(energy, pairs, sums, column):
    tiles = energy.shape[0]
    for tile in range(tiles):
        column[pl.ds(tile * LANES, LANES), :] = jnp.broadcast_to(energy[tile : tile + 1, :], (LANES, LANES)).T
    width = 2 * LANES

    @pl.loop(0, pairs.shape[1] // width)
    def _(step):
        here = pl.ds(pl.multiple_of(step * width, width), width)
        first = jnp.broadcast_to(pairs[0:1, here], (8, width))
        second = jnp.broadcast_to(pairs[1:2, here], (8, width))
        sublane = lax.broadcasted_iota(jnp.int32, (8, width), 0)

        def add(group, total):
            value = column[pl.ds(pl.multiple_of(group * 8, 8), 8), :]
            value = jnp.concatenate([value, value], axis=1)
            index = sublane + group * 8
            return total + (jnp.where(index == first, value, 0.0) + jnp.where(index == second, value, 0.0))

        total = lax.fori_loop(0, tiles * (LANES // 8), add, jnp.zeros((8, width), jnp.float32), unroll=16)
        sums[0:1, here] = jnp.sum(total, axis=0, keepdims=True)


def energy_kernel(occ, vir, occ_pairs, vir_pairs, occ_sum, vir_sum, column):
    look_up(occ, occ_pairs, occ_sum, column)
    look_up(vir, vir_pairs, vir_sum, column)


def energy_sums(occ_energy, vir_energy, occ_pairs, vir_pairs):
    return pl.pallas_call(
        energy_kernel,
        name="energy_sums",
        out_shape=(
            jax.ShapeDtypeStruct((1, occ_pairs.shape[0]), jnp.float32),
            jax.ShapeDtypeStruct((1, vir_pairs.shape[0]), jnp.float32),
        ),
        scratch_shapes=[pltpu.VMEM((max(vir_energy.shape[0], occ_energy.shape[0]), LANES), jnp.float32)],
        compiler_params=PARAMS,
    )(occ_energy.reshape(-1, LANES), vir_energy.reshape(-1, LANES), occ_pairs.T, vir_pairs.T)


def divide_transposed(raw, occ_sum, vir_sum, vir_start, out, out_start, out_column):
    rows, width = raw.shape
    step = 2 * LANES if width % (2 * LANES) == 0 else LANES
    columns = pl.ds(out_column, rows)
    for start in range(0, width, step):
        vir = vir_sum[0:1, pl.ds(pl.multiple_of(vir_start + start, LANES), step)]
        vir = jnp.broadcast_to(vir, (LANES, step)).T
        vir = jnp.concatenate([vir] * (rows // LANES), axis=1)
        out[pl.ds(out_start + start, step), columns] = raw[:, start : start + step].T / (vir - occ_sum[0:1, columns])


def divide_kernel(starts, occ_sum, vir_sum, *refs):
    blocks, (out, held, sems) = refs[:-3], refs[-3:]
    width = held.shape[2]
    copies = [pltpu.make_async_copy(block, held.at[i], sems.at[i]) for i, block in enumerate(blocks)]
    for copy in copies:
        copy.start()
    for i, copy in enumerate(copies):
        copy.wait()
        divide_transposed(held.at[i], occ_sum, vir_sum, starts[i], out, i * width, 0)


def divided(starts, occ_sum, vir_sum, *blocks):
    rows, width = blocks[0].shape
    count = len(blocks)
    return pl.pallas_call(
        divide_kernel,
        name="divided",
        in_specs=[SMEM, VMEM, VMEM] + [ANY] * count,
        out_shape=jax.ShapeDtypeStruct((width * count, rows), jnp.float32),
        scratch_shapes=[pltpu.VMEM((count, rows, width), jnp.float32), pltpu.SemaphoreType.DMA((count,))],
        compiler_params=PARAMS,
    )(starts, occ_sum, vir_sum, *blocks)


def order_kernel(chunk, row_of, starts, bases, occ_sum, vir_sum, done, *refs):
    parts, (high, low, held, raw, rows, sems, done_sem) = refs[:-7], refs[-7:]
    size, width = done.shape[0], raw.shape[1]
    copies, at = [], 0
    for i, part in enumerate(parts):
        copies.append(pltpu.make_async_copy(part, raw.at[pl.ds(at, part.shape[0])], sems.at[i]))
        copies[i].start()
        at += part.shape[0]
    done_copy = pltpu.make_async_copy(done, held.at[pl.ds(0, size)], done_sem)
    done_copy.start()
    at = 0
    for i, part in enumerate(parts):
        copies[i].wait()
        here = raw.at[pl.ds(at, part.shape[0])]
        divide_transposed(here, occ_sum, vir_sum, starts[starts.shape[0] - 1], held, size, at)
        at += part.shape[0]
    done_copy.wait()

    @pl.loop(0, high.shape[0] // chunk)
    def _(step):
        base = bases[step]
        for row in range(chunk):
            rows[pl.ds(row, 1), :] = held[pl.ds(row_of[base + row], 1), :]
        here = pl.ds(pl.multiple_of(step * chunk, chunk), chunk)
        high[here, :], low[here, :] = split(rows[...])


def in_order(row_of, starts, bases, occ_sum, vir_sum, done, *parts):
    pairs, rows = row_of.shape[0], done.shape[1]
    chunk = pairs // bases.shape[0]
    return pl.pallas_call(
        functools.partial(order_kernel, chunk),
        name="in_order",
        in_specs=[SMEM, SMEM, SMEM, VMEM, VMEM, ANY] + [ANY] * len(parts),
        out_shape=(jax.ShapeDtypeStruct((pairs, rows), jnp.bfloat16),) * 2,
        scratch_shapes=[
            pltpu.VMEM((pairs, rows), jnp.float32),
            pltpu.VMEM((rows, parts[0].shape[1]), jnp.float32),
            pltpu.VMEM((chunk, rows), jnp.float32),
            pltpu.SemaphoreType.DMA((len(parts),)),
            pltpu.SemaphoreType.DMA,
        ],
        compiler_params=PARAMS,
    )(row_of, starts, bases, occ_sum, vir_sum, done, *parts)


def product(high, low, block):
    dot = functools.partial(
        lax.dot_general, dimension_numbers=(((0,), (0,)), ((), ())), preferred_element_type=jnp.float32
    )
    block_high, block_low = split(block)
    return dot(high, block_high) + (dot(high, block_low) + dot(low, block_high))


def product_kernel(first, sizes, has_total, high, low, *refs):
    count = len(sizes)
    out, high_held, low_held, total_held, held, sems, more_sems = refs[-7:]
    starts = [sum(sizes[:i]) for i in range(count)]
    copies = [
        pltpu.make_async_copy(refs[i], held.at[pl.ds(starts[i], sizes[i])], sems.at[i]) for i in range(count)
    ]
    ours = pl.ds(first, sum(sizes))
    more = [
        pltpu.make_async_copy(high.at[ours], high_held, more_sems.at[0]),
        pltpu.make_async_copy(low.at[ours], low_held, more_sems.at[1]),
    ]
    if has_total:
        more.append(pltpu.make_async_copy(refs[count], total_held, more_sems.at[2]))
    for copy in more + copies:
        copy.start()
    for copy in more:
        copy.wait()
    for i in range(count):
        copies[i].wait()
        here = pl.ds(starts[i], sizes[i])
        term = product(high_held[here, :], low_held[here, :], held[here, :])
        if i == 0:
            out[...] = total_held[...] + term if has_total else term
        else:
            out[...] += term


def summed(high, low, first, blocks, total=None):
    sizes = [block.shape[0] for block in blocks]
    depth, columns, rows = sum(sizes), blocks[0].shape[1], high.shape[1]
    more = [total] if total is not None else []
    return pl.pallas_call(
        functools.partial(product_kernel, first, sizes, total is not None),
        name="summed",
        in_specs=[ANY, ANY] + [ANY] * len(blocks + more),
        out_specs=VMEM,
        out_shape=jax.ShapeDtypeStruct((rows, columns), jnp.float32),
        scratch_shapes=[
            pltpu.VMEM((depth, rows), jnp.bfloat16),
            pltpu.VMEM((depth, rows), jnp.bfloat16),
            pltpu.VMEM((rows, columns), jnp.float32),
            pltpu.VMEM((depth, columns), jnp.float32),
            pltpu.SemaphoreType.DMA((len(sizes),)),
            pltpu.SemaphoreType.DMA((3,)),
        ],
        compiler_params=PARAMS,
    )(high, low, *blocks, *more)


def four_chips_each(raw_amps, integrals, occ_energy, vir_energy, occ_pairs, vir_pairs, pair_order):
    row, col = lax.axis_index("row"), lax.axis_index("col")
    chip, core = row // 2, row % 2
    (rows, width), depth = raw_amps.shape, integrals.shape[0]

    def other_chip(block, mask):
        return lax.ppermute(block, "row", [(i, i ^ (2 * mask)) for i in range(8)])

    def other_core(block):
        return lax.ppermute(block, "row", [(i, i ^ 1) for i in range(8)])

    def across(block, mask):
        return lax.ppermute(block, "col", [(i, i ^ mask) for i in range(4)])

    next_chip, second_chip = other_chip(integrals, 1), other_chip(integrals, 2)
    raw_x, raw_y = across(raw_amps, 1), across(raw_amps, 2)

    occ_sum, vir_sum = energy_sums(occ_energy, vir_energy, occ_pairs, vir_pairs)
    starts = (col ^ jnp.arange(4, dtype=jnp.int32)) * width
    row_of = ((pair_order // width) ^ col) * width + pair_order % width
    runs = [(m, s, at) for m in range(4) for s in range(2) for at in range(0, depth, LANES)]
    bases = jnp.stack([((chip ^ m) * 2 + (core ^ s)) * depth + at for m, s, at in runs])

    raw_x, raw_y, vir_sum, bases, row_of = lax.optimization_barrier((raw_x, raw_y, vir_sum, bases, row_of))
    raw_d = [across(raw_x[: rows // 2], 2), across(raw_y[rows // 2 :], 1)]
    done = divided(starts[:3], occ_sum, vir_sum, raw_amps, raw_x, raw_y)

    second_chip, next_chip, done, *raw_d = lax.optimization_barrier((second_chip, next_chip, done, *raw_d))
    third_chip = other_chip(second_chip, 1)
    high, low = in_order(row_of, starts, bases, occ_sum, vir_sum, done, *raw_d)
    blocks = []
    for block in (integrals, next_chip, second_chip):
        blocks += [block, other_core(block)]
    total = summed(high, low, 0, blocks)
    third_chip, total = lax.optimization_barrier((third_chip, total))
    return summed(high, low, 6 * depth, [third_chip, other_core(third_chip)], total)


def any_mesh(raw_amps, integrals, occ_energy, vir_energy, occ_pairs, vir_pairs, pair_order):
    occ_sum, vir_sum = energy_sums(occ_energy, vir_energy, occ_pairs, vir_pairs)
    raw = lax.all_gather(raw_amps, "col", axis=1, tiled=True)
    half = raw.shape[1] // 2
    starts = jnp.arange(2, dtype=jnp.int32) * half
    done = divided(starts[:1], occ_sum, vir_sum, raw[:, :half])
    bases = jnp.arange(0, raw.shape[1], LANES, dtype=jnp.int32)
    high, low = in_order(pair_order, starts, bases, occ_sum, vir_sum, done, raw[:, half:])
    return summed(high, low, 0, [lax.all_gather(integrals, "row", axis=0, tiled=True)])


def solution(mesh):
    placed = (P("row", "col"), P("row", "col"), P(), P(), P("row", None), P(), P())
    on_device = four_chips_each if (mesh.shape["row"], mesh.shape["col"]) == (8, 4) else any_mesh
    return jax.shard_map(
        on_device, mesh=mesh, in_specs=placed, out_specs=P("row", "col"), check_vma=False
    )
```

time: 104 us -> 66.9 us (0.64)
  the two profiles are of different devices: /device:TPU:17 before, /device:TPU:0 now
where the time goes in v2:
time: 66.9 us; the launch traced here: 66.6 us
  waiting for transfers between devices  26.9 us (40%)
  Pallas kernels  23.1 us (35%)
  starting transfers between devices  12.8 us (19%)
  local copies, waits for them, and re-layouts  2.96 us (4%)
  other arithmetic  0.73 us (1%)
    ppermute x3, waiting for transfers between devices, other_chip(): return lax.ppermute(block, 'row', [(i, i ^ 2 * mask) for i in range(8)])  21.8 us
    pallas_call x1, Pallas kernels, in_order(): pl.pallas_call(functools.partial(order_kernel, chunk), name='in_order', i...  7.85 us
    pallas_call x1, Pallas kernels, energy_sums(): pl.pallas_call(energy_kernel, name='energy_sums', out_shape=(jax.ShapeDty...  7.08 us
    ppermute x4, starting transfers between devices, across(): return lax.ppermute(block, 'col', [(i, i ^ mask) for i in range(4)])  6.64 us
    pallas_call x2, Pallas kernels, summed(): pl.pallas_call(functools.partial(product_kernel, first, sizes, total is n...  6.35 us
    ppermute x3, starting transfers between devices, other_chip(): return lax.ppermute(block, 'row', [(i, i ^ 2 * mask) for i in range(8)])  5.6 us
    ppermute x4, waiting for transfers between devices, across(): return lax.ppermute(block, 'col', [(i, i ^ mask) for i in range(4)])  2.81 us
    unnamed x12, local copies, waits for them, and re-layouts  2.8 us
  transfers between devices with their start and end apart: 11, of which 6 were waited for; matrix products, arithmetic and copies ran while one was open for 1% of the time, Pallas kernels for 31%

profile of v2, /device:TPU:0, one launch (start us, length us, event | category | flops | bytes accessed | tf_op | source)
XLA Modules:
  0.0 66.6 jit_solution(14517282996411028547)
XLA Ops:
  0.0 2.9 %collective-permute-start = (f32[256,768]{1,0:T(8,128)}, f32[256,768]{1,0:T(8,128)S(1)}, u32[]{:S(2)}, u32[]{:S(2)}) collective-permute-start(f32[256,768]{1,0:T(8,128)} %refs_0_.2), channel_id=1, source_target_pairs={{0,1},{1,0},{2,3},{3,2},{4,5},{5,4},{6,7},{7,6},{8,9},{9,8},{10,11... | collective-permute-start | bytes 2359304 | tf_op jit(solution)/shard_map/ppermute | solution.py:214
  2.9 1.5 %collective-permute-start.1 = (f32[256,768]{1,0:T(8,128)}, f32[256,768]{1,0:T(8,128)S(1)}, u32[]{:S(2)}, u32[]{:S(2)}) collective-permute-start(f32[256,768]{1,0:T(8,128)} %refs_0_.2), channel_id=1, source_target_pairs={{0,2},{1,3},{2,0},{3,1},{4,6},{5,7},{6,4},{7,5},{8,10},{9,11},{10,... | collective-permute-start | bytes 2359304 | tf_op jit(solution)/shard_map/ppermute | solution.py:214
  4.5 2.6 %collective-permute-start.2 = (f32[384,512]{1,0:T(8,128)}, f32[384,512]{1,0:T(8,128)}, u32[]{:S(2)}, u32[]{:S(2)}) collective-permute-start(f32[384,512]{1,0:T(8,128)} %refs_0_.3), channel_id=1, source_target_pairs={{0,16},{4,20},{8,24},{12,28},{16,0},{20,4},{24,8},{28,12},{1,17},{... | collective-permute-start | bytes 2359304 | tf_op jit(solution)/shard_map/ppermute | solution.py:208
  7.1 1.6 %collective-permute-start.3 = (f32[384,512]{1,0:T(8,128)}, f32[384,512]{1,0:T(8,128)}, u32[]{:S(2)}, u32[]{:S(2)}) collective-permute-start(f32[384,512]{1,0:T(8,128)} %refs_0_.3), channel_id=1, source_target_pairs={{0,8},{4,12},{8,0},{12,4},{16,24},{20,28},{24,16},{28,20},{1,9},{5... | collective-permute-start | bytes 2359304 | tf_op jit(solution)/shard_map/ppermute | solution.py:208
  8.6 0.7 %copy-done.2 = s32[3072,2]{0,1:T(2,128)S(1)} copy-done((s32[3072,2]{0,1:T(2,128)S(1)}, s32[3072,2]{0,1:T(2,128)}, u32[]{:S(2)}) %copy-start.2) | copy-done | bytes 24600
  9.4 0.7 %copy-done.3 = f32[2048]{0:T(1024)S(1)} copy-done((f32[2048]{0:T(1024)S(1)}, f32[2048]{0:T(1024)}, u32[]{:S(2)}) %copy-start.3) | copy-done | bytes 8216
  10.1 0.7 %copy-done.4 = s32[256,2]{0,1:T(2,128)S(1)} copy-done((s32[256,2]{0,1:T(2,128)S(1)}, s32[256,2]{0,1:T(2,128)}, u32[]{:S(2)}) %copy-start.4) | copy-done | bytes 2072
  10.7 0.7 %copy-done.5 = f32[256]{0:T(256)S(1)} copy-done((f32[256]{0:T(256)S(1)}, f32[256]{0:T(256)}, u32[]{:S(2)}) %copy-start.5) | copy-done | bytes 1048
  11.4 7.1 %energy_sums.1 = (f32[1,256]{1,0:T(1,128)S(1)}, f32[1,3072]{1,0:T(1,128)S(1)}) custom-call(f32[2,128]{1,0:T(2,128)S(1)} %bitcast.33, f32[16,128]{1,0:T(8,128)S(1)} %bitcast.30, s32[2,256]{1,0:T(2,128)S(1)} %bitcast.31, s32[2,3072]{1,0:T(2,128)S(1)} %bitcast.29), custom_call_target="tpu_custom_call" | custom-call | tf_op jit(solution)/shard_map/energy_sums/pallas_call | solution.py:51
  18.5 0.1 stack.99.bases
  18.6 0.7 %fusion.2.row_of = s32[3072]{0:T(1024)S(1)} fusion(s32[3072]{0:T(1024)} %param.13, s32[]{:T(128)S(6)} %axis_index.25), kind=kLoop, calls=%fused_computation.4 | loop fusion | flops 46080 | bytes 24580 | tf_op jit(solution)/shard_map/add | solution.py:221
  19.4 1.4 %collective-permute-done.refs_1_ = f32[256,768]{1,0:T(8,128)S(1)} collective-permute-done((f32[256,768]{1,0:T(8,128)}, f32[256,768]{1,0:T(8,128)S(1)}, u32[]{:S(2)}, u32[]{:S(2)}) %collective-permute-start) | collective-permute-done | bytes 786464 | tf_op jit(solution)/shard_map/ppermute | solution.py:214
  20.8 1.4 %collective-permute-done.1.refs_2_ = f32[256,768]{1,0:T(8,128)S(1)} collective-permute-done((f32[256,768]{1,0:T(8,128)}, f32[256,768]{1,0:T(8,128)S(1)}, u32[]{:S(2)}, u32[]{:S(2)}) %collective-permute-start.1) | collective-permute-done | bytes 786464 | tf_op jit(solution)/shard_map/ppermute | solution.py:214
  22.2 1.6 %collective-permute-start.4 = (f32[128,768]{1,0:T(8,128)S(1)}, f32[128,768]{1,0:T(8,128)S(1)}, u32[]{:S(2)}, u32[]{:S(2)}) collective-permute-start(f32[128,768]{1,0:T(8,128)S(1)} %slice.10), channel_id=1, source_target_pairs={{0,2},{1,3},{2,0},{3,1},{4,6},{5,7},{6,4},{7,5},{8,10},{9,11},{10,... | collective-permute-start | bytes 1179656 | tf_op jit(solution)/shard_map/ppermute | solution.py:214
  23.8 0.6 collective-permute-start.5
  24.4 0.0 collective-permute-start.7
  24.4 1.9 %divided.1.done = f32[2304,256]{1,0:T(8,128)S(1)} custom-call(s32[3]{0:T(128)S(1)} %bitcast.32, f32[1,256]{1,0:T(1,128)S(1)} %get-tuple-element.24.occ_sum, f32[1,3072]{1,0:T(1,128)S(1)} %get-tuple-element.25.vir_sum, f32[256,768]{1,0:T(8,128)S(1)} %copy-done, f32[256,768]{1,0:T(8,128)S(1)} %collective-permute-done.refs_1_, ...), custom_call_target="tpu_custom_call" | custom-call | tf_op jit(solution)/shard_map/divided/pallas_call | solution.py:88
  26.3 15.1 %collective-permute-done.2.refs_4_ = f32[384,512]{1,0:T(8,128)} collective-permute-done((f32[384,512]{1,0:T(8,128)}, f32[384,512]{1,0:T(8,128)}, u32[]{:S(2)}, u32[]{:S(2)}) %collective-permute-start.2) | collective-permute-done | bytes 786464 | tf_op jit(solution)/shard_map/ppermute | solution.py:208
  41.4 0.2 collective-permute-done.3.refs_2_
  41.5 0.0 collective-permute-done.4.refs_0_
  41.6 0.0 collective-permute-done.5.refs_1_
  41.6 0.0 collective-permute-start.8
  41.6 0.5 collective-permute-start.9
  42.1 1.4 %collective-permute-start.6 = (f32[384,512]{1,0:T(8,128)}, f32[384,512]{1,0:T(8,128)S(1)}, u32[]{:S(2)}, u32[]{:S(2)}) collective-permute-start(f32[384,512]{1,0:T(8,128)} %collective-permute-done.2.refs_4_), channel_id=1, source_target_pairs={{0,8},{4,12},{8,0},{12,4},{16,24},{20,28},{24,16},{28,20},{1,9},{5... | collective-permute-start | bytes 2359304 | tf_op jit(solution)/shard_map/ppermute | solution.py:208
  43.5 7.9 %in_order.1 = (bf16[3072,256]{1,0:T(8,128)(2,1)S(1)}, bf16[3072,256]{1,0:T(8,128)(2,1)S(1)}) custom-call(s32[3072]{0:T(1024)S(1)} %fusion.2.row_of, s32[4]{0:T(128)S(1)} %xor_multiply_fusion.starts, s32[24]{0:T(128)S(1)} %stack.99.bases, f32[1,256]{1,0:T(1,128)S(1)} %get-tuple-element.24.occ_sum, f32[1,3072]{1,0:T(1,128)S(1)} %get-tuple-element.25.vir_sum, ...), custom_call_target="tpu_custom_call" | custom-call | tf_op jit(solution)/shard_map/in_order/pallas_call | solution.py:128
  51.4 0.0 collective-permute-done.8.refs_3_
  51.4 0.0 collective-permute-done.9.refs_5_
  51.4 3.9 %summed.2.refs_2_ = f32[256,512]{1,0:T(8,128)S(1)} custom-call(bf16[3072,256]{1,0:T(8,128)(2,1)S(1)} %get-tuple-element.31.high, bf16[3072,256]{1,0:T(8,128)(2,1)S(1)} %get-tuple-element.32.low, f32[384,512]{1,0:T(8,128)S(1)} %copy-done.1, f32[384,512]{1,0:T(8,128)S(1)} %collective-permute-done.7.refs_1_, f32[384,512]{1,0:T(8,128)} %collective-permute-done.3.refs_2_, ...), custom_call_target="tpu_custom_call" | custom-call | tf_op jit(solution)/shard_map/summed/pallas_call | solution.py:184
  55.3 6.5 %collective-permute-done.6.refs_0_ = f32[384,512]{1,0:T(8,128)S(1)} collective-permute-done((f32[384,512]{1,0:T(8,128)}, f32[384,512]{1,0:T(8,128)S(1)}, u32[]{:S(2)}, u32[]{:S(2)}) %collective-permute-start.6) | collective-permute-done | bytes 786464 | tf_op jit(solution)/shard_map/ppermute | solution.py:208
  61.8 0.0 collective-permute-start.10
  61.8 2.3 %collective-permute-done.10.refs_1_ = f32[384,512]{1,0:T(8,128)S(1)} collective-permute-done((f32[384,512]{1,0:T(8,128)S(1)}, f32[384,512]{1,0:T(8,128)S(1)}, u32[]{:S(2)}, u32[]{:S(2)}) %collective-permute-start.10) | collective-permute-done | bytes 786464 | tf_op jit(solution)/shard_map/ppermute | solution.py:211
  64.1 2.5 %summed.3 = f32[256,512]{1,0:T(8,128)} custom-call(bf16[3072,256]{1,0:T(8,128)(2,1)S(1)} %get-tuple-element.31.high, bf16[3072,256]{1,0:T(8,128)(2,1)S(1)} %get-tuple-element.32.low, f32[384,512]{1,0:T(8,128)S(1)} %collective-permute-done.6.refs_0_, f32[384,512]{1,0:T(8,128)S(1)} %collective-permute-done.10.refs_1_, f32[256,512]{1,0:T(8,128)S(1)} %summed.2.refs_2_), custom_call_target="tpu_custom_call" | custom-call | tf_op jit(solution)/shard_map/summed/pallas_call | solution.py:184
  (12 shorter events, 0.1 us)
Async XLA Ops:
  0.0 24.4 %copy-start = (f32[256,768]{1,0:T(8,128)S(1)}, f32[256,768]{1,0:T(8,128)}, u32[]{:S(2)}) copy-start(f32[256,768]{1,0:T(8,128)} %refs_0_.2) | copy-start | bytes 2359300
  0.0 24.4 %copy-start.1 = (f32[384,512]{1,0:T(8,128)S(1)}, f32[384,512]{1,0:T(8,128)}, u32[]{:S(2)}) copy-start(f32[384,512]{1,0:T(8,128)} %refs_0_.3) | copy-start | bytes 2359300
  0.0 20.8 %collective-permute-start = (f32[256,768]{1,0:T(8,128)}, f32[256,768]{1,0:T(8,128)S(1)}, u32[]{:S(2)}, u32[]{:S(2)}) collective-permute-start(f32[256,768]{1,0:T(8,128)} %refs_0_.2), channel_id=1, source_target_pairs={{0,1},{1,0},{2,3},{3,2},{4,5},{5,4},{6,7},{7,6},{8,9},{9,8},{10,11... | collective-permute-start | bytes 2359304 | tf_op jit(solution)/shard_map/ppermute | solution.py:214
  2.9 19.2 %collective-permute-start.1 = (f32[256,768]{1,0:T(8,128)}, f32[256,768]{1,0:T(8,128)S(1)}, u32[]{:S(2)}, u32[]{:S(2)}) collective-permute-start(f32[256,768]{1,0:T(8,128)} %refs_0_.2), channel_id=1, source_target_pairs={{0,2},{1,3},{2,0},{3,1},{4,6},{5,7},{6,4},{7,5},{8,10},{9,11},{10,... | collective-permute-start | bytes 2359304 | tf_op jit(solution)/shard_map/ppermute | solution.py:214
  4.5 36.9 %collective-permute-start.2 = (f32[384,512]{1,0:T(8,128)}, f32[384,512]{1,0:T(8,128)}, u32[]{:S(2)}, u32[]{:S(2)}) collective-permute-start(f32[384,512]{1,0:T(8,128)} %refs_0_.3), channel_id=1, source_target_pairs={{0,16},{4,20},{8,24},{12,28},{16,0},{20,4},{24,8},{28,12},{1,17},{... | collective-permute-start | bytes 2359304 | tf_op jit(solution)/shard_map/ppermute | solution.py:208
  7.1 34.5 %collective-permute-start.3 = (f32[384,512]{1,0:T(8,128)}, f32[384,512]{1,0:T(8,128)}, u32[]{:S(2)}, u32[]{:S(2)}) collective-permute-start(f32[384,512]{1,0:T(8,128)} %refs_0_.3), channel_id=1, source_target_pairs={{0,8},{4,12},{8,0},{12,4},{16,24},{20,28},{24,16},{28,20},{1,9},{5... | collective-permute-start | bytes 2359304 | tf_op jit(solution)/shard_map/ppermute | solution.py:208
  8.6 0.7 %copy-start.2 = (s32[3072,2]{0,1:T(2,128)S(1)}, s32[3072,2]{0,1:T(2,128)}, u32[]{:S(2)}) copy-start(s32[3072,2]{0,1:T(2,128)} %param.12) | copy-start | bytes 73732
  9.4 0.7 %copy-start.3 = (f32[2048]{0:T(1024)S(1)}, f32[2048]{0:T(1024)}, u32[]{:S(2)}) copy-start(f32[2048]{0:T(1024)} %param.10) | copy-start | bytes 24580
  10.1 0.7 %copy-start.4 = (s32[256,2]{0,1:T(2,128)S(1)}, s32[256,2]{0,1:T(2,128)}, u32[]{:S(2)}) copy-start(s32[256,2]{0,1:T(2,128)} %param.11) | copy-start | bytes 6148
  10.7 0.7 %copy-start.5 = (f32[256]{0:T(256)S(1)}, f32[256]{0:T(256)}, u32[]{:S(2)}) copy-start(f32[256]{0:T(256)} %param.9) | copy-start | bytes 3076
  22.2 19.4 %collective-permute-start.4 = (f32[128,768]{1,0:T(8,128)S(1)}, f32[128,768]{1,0:T(8,128)S(1)}, u32[]{:S(2)}, u32[]{:S(2)}) collective-permute-start(f32[128,768]{1,0:T(8,128)S(1)} %slice.10), channel_id=1, source_target_pairs={{0,2},{1,3},{2,0},{3,1},{4,6},{5,7},{6,4},{7,5},{8,10},{9,11},{10,... | collective-permute-start | bytes 1179656 | tf_op jit(solution)/shard_map/ppermute | solution.py:214
  23.8 17.8 %collective-permute-start.5 = (f32[128,768]{1,0:T(8,128)S(1)}, f32[128,768]{1,0:T(8,128)S(1)}, u32[]{:S(2)}, u32[]{:S(2)}) collective-permute-start(f32[128,768]{1,0:T(8,128)S(1)} %slice.11), channel_id=1, source_target_pairs={{0,1},{1,0},{2,3},{3,2},{4,5},{5,4},{6,7},{7,6},{8,9},{9,8},{10,11... | collective-permute-start | bytes 1179656 | tf_op jit(solution)/shard_map/ppermute | solution.py:214
  24.4 27.0 %collective-permute-start.7 = (f32[384,512]{1,0:T(8,128)S(1)}, f32[384,512]{1,0:T(8,128)S(1)}, u32[]{:S(2)}, u32[]{:S(2)}) collective-permute-start(f32[384,512]{1,0:T(8,128)S(1)} %copy-done.1), channel_id=1, source_target_pairs={{0,4},{4,0},{8,12},{12,8},{16,20},{20,16},{24,28},{28,24},{1,5},{5... | collective-permute-start | bytes 2359304 | tf_op jit(solution)/shard_map/ppermute | solution.py:211
  41.6 9.8 %collective-permute-start.8 = (f32[384,512]{1,0:T(8,128)}, f32[384,512]{1,0:T(8,128)S(1)}, u32[]{:S(2)}, u32[]{:S(2)}) collective-permute-start(f32[384,512]{1,0:T(8,128)} %collective-permute-done.3.refs_2_), channel_id=1, source_target_pairs={{0,4},{4,0},{8,12},{12,8},{16,20},{20,16},{24,28},{28,24},{1,5},{5... | collective-permute-start | bytes 2359304 | tf_op jit(solution)/shard_map/ppermute | solution.py:211
  41.6 9.8 %collective-permute-start.9 = (f32[384,512]{1,0:T(8,128)}, f32[384,512]{1,0:T(8,128)S(1)}, u32[]{:S(2)}, u32[]{:S(2)}) collective-permute-start(f32[384,512]{1,0:T(8,128)} %collective-permute-done.2.refs_4_), channel_id=1, source_target_pairs={{0,4},{4,0},{8,12},{12,8},{16,20},{20,16},{24,28},{28,24},{1,5},{5... | collective-permute-start | bytes 2359304 | tf_op jit(solution)/shard_map/ppermute | solution.py:211
  42.1 19.7 %collective-permute-start.6 = (f32[384,512]{1,0:T(8,128)}, f32[384,512]{1,0:T(8,128)S(1)}, u32[]{:S(2)}, u32[]{:S(2)}) collective-permute-start(f32[384,512]{1,0:T(8,128)} %collective-permute-done.2.refs_4_), channel_id=1, source_target_pairs={{0,8},{4,12},{8,0},{12,4},{16,24},{20,28},{24,16},{28,20},{1,9},{5... | collective-permute-start | bytes 2359304 | tf_op jit(solution)/shard_map/ppermute | solution.py:208
  61.8 2.3 %collective-permute-start.10 = (f32[384,512]{1,0:T(8,128)S(1)}, f32[384,512]{1,0:T(8,128)S(1)}, u32[]{:S(2)}, u32[]{:S(2)}) collective-permute-start(f32[384,512]{1,0:T(8,128)S(1)} %collective-permute-done.6.refs_0_), channel_id=1, source_target_pairs={{0,4},{4,0},{8,12},{12,8},{16,20},{20,16},{24,28},{28,24},{1,5},{5... | collective-permute-start | bytes 2359304 | tf_op jit(solution)/shard_map/ppermute | solution.py:211

commit v3 on v2

--- a/solution.py
+++ b/solution.py
@@ -60,85 +60,58 @@
     )(occ_energy.reshape(-1, LANES), vir_energy.reshape(-1, LANES), occ_pairs.T, vir_pairs.T)
 
 
-def divide_transposed(raw, occ_sum, vir_sum, vir_start, out, out_start, out_column):
+def divide_turned(raw, occ_sum, vir_sum, vir_start, held, at):
     rows, width = raw.shape
+    tiles = rows // LANES
     step = 2 * LANES if width % (2 * LANES) == 0 else LANES
-    columns = pl.ds(out_column, rows)
     for start in range(0, width, step):
         vir = vir_sum[0:1, pl.ds(pl.multiple_of(vir_start + start, LANES), step)]
         vir = jnp.broadcast_to(vir, (LANES, step)).T
-        vir = jnp.concatenate([vir] * (rows // LANES), axis=1)
-        out[pl.ds(out_start + start, step), columns] = raw[:, start : start + step].T / (vir - occ_sum[0:1, columns])
-
-
-def divide_kernel(starts, occ_sum, vir_sum, *refs):
-    blocks, (out, held, sems) = refs[:-3], refs[-3:]
-    width = held.shape[2]
-    copies = [pltpu.make_async_copy(block, held.at[i], sems.at[i]) for i, block in enumerate(blocks)]
+        for tile in range(tiles):
+            mine = pl.ds(tile * LANES, LANES)
+            part = raw[mine, start : start + step].T / (vir - occ_sum[0:1, mine])
+            held[pl.ds((at + start) * tiles + tile, step, stride=tiles), :] = part
+
+
+def order_kernel(chunk, row_of, starts, bases, occ_sum, vir_sum, *refs):
+    blocks, (high, low, raw, held, rows, sems) = refs[:-6], refs[-6:]
+    width = raw.shape[2]
+    tiles = high.shape[1] // LANES
+    copies = [pltpu.make_async_copy(block, raw.at[i], sems.at[i]) for i, block in enumerate(blocks)]
     for copy in copies:
         copy.start()
     for i, copy in enumerate(copies):
         copy.wait()
-        divide_transposed(held.at[i], occ_sum, vir_sum, starts[i], out, i * width, 0)
-
-
-def divided(starts, occ_sum, vir_sum, *blocks):
-    rows, width = blocks[0].shape
-    count = len(blocks)
-    return pl.pallas_call(
-        divide_kernel,
-        name="divided",
-        in_specs=[SMEM, VMEM, VMEM] + [ANY] * count,
-        out_shape=jax.ShapeDtypeStruct((width * count, rows), jnp.float32),
-        scratch_shapes=[pltpu.VMEM((count, rows, width), jnp.float32), pltpu.SemaphoreType.DMA((count,))],
-        compiler_params=PARAMS,
-    )(starts, occ_sum, vir_sum, *blocks)
-
-
-def order_kernel(chunk, row_of, starts, bases, occ_sum, vir_sum, done, *refs):
-    parts, (high, low, held, raw, rows, sems, done_sem) = refs[:-7], refs[-7:]
-    size, width = done.shape[0], raw.shape[1]
-    copies, at = [], 0
-    for i, part in enumerate(parts):
-        copies.append(pltpu.make_async_copy(part, raw.at[pl.ds(at, part.shape[0])], sems.at[i]))
-        copies[i].start()
-        at += part.shape[0]
-    done_copy = pltpu.make_async_copy(done, held.at[pl.ds(0, size)], done_sem)
-    done_copy.start()
-    at = 0
-    for i, part in enumerate(parts):
-        copies[i].wait()
-        here = raw.at[pl.ds(at, part.shape[0])]
-        divide_transposed(here, occ_sum, vir_sum, starts[starts.shape[0] - 1], held, size, at)
-        at += part.shape[0]
-    done_copy.wait()
+        divide_turned(raw.at[i], occ_sum, vir_sum, starts[i], held, i * width)
 
     @pl.loop(0, high.shape[0] // chunk)
     def _(step):
         base = bases[step]
         for row in range(chunk):
-            rows[pl.ds(row, 1), :] = held[pl.ds(row_of[base + row], 1), :]
+            rows[pl.ds(row * tiles, tiles), :] = held[pl.ds(row_of[base + row], tiles), :]
         here = pl.ds(pl.multiple_of(step * chunk, chunk), chunk)
-        high[here, :], low[here, :] = split(rows[...])
-
-
-def in_order(row_of, starts, bases, occ_sum, vir_sum, done, *parts):
-    pairs, rows = row_of.shape[0], done.shape[1]
-    chunk = pairs // bases.shape[0]
+        for tile in range(tiles):
+            mine = pl.ds(tile * LANES, LANES)
+            high[here, mine], low[here, mine] = split(rows[pl.ds(tile, chunk, stride=tiles), :])
+
+
+def ordered(place_of, starts, bases, occ_sum, vir_sum, *blocks):
+    rows, width = blocks[0].shape
+    pairs, count = place_of.shape[0], len(blocks)
+    chunk, tiles = pairs // bases.shape[0], rows // LANES
     return pl.pallas_call(
         functools.partial(order_kernel, chunk),
-        name="in_order",
-        in_specs=[SMEM, SMEM, SMEM, VMEM, VMEM, ANY] + [ANY] * len(parts),
+        name="ordered",
+        in_specs=[SMEM, SMEM, SMEM, VMEM, VMEM] + [ANY] * count,
         out_shape=(jax.ShapeDtypeStruct((pairs, rows), jnp.bfloat16),) * 2,
         scratch_shapes=[
-            pltpu.VMEM((pairs, rows), jnp.float32),
-            pltpu.VMEM((rows, parts[0].shape[1]), jnp.float32),
-            pltpu.VMEM((chunk, rows), jnp.float32),
-            pltpu.SemaphoreType.DMA((len(parts),)),
-            pltpu.SemaphoreType.DMA,
+            pltpu.VMEM((count, rows, width), jnp.float32),
+            pltpu.VMEM((pairs * tiles, LANES), jnp.float32),
+            pltpu.VMEM((chunk * tiles, LANES), jnp.float32),
+            pltpu.SemaphoreType.DMA((count,)),
         ],
         compiler_params=PARAMS,
-    )(row_of, starts, bases, occ_sum, vir_sum, done, *parts)
+    )(place_of * tiles, starts, bases, occ_sum, vir_sum, *blocks)
 
 
 def product(high, low, block):
@@ -202,7 +175,7 @@
 def four_chips_each(raw_amps, integrals, occ_energy, vir_energy, occ_pairs, vir_pairs, pair_order):
     row, col = lax.axis_index("row"), lax.axis_index("col")
     chip, core = row // 2, row % 2
-    (rows, width), depth = raw_amps.shape, integrals.shape[0]
+    width, depth = raw_amps.shape[1], integrals.shape[0]
 
     def other_chip(block, mask):
         return lax.ppermute(block, "row", [(i, i ^ (2 * mask)) for i in range(8)])
@@ -214,37 +187,30 @@
         return lax.ppermute(block, "col", [(i, i ^ mask) for i in range(4)])
 
     next_chip, second_chip = other_chip(integrals, 1), other_chip(integrals, 2)
-    raw_x, raw_y = across(raw_amps, 1), across(raw_amps, 2)
+    raw = [raw_amps] + [across(raw_amps, mask) for mask in (1, 2, 3)]
+    crossed = other_core(integrals)
+    crossed, vir_energy = lax.optimization_barrier((crossed, vir_energy))
 
     occ_sum, vir_sum = energy_sums(occ_energy, vir_energy, occ_pairs, vir_pairs)
     starts = (col ^ jnp.arange(4, dtype=jnp.int32)) * width
-    row_of = ((pair_order // width) ^ col) * width + pair_order % width
-    runs = [(m, s, at) for m in range(4) for s in range(2) for at in range(0, depth, LANES)]
+    place_of = ((pair_order // width) ^ col) * width + pair_order % width
+    runs = [(m, s, at) for m, s in ((0, 0), (0, 1), (1, 0), (2, 0), (1, 1), (2, 1), (3, 0), (3, 1)) for at in range(0, depth, LANES)]
     bases = jnp.stack([((chip ^ m) * 2 + (core ^ s)) * depth + at for m, s, at in runs])
 
-    raw_x, raw_y, vir_sum, bases, row_of = lax.optimization_barrier((raw_x, raw_y, vir_sum, bases, row_of))
-    raw_d = [across(raw_x[: rows // 2], 2), across(raw_y[rows // 2 :], 1)]
-    done = divided(starts[:3], occ_sum, vir_sum, raw_amps, raw_x, raw_y)
-
-    second_chip, next_chip, done, *raw_d = lax.optimization_barrier((second_chip, next_chip, done, *raw_d))
+    second_chip, next_chip, vir_sum, bases, place_of = lax.optimization_barrier((second_chip, next_chip, vir_sum, bases, place_of))
     third_chip = other_chip(second_chip, 1)
-    high, low = in_order(row_of, starts, bases, occ_sum, vir_sum, done, *raw_d)
-    blocks = []
-    for block in (integrals, next_chip, second_chip):
-        blocks += [block, other_core(block)]
-    total = summed(high, low, 0, blocks)
+    high, low = ordered(place_of, starts, bases, occ_sum, vir_sum, *raw)
+    total = summed(high, low, 0, [integrals, crossed, next_chip, second_chip])
     third_chip, total = lax.optimization_barrier((third_chip, total))
-    return summed(high, low, 6 * depth, [third_chip, other_core(third_chip)], total)
+    total = summed(high, low, 4 * depth, [other_core(next_chip), other_core(second_chip), third_chip], total)
+    return summed(high, low, 7 * depth, [other_core(third_chip)], total)
 
 
 def any_mesh(raw_amps, integrals, occ_energy, vir_energy, occ_pairs, vir_pairs, pair_order):
     occ_sum, vir_sum = energy_sums(occ_energy, vir_energy, occ_pairs, vir_pairs)
     raw = lax.all_gather(raw_amps, "col", axis=1, tiled=True)
-    half = raw.shape[1] // 2
-    starts = jnp.arange(2, dtype=jnp.int32) * half
-    done = divided(starts[:1], occ_sum, vir_sum, raw[:, :half])
     bases = jnp.arange(0, raw.shape[1], LANES, dtype=jnp.int32)
-    high, low = in_order(pair_order, starts, bases, occ_sum, vir_sum, done, raw[:, half:])
+    high, low = ordered(pair_order, jnp.zeros(1, jnp.int32), bases, occ_sum, vir_sum, raw)
     return summed(high, low, 0, [lax.all_gather(integrals, "row", axis=0, tiled=True)])
 
 

time: 66.9 us -> 63.2 us (0.945)
  Pallas kernels: 23.1 us -> 19.8 us
  starting transfers between devices: 12.8 us -> 10.1 us
  waiting for transfers between devices: 26.9 us -> 28.1 us
  local copies, waits for them, and re-layouts: 2.96 us -> 4.03 us
    ppermute x3, waiting for transfers between devices: 21.8 us -> 26.3 us  [other_chip(): return lax.ppermute(block, 'row', [(i, i ^ 2 * mask) for i in range(8)])]
    pallas_call x2 -> x1, Pallas kernels: 9.71 us -> 5.68 us  [ordered(): pl.pallas_call(functools.partial(order_kernel, chunk), name='ordered', in...]
    ppermute x4 -> x3, starting transfers between devices: 6.64 us -> 3.55 us  [across(): return lax.ppermute(block, 'col', [(i, i ^ mask) for i in range(4)])]
    ppermute x4, waiting for transfers between devices: 2.29 us -> 0.16 us  [other_core(): return lax.ppermute(block, 'row', [(i, i ^ 1) for i in range(8)])]
    ppermute x4 -> x3, waiting for transfers between devices: 2.81 us -> 1.58 us  [across(): return lax.ppermute(block, 'col', [(i, i ^ mask) for i in range(4)])]
    unnamed x12, local copies, waits for them, and re-layouts: 2.8 us -> 3.93 us
    pallas_call x2 -> x3, Pallas kernels: 6.35 us -> 7.06 us  [summed(): pl.pallas_call(functools.partial(product_kernel, first, sizes, total is n...]
  transfers between devices with their start and end apart: 11 -> 10, of which waited for: 6 -> 5; matrix products, arithmetic and copies ran while one was open for 1% -> 1% of each run, Pallas kernels for 31% -> 28%
where the time goes in v3:
time: 63.2 us; the launch traced here: 62.8 us
  waiting for transfers between devices  28.1 us (44%)
  Pallas kernels  19.8 us (31%)
  starting transfers between devices  10.1 us (16%)
  local copies, waits for them, and re-layouts  4.03 us (6%)
  other arithmetic  0.74 us (1%)
    ppermute x3, waiting for transfers between devices, other_chip(): return lax.ppermute(block, 'row', [(i, i ^ 2 * mask) for i in range(8)])  26.3 us
    pallas_call x1, Pallas kernels, energy_sums(): pl.pallas_call(energy_kernel, name='energy_sums', out_shape=(jax.ShapeDty...  7.08 us
    pallas_call x3, Pallas kernels, summed(): pl.pallas_call(functools.partial(product_kernel, first, sizes, total is n...  7.06 us
    pallas_call x1, Pallas kernels, ordered(): pl.pallas_call(functools.partial(order_kernel, chunk), name='ordered', in...  5.68 us
    ppermute x3, starting transfers between devices, other_chip(): return lax.ppermute(block, 'row', [(i, i ^ 2 * mask) for i in range(8)])  5.59 us
    unnamed x12, local copies, waits for them, and re-layouts  3.93 us
    ppermute x3, starting transfers between devices, across(): return lax.ppermute(block, 'col', [(i, i ^ mask) for i in range(4)])  3.55 us
    ppermute x3, waiting for transfers between devices, across(): return lax.ppermute(block, 'col', [(i, i ^ mask) for i in range(4)])  1.58 us
  transfers between devices with their start and end apart: 10, of which 5 were waited for; matrix products, arithmetic and copies ran while one was open for 1% of the time, Pallas kernels for 28%

profile of v3, /device:TPU:0, one launch (start us, length us, event | category | flops | bytes accessed | tf_op | source)
XLA Modules:
  0.0 62.8 jit_solution(14897684933373125646)
XLA Ops:
  0.0 0.5 collective-permute-start.2
  0.5 2.6 %collective-permute-start.1 = (f32[384,512]{1,0:T(8,128)}, f32[384,512]{1,0:T(8,128)S(1)}, u32[]{:S(2)}, u32[]{:S(2)}) collective-permute-start(f32[384,512]{1,0:T(8,128)} %refs_0_.3), channel_id=1, source_target_pairs={{0,8},{4,12},{8,0},{12,4},{16,24},{20,28},{24,16},{28,20},{1,9},{5... | collective-permute-start | bytes 2359304 | tf_op jit(solution)/shard_map/ppermute | solution.py:181
  3.0 2.6 %collective-permute-start = (f32[384,512]{1,0:T(8,128)}, f32[384,512]{1,0:T(8,128)S(1)}, u32[]{:S(2)}, u32[]{:S(2)}) collective-permute-start(f32[384,512]{1,0:T(8,128)} %refs_0_.3), channel_id=1, source_target_pairs={{0,16},{4,20},{8,24},{12,28},{16,0},{20,4},{24,8},{28,12},{1,17},{... | collective-permute-start | bytes 2359304 | tf_op jit(solution)/shard_map/ppermute | solution.py:181
  5.6 1.5 %collective-permute-start.4 = (f32[256,768]{1,0:T(8,128)}, f32[256,768]{1,0:T(8,128)S(1)}, u32[]{:S(2)}, u32[]{:S(2)}) collective-permute-start(f32[256,768]{1,0:T(8,128)} %refs_0_.2), channel_id=1, source_target_pairs={{0,2},{1,3},{2,0},{3,1},{4,6},{5,7},{6,4},{7,5},{8,10},{9,11},{10,... | collective-permute-start | bytes 2359304 | tf_op jit(solution)/shard_map/ppermute | solution.py:187
  7.1 1.5 %collective-permute-start.3 = (f32[256,768]{1,0:T(8,128)}, f32[256,768]{1,0:T(8,128)S(1)}, u32[]{:S(2)}, u32[]{:S(2)}) collective-permute-start(f32[256,768]{1,0:T(8,128)} %refs_0_.2), channel_id=1, source_target_pairs={{0,1},{1,0},{2,3},{3,2},{4,5},{5,4},{6,7},{7,6},{8,9},{9,8},{10,11... | collective-permute-start | bytes 2359304 | tf_op jit(solution)/shard_map/ppermute | solution.py:187
  8.6 0.1 stack.99.bases
  8.7 0.7 %fusion.2 = s32[3072]{0:T(1024)S(1)} fusion(s32[3072]{0:T(1024)} %param.13, s32[]{:T(128)S(6)} %axis_index.25), kind=kLoop, calls=%fused_computation.4 | loop fusion | flops 46080 | bytes 24580 | tf_op jit(solution)/shard_map/add | solution.py:196
  9.5 0.0 collective-permute-done.2.refs_1_
  9.5 0.5 collective-permute-start.5
  10.0 0.7 %copy-done.2 = s32[3072,2]{0,1:T(2,128)S(1)} copy-done((s32[3072,2]{0,1:T(2,128)S(1)}, s32[3072,2]{0,1:T(2,128)}, u32[]{:S(2)}) %copy-start.2) | copy-done | bytes 24600
  10.8 0.7 %copy-done.3 = f32[2048]{0:T(1024)S(1)} copy-done((f32[2048]{0:T(1024)S(1)}, f32[2048]{0:T(1024)}, u32[]{:S(2)}) %copy-start.3) | copy-done | bytes 8216
  11.5 0.7 %copy-done.4 = s32[256,2]{0,1:T(2,128)S(1)} copy-done((s32[256,2]{0,1:T(2,128)S(1)}, s32[256,2]{0,1:T(2,128)}, u32[]{:S(2)}) %copy-start.4) | copy-done | bytes 2072
  12.1 0.7 %copy-done.5 = f32[256]{0:T(256)S(1)} copy-done((f32[256]{0:T(256)S(1)}, f32[256]{0:T(256)}, u32[]{:S(2)}) %copy-start.5) | copy-done | bytes 1048
  12.8 7.1 %energy_sums.1 = (f32[1,256]{1,0:T(1,128)S(1)}, f32[1,3072]{1,0:T(1,128)S(1)}) custom-call(f32[2,128]{1,0:T(2,128)S(1)} %bitcast.31, f32[16,128]{1,0:T(8,128)S(1)} %bitcast.29, s32[2,256]{1,0:T(2,128)S(1)} %bitcast.30, s32[2,3072]{1,0:T(2,128)S(1)} %bitcast.28), custom_call_target="tpu_custom_call" | custom-call | tf_op jit(solution)/shard_map/energy_sums/pallas_call | solution.py:51
  19.9 18.3 %collective-permute-done.1.refs_2_ = f32[384,512]{1,0:T(8,128)S(1)} collective-permute-done((f32[384,512]{1,0:T(8,128)}, f32[384,512]{1,0:T(8,128)S(1)}, u32[]{:S(2)}, u32[]{:S(2)}) %collective-permute-start.1) | collective-permute-done | bytes 786464 | tf_op jit(solution)/shard_map/ppermute | solution.py:181
  38.2 2.6 %collective-permute-done.refs_3_ = f32[384,512]{1,0:T(8,128)S(1)} collective-permute-done((f32[384,512]{1,0:T(8,128)}, f32[384,512]{1,0:T(8,128)S(1)}, u32[]{:S(2)}, u32[]{:S(2)}) %collective-permute-start) | collective-permute-done | bytes 786464 | tf_op jit(solution)/shard_map/ppermute | solution.py:181
  40.7 0.4 collective-permute-start.6
  41.2 0.0 collective-permute-start.9
  41.2 0.0 collective-permute-done.4.refs_2_
  41.2 0.5 collective-permute-start.8
  41.7 0.0 collective-permute-done.3.refs_1_
  41.7 1.6 %collective-permute-done.5.refs_3_ = f32[256,768]{1,0:T(8,128)S(1)} collective-permute-done((f32[256,768]{1,0:T(8,128)}, f32[256,768]{1,0:T(8,128)S(1)}, u32[]{:S(2)}, u32[]{:S(2)}) %collective-permute-start.5) | collective-permute-done | bytes 786464 | tf_op jit(solution)/shard_map/ppermute | solution.py:187
  43.3 1.1 %copy-done = f32[256,768]{1,0:T(8,128)S(1)} copy-done((f32[256,768]{1,0:T(8,128)S(1)}, f32[256,768]{1,0:T(8,128)}, u32[]{:S(2)}) %copy-start) | copy-done | bytes 786456
  44.4 5.7 %ordered.1 = (bf16[3072,256]{1,0:T(8,128)(2,1)S(1)}, bf16[3072,256]{1,0:T(8,128)(2,1)S(1)}) custom-call(s32[3072]{0:T(1024)S(1)} %broadcast_multiply_fusion.row_of, s32[4]{0:T(128)S(1)} %xor_multiply_fusion.starts, s32[24]{0:T(128)S(1)} %stack.99.bases, f32[1,256]{1,0:T(1,128)S(1)} %get-tuple-element.22.occ_sum, f32[1,3072]{1,0:T(1,128)S(1)} %get-tuple-element.23.vir_sum, ...), custom_call_target="tpu_custom_call" | custom-call | tf_op jit(solution)/shard_map/ordered/pallas_call | solution.py:102
  50.1 2.9 %summed.3.refs_3_ = f32[256,512]{1,0:T(8,128)S(1)} custom-call(bf16[3072,256]{1,0:T(8,128)(2,1)S(1)} %get-tuple-element.24.high, bf16[3072,256]{1,0:T(8,128)(2,1)S(1)} %get-tuple-element.25.low, f32[384,512]{1,0:T(8,128)S(1)} %copy-done.1, f32[384,512]{1,0:T(8,128)} %collective-permute-done.2.refs_1_, f32[384,512]{1,0:T(8,128)S(1)} %collective-permute-done.1.refs_2_, ...), custom_call_target="tpu_custom_call" | custom-call | tf_op jit(solution)/shard_map/summed/pallas_call | solution.py:157
  53.0 5.5 %collective-permute-done.6.refs_2_ = f32[384,512]{1,0:T(8,128)S(1)} collective-permute-done((f32[384,512]{1,0:T(8,128)S(1)}, f32[384,512]{1,0:T(8,128)S(1)}, u32[]{:S(2)}, u32[]{:S(2)}) %collective-permute-start.6) | collective-permute-done | bytes 786464 | tf_op jit(solution)/shard_map/ppermute | solution.py:181
  58.5 0.0 collective-permute-start.7
  58.5 0.0 collective-permute-done.8.refs_0_
  58.5 0.0 collective-permute-done.9.refs_1_
  58.5 2.1 %summed.4.refs_1_ = f32[256,512]{1,0:T(8,128)S(1)} custom-call(bf16[3072,256]{1,0:T(8,128)(2,1)S(1)} %get-tuple-element.24.high, bf16[3072,256]{1,0:T(8,128)(2,1)S(1)} %get-tuple-element.25.low, f32[384,512]{1,0:T(8,128)S(1)} %collective-permute-done.8.refs_0_, f32[384,512]{1,0:T(8,128)S(1)} %collective-permute-done.9.refs_1_, ...), custom_call_target="tpu_custom_call" | custom-call | tf_op jit(solution)/shard_map/summed/pallas_call | solution.py:157
  60.7 0.1 collective-permute-done.7.refs_0_
  60.8 2.0 %summed.5 = f32[256,512]{1,0:T(8,128)} custom-call(bf16[3072,256]{1,0:T(8,128)(2,1)S(1)} %get-tuple-element.24.high, bf16[3072,256]{1,0:T(8,128)(2,1)S(1)} %get-tuple-element.25.low, f32[384,512]{1,0:T(8,128)S(1)} %collective-permute-done.7.refs_0_, f32[256,512]{1,0:T(8,128)S(1)} %summed.4.refs_1_), custom_call_target="tpu_custom_call" | custom-call | tf_op jit(solution)/shard_map/summed/pallas_call | solution.py:157
  (9 shorter events, 0.0 us)
Async XLA Ops:
  0.0 9.5 %collective-permute-start.2 = (f32[384,512]{1,0:T(8,128)}, f32[384,512]{1,0:T(8,128)}, u32[]{:S(2)}, u32[]{:S(2)}) collective-permute-start(f32[384,512]{1,0:T(8,128)} %refs_0_.3), channel_id=1, source_target_pairs={{0,4},{4,0},{8,12},{12,8},{16,20},{20,16},{24,28},{28,24},{1,5},{5... | collective-permute-start | bytes 2359304 | tf_op jit(solution)/shard_map/ppermute | solution.py:184
  0.5 37.7 %collective-permute-start.1 = (f32[384,512]{1,0:T(8,128)}, f32[384,512]{1,0:T(8,128)S(1)}, u32[]{:S(2)}, u32[]{:S(2)}) collective-permute-start(f32[384,512]{1,0:T(8,128)} %refs_0_.3), channel_id=1, source_target_pairs={{0,8},{4,12},{8,0},{12,4},{16,24},{20,28},{24,16},{28,20},{1,9},{5... | collective-permute-start | bytes 2359304 | tf_op jit(solution)/shard_map/ppermute | solution.py:181
  3.0 37.7 %collective-permute-start = (f32[384,512]{1,0:T(8,128)}, f32[384,512]{1,0:T(8,128)S(1)}, u32[]{:S(2)}, u32[]{:S(2)}) collective-permute-start(f32[384,512]{1,0:T(8,128)} %refs_0_.3), channel_id=1, source_target_pairs={{0,16},{4,20},{8,24},{12,28},{16,0},{20,4},{24,8},{28,12},{1,17},{... | collective-permute-start | bytes 2359304 | tf_op jit(solution)/shard_map/ppermute | solution.py:181
  5.6 35.6 %collective-permute-start.4 = (f32[256,768]{1,0:T(8,128)}, f32[256,768]{1,0:T(8,128)S(1)}, u32[]{:S(2)}, u32[]{:S(2)}) collective-permute-start(f32[256,768]{1,0:T(8,128)} %refs_0_.2), channel_id=1, source_target_pairs={{0,2},{1,3},{2,0},{3,1},{4,6},{5,7},{6,4},{7,5},{8,10},{9,11},{10,... | collective-permute-start | bytes 2359304 | tf_op jit(solution)/shard_map/ppermute | solution.py:187
  7.1 34.5 %collective-permute-start.3 = (f32[256,768]{1,0:T(8,128)}, f32[256,768]{1,0:T(8,128)S(1)}, u32[]{:S(2)}, u32[]{:S(2)}) collective-permute-start(f32[256,768]{1,0:T(8,128)} %refs_0_.2), channel_id=1, source_target_pairs={{0,1},{1,0},{2,3},{3,2},{4,5},{5,4},{6,7},{7,6},{8,9},{9,8},{10,11... | collective-permute-start | bytes 2359304 | tf_op jit(solution)/shard_map/ppermute | solution.py:187
  9.5 33.8 %collective-permute-start.5 = (f32[256,768]{1,0:T(8,128)}, f32[256,768]{1,0:T(8,128)S(1)}, u32[]{:S(2)}, u32[]{:S(2)}) collective-permute-start(f32[256,768]{1,0:T(8,128)} %refs_0_.2), channel_id=1, source_target_pairs={{0,3},{1,2},{2,1},{3,0},{4,7},{5,6},{6,5},{7,4},{8,11},{9,10},{10,... | collective-permute-start | bytes 2359304 | tf_op jit(solution)/shard_map/ppermute | solution.py:187
  10.0 0.7 %copy-start.2 = (s32[3072,2]{0,1:T(2,128)S(1)}, s32[3072,2]{0,1:T(2,128)}, u32[]{:S(2)}) copy-start(s32[3072,2]{0,1:T(2,128)} %param.12) | copy-start | bytes 73732
  10.8 0.7 %copy-start.3 = (f32[2048]{0:T(1024)S(1)}, f32[2048]{0:T(1024)}, u32[]{:S(2)}) copy-start(f32[2048]{0:T(1024)} %param.10) | copy-start | bytes 24580
  11.5 0.7 %copy-start.4 = (s32[256,2]{0,1:T(2,128)S(1)}, s32[256,2]{0,1:T(2,128)}, u32[]{:S(2)}) copy-start(s32[256,2]{0,1:T(2,128)} %param.11) | copy-start | bytes 6148
  12.1 0.7 %copy-start.5 = (f32[256]{0:T(256)S(1)}, f32[256]{0:T(256)}, u32[]{:S(2)}) copy-start(f32[256]{0:T(256)} %param.9) | copy-start | bytes 3076
  40.7 17.8 %collective-permute-start.6 = (f32[384,512]{1,0:T(8,128)S(1)}, f32[384,512]{1,0:T(8,128)S(1)}, u32[]{:S(2)}, u32[]{:S(2)}) collective-permute-start(f32[384,512]{1,0:T(8,128)S(1)} %collective-permute-done.refs_3_), channel_id=1, source_target_pairs={{0,8},{4,12},{8,0},{12,4},{16,24},{20,28},{24,16},{28,20},{1,9},{5... | collective-permute-start | bytes 2359304 | tf_op jit(solution)/shard_map/ppermute | solution.py:181
  41.2 17.4 %collective-permute-start.9 = (f32[384,512]{1,0:T(8,128)S(1)}, f32[384,512]{1,0:T(8,128)S(1)}, u32[]{:S(2)}, u32[]{:S(2)}) collective-permute-start(f32[384,512]{1,0:T(8,128)S(1)} %collective-permute-done.refs_3_), channel_id=1, source_target_pairs={{0,4},{4,0},{8,12},{12,8},{16,20},{20,16},{24,28},{28,24},{1,5},{5... | collective-permute-start | bytes 2359304 | tf_op jit(solution)/shard_map/ppermute | solution.py:184
  41.2 17.4 %collective-permute-start.8 = (f32[384,512]{1,0:T(8,128)S(1)}, f32[384,512]{1,0:T(8,128)S(1)}, u32[]{:S(2)}, u32[]{:S(2)}) collective-permute-start(f32[384,512]{1,0:T(8,128)S(1)} %collective-permute-done.1.refs_2_), channel_id=1, source_target_pairs={{0,4},{4,0},{8,12},{12,8},{16,20},{20,16},{24,28},{28,24},{1,5},{5... | collective-permute-start | bytes 2359304 | tf_op jit(solution)/shard_map/ppermute | solution.py:184
  43.3 1.1 %copy-start = (f32[256,768]{1,0:T(8,128)S(1)}, f32[256,768]{1,0:T(8,128)}, u32[]{:S(2)}) copy-start(f32[256,768]{1,0:T(8,128)} %refs_0_.2) | copy-start | bytes 2359300
  44.4 5.7 %copy-start.1 = (f32[384,512]{1,0:T(8,128)S(1)}, f32[384,512]{1,0:T(8,128)}, u32[]{:S(2)}) copy-start(f32[384,512]{1,0:T(8,128)} %refs_0_.3) | copy-start | bytes 2359300
  58.5 2.3 %collective-permute-start.7 = (f32[384,512]{1,0:T(8,128)S(1)}, f32[384,512]{1,0:T(8,128)S(1)}, u32[]{:S(2)}, u32[]{:S(2)}) collective-permute-start(f32[384,512]{1,0:T(8,128)S(1)} %collective-permute-done.6.refs_2_), channel_id=1, source_target_pairs={{0,4},{4,0},{8,12},{12,8},{16,20},{20,16},{24,28},{28,24},{1,5},{5... | collective-permute-start | bytes 2359304 | tf_op jit(solution)/shard_map/ppermute | solution.py:184

commit v4 on v3

v4 whole, which is shorter than its diff:
```python
import functools

import jax
import jax.numpy as jnp
from jax import lax
from jax.experimental import pallas as pl
from jax.experimental.pallas import tpu as pltpu
from jax.sharding import PartitionSpec as P

LANES = 128
RUN = 128
VMEM = pl.BlockSpec(memory_space=pltpu.VMEM)
SMEM = pl.BlockSpec(memory_space=pltpu.SMEM)
ANY = pl.BlockSpec(memory_space=pl.ANY)
PARAMS = pltpu.CompilerParams(vmem_limit_bytes=40 * 2**20)


def split(x):
    high = x.astype(jnp.bfloat16)
    return high, (x - high.astype(jnp.float32)).astype(jnp.bfloat16)


def look_up(energy, pairs, sums, column):
    tiles = energy.shape[0]
    for tile in range(tiles):
        column[pl.ds(tile * LANES, LANES), :] = jnp.broadcast_to(energy[tile : tile + 1, :], (LANES, LANES)).T
    width = 2 * LANES

    @pl.loop(0, pairs.shape[1] // width)
    def _(step):
        here = pl.ds(pl.multiple_of(step * width, width), width)
        first = jnp.broadcast_to(pairs[0:1, here], (8, width))
        second = jnp.broadcast_to(pairs[1:2, here], (8, width))
        sublane = lax.broadcasted_iota(jnp.int32, (8, width), 0)

        def add(group, total):
            value = column[pl.ds(pl.multiple_of(group * 8, 8), 8), :]
            value = jnp.concatenate([value, value], axis=1)
            index = sublane + group * 8
            return total + (jnp.where(index == first, value, 0.0) + jnp.where(index == second, value, 0.0))

        total = lax.fori_loop(0, tiles * (LANES // 8), add, jnp.zeros((8, width), jnp.float32), unroll=16)
        sums[0:1, here] = jnp.sum(total, axis=0, keepdims=True)


def energy_sums(energy, pairs, name, cost=None):
    return pl.pallas_call(
        look_up,
        name=name,
        out_shape=jax.ShapeDtypeStruct((1, pairs.shape[0]), jnp.float32),
        scratch_shapes=[pltpu.VMEM((energy.shape[0], LANES), jnp.float32)],
        compiler_params=PARAMS,
        cost_estimate=cost,
    )(energy.reshape(-1, LANES), pairs.T)


def divide_turned(raw, occ_sum, vir_sum, vir_start, held, at):
    rows, width = raw.shape
    tiles = rows // LANES
    step = 2 * LANES if width % (2 * LANES) == 0 else LANES
    for start in range(0, width, step):
        vir = vir_sum[0:1, pl.ds(pl.multiple_of(vir_start + start, LANES), step)]
        vir = jnp.broadcast_to(vir, (LANES, step)).T
        for tile in range(tiles):
            mine = pl.ds(tile * LANES, LANES)
            part = raw[mine, start : start + step].T / (vir - occ_sum[0:1, mine])
            held[pl.ds((at + start) * tiles + tile, step, stride=tiles), :] = part


def order_kernel(row_of, starts, bases, occ_sum, vir_sum, *refs):
    blocks, (high, low, held, rows) = refs[:-4], refs[-4:]
    width = blocks[0].shape[1]
    tiles = high.shape[0] // LANES
    for i, block in enumerate(blocks):
        divide_turned(block, occ_sum, vir_sum, starts[i], held, i * width)

    @pl.loop(0, high.shape[1] // RUN)
    def _(step):
        base = bases[step]
        for row in range(RUN):
            rows[pl.ds(row * tiles, tiles), :] = held[pl.ds(row_of[base + row], tiles), :]
        here = pl.ds(pl.multiple_of(step * RUN, RUN), RUN)
        for tile in range(tiles):
            mine = pl.ds(tile * LANES, LANES)
            high[mine, here], low[mine, here] = split(rows[pl.ds(tile, RUN, stride=tiles), :].T)


def ordered(place_of, starts, bases, occ_sum, vir_sum, *blocks):
    rows, pairs = blocks[0].shape[0], place_of.shape[0]
    tiles = rows // LANES
    return pl.pallas_call(
        order_kernel,
        name="ordered",
        in_specs=[SMEM, SMEM, SMEM] + [VMEM] * (2 + len(blocks)),
        out_shape=(jax.ShapeDtypeStruct((rows, pairs), jnp.bfloat16),) * 2,
        scratch_shapes=[
            pltpu.VMEM((pairs * tiles, LANES), jnp.float32),
            pltpu.VMEM((RUN * tiles, LANES), jnp.float32),
        ],
        compiler_params=PARAMS,
    )(place_of * tiles, starts, bases, occ_sum, vir_sum, *blocks)


def product(high, low, block):
    dot = functools.partial(jnp.dot, preferred_element_type=jnp.float32)
    block_high, block_low = split(block)
    return dot(high, block_high) + (dot(high, block_low) + dot(low, block_high))


def product_kernel(first, sizes, has_total, last, high, low, *refs):
    count = len(sizes)
    blocks, refs = refs[:count], refs[count:]
    total, refs = (refs[0], refs[1:]) if has_total else (None, refs)
    if last:
        out, result, sems = refs
    else:
        out = result = refs[0]
    parts = 2 if last else 1
    height = result.shape[0] // parts
    stores = []
    for i in range(count):
        here = pl.ds(first + sum(sizes[:i]), sizes[i])
        for part in range(parts):
            mine = pl.ds(part * height, height)
            term = product(high[mine, here], low[mine, here], blocks[i][...])
            if i == 0:
                result[mine, :] = total[mine, :] + term if has_total else term
            else:
                result[mine, :] += term
            if last and i == count - 1:
                stores.append(pltpu.make_async_copy(result.at[mine], out.at[mine], sems.at[part]))
                stores[part].start()
    for store in stores:
        store.wait()


def summed(high, low, first, blocks, total=None, last=False):
    sizes = [block.shape[0] for block in blocks]
    columns, rows = blocks[0].shape[1], high.shape[0]
    more = [total] if total is not None else []
    return pl.pallas_call(
        functools.partial(product_kernel, first, sizes, total is not None, last),
        name="summed",
        in_specs=[VMEM] * (2 + len(blocks) + len(more)),
        out_specs=ANY if last else VMEM,
        out_shape=jax.ShapeDtypeStruct((rows, columns), jnp.float32),
        scratch_shapes=[pltpu.VMEM((rows, columns), jnp.float32), pltpu.SemaphoreType.DMA((2,))] if last else [],
        compiler_params=PARAMS,
    )(high, low, *blocks, *more)


def four_chips_each(raw_amps, integrals, occ_energy, vir_energy, occ_pairs, vir_pairs, pair_order):
    row, col = lax.axis_index("row"), lax.axis_index("col")
    chip, core = row // 2, row % 2
    width, depth = raw_amps.shape[1], integrals.shape[0]

    def other_chip(block, mask):
        return lax.ppermute(block, "row", [(i, i ^ (2 * mask)) for i in range(8)])

    def other_core(block):
        return lax.ppermute(block, "row", [(i, i ^ 1) for i in range(8)])

    def across(block, mask):
        return lax.ppermute(block, "col", [(i, i ^ mask) for i in range(4)])

    next_chip, second_chip = other_chip(integrals, 1), other_chip(integrals, 2)
    raw = [across(raw_amps, mask) for mask in (1, 2, 3)]

    vir_sum = energy_sums(vir_energy, vir_pairs, "vir_sums")
    starts = (col ^ jnp.arange(4, dtype=jnp.int32)) * width
    place_of = ((pair_order // width) ^ col) * width + pair_order % width
    blocks = ((0, 0), (1, 0), (2, 0), (0, 1), (1, 1), (2, 1), (3, 0), (3, 1))
    runs = [(m, s, at) for m, s in blocks for at in range(0, depth, RUN)]
    bases = jnp.stack([((chip ^ m) * 2 + (core ^ s)) * depth + at for m, s, at in runs])

    second_chip, vir_sum, bases, place_of = lax.optimization_barrier((second_chip, vir_sum, bases, place_of))
    third_chip = other_chip(second_chip, 1)
    next_chip, occ_energy = lax.optimization_barrier((next_chip, occ_energy))
    occ_sum = energy_sums(occ_energy, occ_pairs, "occ_sums", None)
    *raw, occ_sum = lax.optimization_barrier((*raw, occ_sum))
    high, low = ordered(place_of, starts, bases, occ_sum, vir_sum, raw_amps, *raw)
    own = [integrals, next_chip, second_chip]
    total = summed(high, low, 0, own)
    third_chip, total = lax.optimization_barrier((third_chip, total))
    total = summed(high, low, 3 * depth, [other_core(block) for block in own] + [third_chip], total)
    return summed(high, low, 7 * depth, [other_core(third_chip)], total, last=True)


def any_mesh(raw_amps, integrals, occ_energy, vir_energy, occ_pairs, vir_pairs, pair_order):
    occ_sum = energy_sums(occ_energy, occ_pairs, "occ_sums")
    vir_sum = energy_sums(vir_energy, vir_pairs, "vir_sums")
    raw = lax.all_gather(raw_amps, "col", axis=1, tiled=True)
    bases = jnp.arange(0, raw.shape[1], RUN, dtype=jnp.int32)
    high, low = ordered(pair_order, jnp.zeros(1, jnp.int32), bases, occ_sum, vir_sum, raw)
    return summed(high, low, 0, [lax.all_gather(integrals, "row", axis=0, tiled=True)])


def solution(mesh):
    placed = (P("row", "col"), P("row", "col"), P(), P(), P("row", None), P(), P())
    on_device = four_chips_each if (mesh.shape["row"], mesh.shape["col"]) == (8, 4) else any_mesh
    return jax.shard_map(
        on_device, mesh=mesh, in_specs=placed, out_specs=P("row", "col"), check_vma=False
    )
```

time: 63.2 us -> 61.4 us (0.972)
  waiting for transfers between devices: 28.1 us -> 25.7 us
    ppermute x3, waiting for transfers between devices: 26.3 us -> 24.2 us  [other_chip(): return lax.ppermute(block, 'row', [(i, i ^ 2 * mask) for i in range(8)])]
    pallas_call x2 -> x3, Pallas kernels: 12.8 us -> 14.4 us  [the longest x1 7.22 us: ordered(): pl.pallas_call(order_kernel, name='ordered', in_specs=[SMEM, SMEM, SMEM]...]
    pallas_call x3, Pallas kernels: 7.06 us -> 5.65 us  [summed(): pl.pallas_call(functools.partial(product_kernel, first, sizes, total is n...]
    ppermute x3, starting transfers between devices: 5.59 us -> 6.33 us  [other_chip(): return lax.ppermute(block, 'row', [(i, i ^ 2 * mask) for i in range(8)])]
  transfers between devices with their start and end apart: 10 -> 10, of which waited for: 5 -> 4; matrix products, arithmetic and copies ran while one was open for 1% -> 1% of each run, Pallas kernels for 28% -> 31%
where the time goes in v4:
time: 61.4 us; the launch traced here: 61 us
  waiting for transfers between devices  25.7 us (42%)
  Pallas kernels  20.1 us (33%)
  starting transfers between devices  10.4 us (17%)
  local copies, waits for them, and re-layouts  4.03 us (7%)
  other arithmetic  0.74 us (1%)
    ppermute x3, waiting for transfers between devices, other_chip(): return lax.ppermute(block, 'row', [(i, i ^ 2 * mask) for i in range(8)])  24.2 us
    pallas_call x1, Pallas kernels, ordered(): pl.pallas_call(order_kernel, name='ordered', in_specs=[SMEM, SMEM, SMEM]...  7.22 us
    pallas_call x2, Pallas kernels, energy_sums(): pl.pallas_call(look_up, name=name, out_shape=jax.ShapeDtypeStruct((1, pai...  7.19 us
    ppermute x3, starting transfers between devices, other_chip(): return lax.ppermute(block, 'row', [(i, i ^ 2 * mask) for i in range(8)])  6.33 us
    pallas_call x3, Pallas kernels, summed(): pl.pallas_call(functools.partial(product_kernel, first, sizes, total is n...  5.65 us
    unnamed x12, local copies, waits for them, and re-layouts  3.92 us
    ppermute x3, starting transfers between devices, across(): return lax.ppermute(block, 'col', [(i, i ^ mask) for i in range(4)])  3.49 us
  transfers between devices with their start and end apart: 10, of which 4 were waited for; matrix products, arithmetic and copies ran while one was open for 1% of the time, Pallas kernels for 31%

profile of v4, /device:TPU:0, one launch (start us, length us, event | category | flops | bytes accessed | tf_op | source)
XLA Modules:
  0.0 61.0 jit_solution(5354811087651742142)
XLA Ops:
  0.0 4.0 %collective-permute-start = (f32[384,512]{1,0:T(8,128)}, f32[384,512]{1,0:T(8,128)S(1)}, u32[]{:S(2)}, u32[]{:S(2)}) collective-permute-start(f32[384,512]{1,0:T(8,128)} %refs_0_.3), channel_id=1, source_target_pairs={{0,16},{4,20},{8,24},{12,28},{16,0},{20,4},{24,8},{28,12},{1,17},{... | collective-permute-start | bytes 2359304 | tf_op jit(solution)/shard_map/ppermute | solution.py:158
  4.0 1.6 %collective-permute-start.4 = (f32[384,512]{1,0:T(8,128)}, f32[384,512]{1,0:T(8,128)}, u32[]{:S(2)}, u32[]{:S(2)}) collective-permute-start(f32[384,512]{1,0:T(8,128)} %refs_0_.3), channel_id=1, source_target_pairs={{0,8},{4,12},{8,0},{12,4},{16,24},{20,28},{24,16},{28,20},{1,9},{5... | collective-permute-start | bytes 2359304 | tf_op jit(solution)/shard_map/ppermute | solution.py:158
  5.6 1.5 %collective-permute-start.1 = (f32[256,768]{1,0:T(8,128)}, f32[256,768]{1,0:T(8,128)S(1)}, u32[]{:S(2)}, u32[]{:S(2)}) collective-permute-start(f32[256,768]{1,0:T(8,128)} %refs_0_.2), channel_id=1, source_target_pairs={{0,1},{1,0},{2,3},{3,2},{4,5},{5,4},{6,7},{7,6},{8,9},{9,8},{10,11... | collective-permute-start | bytes 2359304 | tf_op jit(solution)/shard_map/ppermute | solution.py:164
  7.1 1.5 %collective-permute-start.2 = (f32[256,768]{1,0:T(8,128)}, f32[256,768]{1,0:T(8,128)S(1)}, u32[]{:S(2)}, u32[]{:S(2)}) collective-permute-start(f32[256,768]{1,0:T(8,128)} %refs_0_.2), channel_id=1, source_target_pairs={{0,2},{1,3},{2,0},{3,1},{4,6},{5,7},{6,4},{7,5},{8,10},{9,11},{10,... | collective-permute-start | bytes 2359304 | tf_op jit(solution)/shard_map/ppermute | solution.py:164
  8.6 0.5 collective-permute-start.3
  9.1 0.7 %copy-done.2 = s32[3072,2]{0,1:T(2,128)S(1)} copy-done((s32[3072,2]{0,1:T(2,128)S(1)}, s32[3072,2]{0,1:T(2,128)}, u32[]{:S(2)}) %copy-start.2) | copy-done | bytes 24600
  9.8 0.7 %copy-done.3 = f32[2048]{0:T(1024)S(1)} copy-done((f32[2048]{0:T(1024)S(1)}, f32[2048]{0:T(1024)}, u32[]{:S(2)}) %copy-start.3) | copy-done | bytes 8216
  10.5 7.0 %vir_sums.1.vir_sum = f32[1,3072]{1,0:T(1,128)S(1)} custom-call(f32[16,128]{1,0:T(8,128)S(1)} %bitcast.29, s32[2,3072]{1,0:T(2,128)S(1)} %bitcast.28), custom_call_target="tpu_custom_call" | custom-call | tf_op jit(solution)/shard_map/vir_sums/pallas_call | solution.py:47
  17.6 0.1 stack.99.bases
  17.7 0.7 %fusion.2 = s32[3072]{0:T(1024)S(1)} fusion(s32[3072]{0:T(1024)} %param.13, s32[]{:T(128)S(6)} %axis_index.25), kind=kLoop, calls=%fused_computation.4 | loop fusion | flops 46080 | bytes 24580 | tf_op jit(solution)/shard_map/add | solution.py:171
  18.4 20.3 %collective-permute-done.refs_2_ = f32[384,512]{1,0:T(8,128)S(1)} collective-permute-done((f32[384,512]{1,0:T(8,128)}, f32[384,512]{1,0:T(8,128)S(1)}, u32[]{:S(2)}, u32[]{:S(2)}) %collective-permute-start) | collective-permute-done | bytes 786464 | tf_op jit(solution)/shard_map/ppermute | solution.py:158
  38.7 0.7 %collective-permute-start.5 = (f32[384,512]{1,0:T(8,128)S(1)}, f32[384,512]{1,0:T(8,128)S(1)}, u32[]{:S(2)}, u32[]{:S(2)}) collective-permute-start(f32[384,512]{1,0:T(8,128)S(1)} %collective-permute-done.refs_2_), channel_id=1, source_target_pairs={{0,8},{4,12},{8,0},{12,4},{16,24},{20,28},{24,16},{28,20},{1,9},{5... | collective-permute-start | bytes 2359304 | tf_op jit(solution)/shard_map/ppermute | solution.py:158
  39.5 0.0 collective-permute-done.4.refs_1_
  39.5 0.0 collective-permute-start.7
  39.5 0.0 copy-start.4
  39.5 0.7 %copy-done.4 = s32[256,2]{0,1:T(2,128)S(1)} copy-done((s32[256,2]{0,1:T(2,128)S(1)}, s32[256,2]{0,1:T(2,128)}, u32[]{:S(2)}) %copy-start.4) | copy-done | bytes 2072
  40.2 0.7 %copy-done.5 = f32[256]{0:T(256)S(1)} copy-done((f32[256]{0:T(256)S(1)}, f32[256]{0:T(256)}, u32[]{:S(2)}) %copy-start.5) | copy-done | bytes 1048
  40.9 0.2 occ_sums.1.occ_sum
  41.0 0.0 collective-permute-done.1.refs_1_
  41.0 0.6 collective-permute-start.9
  41.6 1.0 %collective-permute-done.2.refs_2_ = f32[256,768]{1,0:T(8,128)S(1)} collective-permute-done((f32[256,768]{1,0:T(8,128)}, f32[256,768]{1,0:T(8,128)S(1)}, u32[]{:S(2)}, u32[]{:S(2)}) %collective-permute-start.2) | collective-permute-done | bytes 786464 | tf_op jit(solution)/shard_map/ppermute | solution.py:164
  42.6 0.0 collective-permute-done.3.refs_3_
  42.6 0.0 collective-permute-start.8
  42.6 0.0 copy-start
  42.6 1.1 %copy-done = f32[256,768]{1,0:T(8,128)S(1)} copy-done((f32[256,768]{1,0:T(8,128)S(1)}, f32[256,768]{1,0:T(8,128)}, u32[]{:S(2)}) %copy-start) | copy-done | bytes 786456
  43.8 7.2 %ordered.1 = (bf16[256,3072]{1,0:T(8,128)(2,1)S(1)}, bf16[256,3072]{1,0:T(8,128)(2,1)S(1)}) custom-call(s32[3072]{0:T(1024)S(1)} %broadcast_multiply_fusion.row_of, s32[4]{0:T(128)S(1)} %xor_multiply_fusion.starts, s32[24]{0:T(128)S(1)} %stack.99.bases, f32[1,256]{1,0:T(1,128)S(1)} %occ_sums.1.occ_sum, f32[1,3072]{1,0:T(1,128)S(1)} %vir_sums.1.vir_sum, ...), custom_call_target="tpu_custom_call" | custom-call | tf_op jit(solution)/shard_map/ordered/pallas_call | solution.py:91
  51.0 2.5 %summed.3.refs_4_ = f32[256,512]{1,0:T(8,128)S(1)} custom-call(bf16[256,3072]{1,0:T(8,128)(2,1)S(1)} %get-tuple-element.27.high, bf16[256,3072]{1,0:T(8,128)(2,1)S(1)} %get-tuple-element.28.low, f32[384,512]{1,0:T(8,128)S(1)} %copy-done.1, f32[384,512]{1,0:T(8,128)} %collective-permute-done.4.refs_1_, f32[384,512]{1,0:T(8,128)S(1)} %collective-permute-done.refs_2_), custom_call_target="tpu_custom_call" | custom-call | tf_op jit(solution)/shard_map/summed/pallas_call | solution.py:141
  53.5 3.9 %collective-permute-done.5.refs_3_ = f32[384,512]{1,0:T(8,128)S(1)} collective-permute-done((f32[384,512]{1,0:T(8,128)S(1)}, f32[384,512]{1,0:T(8,128)S(1)}, u32[]{:S(2)}, u32[]{:S(2)}) %collective-permute-start.5) | collective-permute-done | bytes 786464 | tf_op jit(solution)/shard_map/ppermute | solution.py:158
  57.4 0.0 collective-permute-done.7.refs_0_
  57.4 1.8 %summed.4.refs_1_ = f32[256,512]{1,0:T(8,128)S(1)} custom-call(bf16[256,3072]{1,0:T(8,128)(2,1)S(1)} %get-tuple-element.27.high, bf16[256,3072]{1,0:T(8,128)(2,1)S(1)} %get-tuple-element.28.low, f32[384,512]{1,0:T(8,128)S(1)} %collective-permute-done.7.refs_0_, f32[384,512]{1,0:T(8,128)S(1)} %collective-permute-done.8.refs_1_, ...), custom_call_target="tpu_custom_call" | custom-call | tf_op jit(solution)/shard_map/summed/pallas_call | solution.py:141
  59.2 0.5 collective-permute-done.6.refs_0_
  59.7 1.3 %summed.5 = f32[256,512]{1,0:T(8,128)} custom-call(bf16[256,3072]{1,0:T(8,128)(2,1)S(1)} %get-tuple-element.27.high, bf16[256,3072]{1,0:T(8,128)(2,1)S(1)} %get-tuple-element.28.low, f32[384,512]{1,0:T(8,128)S(1)} %collective-permute-done.6.refs_0_, f32[256,512]{1,0:T(8,128)S(1)} %summed.4.refs_1_), custom_call_target="tpu_custom_call" | custom-call | tf_op jit(solution)/shard_map/summed/pallas_call | solution.py:141
  (10 shorter events, 0.0 us)
Async XLA Ops:
  0.0 38.7 %collective-permute-start = (f32[384,512]{1,0:T(8,128)}, f32[384,512]{1,0:T(8,128)S(1)}, u32[]{:S(2)}, u32[]{:S(2)}) collective-permute-start(f32[384,512]{1,0:T(8,128)} %refs_0_.3), channel_id=1, source_target_pairs={{0,16},{4,20},{8,24},{12,28},{16,0},{20,4},{24,8},{28,12},{1,17},{... | collective-permute-start | bytes 2359304 | tf_op jit(solution)/shard_map/ppermute | solution.py:158
  4.0 35.4 %collective-permute-start.4 = (f32[384,512]{1,0:T(8,128)}, f32[384,512]{1,0:T(8,128)}, u32[]{:S(2)}, u32[]{:S(2)}) collective-permute-start(f32[384,512]{1,0:T(8,128)} %refs_0_.3), channel_id=1, source_target_pairs={{0,8},{4,12},{8,0},{12,4},{16,24},{20,28},{24,16},{28,20},{1,9},{5... | collective-permute-start | bytes 2359304 | tf_op jit(solution)/shard_map/ppermute | solution.py:158
  5.6 35.4 %collective-permute-start.1 = (f32[256,768]{1,0:T(8,128)}, f32[256,768]{1,0:T(8,128)S(1)}, u32[]{:S(2)}, u32[]{:S(2)}) collective-permute-start(f32[256,768]{1,0:T(8,128)} %refs_0_.2), channel_id=1, source_target_pairs={{0,1},{1,0},{2,3},{3,2},{4,5},{5,4},{6,7},{7,6},{8,9},{9,8},{10,11... | collective-permute-start | bytes 2359304 | tf_op jit(solution)/shard_map/ppermute | solution.py:164
  7.1 35.5 %collective-permute-start.2 = (f32[256,768]{1,0:T(8,128)}, f32[256,768]{1,0:T(8,128)S(1)}, u32[]{:S(2)}, u32[]{:S(2)}) collective-permute-start(f32[256,768]{1,0:T(8,128)} %refs_0_.2), channel_id=1, source_target_pairs={{0,2},{1,3},{2,0},{3,1},{4,6},{5,7},{6,4},{7,5},{8,10},{9,11},{10,... | collective-permute-start | bytes 2359304 | tf_op jit(solution)/shard_map/ppermute | solution.py:164
  8.6 34.0 %collective-permute-start.3 = (f32[256,768]{1,0:T(8,128)}, f32[256,768]{1,0:T(8,128)S(1)}, u32[]{:S(2)}, u32[]{:S(2)}) collective-permute-start(f32[256,768]{1,0:T(8,128)} %refs_0_.2), channel_id=1, source_target_pairs={{0,3},{1,2},{2,1},{3,0},{4,7},{5,6},{6,5},{7,4},{8,11},{9,10},{10,... | collective-permute-start | bytes 2359304 | tf_op jit(solution)/shard_map/ppermute | solution.py:164
  9.1 0.7 %copy-start.2 = (s32[3072,2]{0,1:T(2,128)S(1)}, s32[3072,2]{0,1:T(2,128)}, u32[]{:S(2)}) copy-start(s32[3072,2]{0,1:T(2,128)} %param.12) | copy-start | bytes 73732
  9.8 0.7 %copy-start.3 = (f32[2048]{0:T(1024)S(1)}, f32[2048]{0:T(1024)}, u32[]{:S(2)}) copy-start(f32[2048]{0:T(1024)} %param.10) | copy-start | bytes 24580
  38.7 18.7 %collective-permute-start.5 = (f32[384,512]{1,0:T(8,128)S(1)}, f32[384,512]{1,0:T(8,128)S(1)}, u32[]{:S(2)}, u32[]{:S(2)}) collective-permute-start(f32[384,512]{1,0:T(8,128)S(1)} %collective-permute-done.refs_2_), channel_id=1, source_target_pairs={{0,8},{4,12},{8,0},{12,4},{16,24},{20,28},{24,16},{28,20},{1,9},{5... | collective-permute-start | bytes 2359304 | tf_op jit(solution)/shard_map/ppermute | solution.py:158
  39.5 17.9 %collective-permute-start.7 = (f32[384,512]{1,0:T(8,128)}, f32[384,512]{1,0:T(8,128)S(1)}, u32[]{:S(2)}, u32[]{:S(2)}) collective-permute-start(f32[384,512]{1,0:T(8,128)} %refs_0_.3), channel_id=1, source_target_pairs={{0,4},{4,0},{8,12},{12,8},{16,20},{20,16},{24,28},{28,24},{1,5},{5... | collective-permute-start | bytes 2359304 | tf_op jit(solution)/shard_map/ppermute | solution.py:161
  39.5 0.7 %copy-start.4 = (s32[256,2]{0,1:T(2,128)S(1)}, s32[256,2]{0,1:T(2,128)}, u32[]{:S(2)}) copy-start(s32[256,2]{0,1:T(2,128)} %param.11) | copy-start | bytes 6148
  40.2 0.7 %copy-start.5 = (f32[256]{0:T(256)S(1)}, f32[256]{0:T(256)}, u32[]{:S(2)}) copy-start(f32[256]{0:T(256)} %param.9) | copy-start | bytes 3076
  41.0 16.4 %collective-permute-start.9 = (f32[384,512]{1,0:T(8,128)S(1)}, f32[384,512]{1,0:T(8,128)S(1)}, u32[]{:S(2)}, u32[]{:S(2)}) collective-permute-start(f32[384,512]{1,0:T(8,128)S(1)} %collective-permute-done.refs_2_), channel_id=1, source_target_pairs={{0,4},{4,0},{8,12},{12,8},{16,20},{20,16},{24,28},{28,24},{1,5},{5... | collective-permute-start | bytes 2359304 | tf_op jit(solution)/shard_map/ppermute | solution.py:161
  42.6 14.8 %collective-permute-start.8 = (f32[384,512]{1,0:T(8,128)}, f32[384,512]{1,0:T(8,128)S(1)}, u32[]{:S(2)}, u32[]{:S(2)}) collective-permute-start(f32[384,512]{1,0:T(8,128)} %collective-permute-done.4.refs_1_), channel_id=1, source_target_pairs={{0,4},{4,0},{8,12},{12,8},{16,20},{20,16},{24,28},{28,24},{1,5},{5... | collective-permute-start | bytes 2359304 | tf_op jit(solution)/shard_map/ppermute | solution.py:161
  42.6 1.1 %copy-start = (f32[256,768]{1,0:T(8,128)S(1)}, f32[256,768]{1,0:T(8,128)}, u32[]{:S(2)}) copy-start(f32[256,768]{1,0:T(8,128)} %refs_0_.2) | copy-start | bytes 2359300
  43.8 7.2 %copy-start.1 = (f32[384,512]{1,0:T(8,128)S(1)}, f32[384,512]{1,0:T(8,128)}, u32[]{:S(2)}) copy-start(f32[384,512]{1,0:T(8,128)} %refs_0_.3) | copy-start | bytes 2359300
  57.4 2.3 %collective-permute-start.6 = (f32[384,512]{1,0:T(8,128)S(1)}, f32[384,512]{1,0:T(8,128)S(1)}, u32[]{:S(2)}, u32[]{:S(2)}) collective-permute-start(f32[384,512]{1,0:T(8,128)S(1)} %collective-permute-done.5.refs_3_), channel_id=1, source_target_pairs={{0,4},{4,0},{8,12},{12,8},{16,20},{20,16},{24,28},{28,24},{1,5},{5... | collective-permute-start | bytes 2359304 | tf_op jit(solution)/shard_map/ppermute | solution.py:161

commit v5 on v4

--- a/solution.py
+++ b/solution.py
@@ -94,17 +94,20 @@
         in_specs=[SMEM, SMEM, SMEM] + [VMEM] * (2 + len(blocks)),
         out_shape=(jax.ShapeDtypeStruct((rows, pairs), jnp.bfloat16),) * 2,
         scratch_shapes=[
-            pltpu.VMEM((pairs * tiles, LANES), jnp.float32),
-            pltpu.VMEM((RUN * tiles, LANES), jnp.float32),
+            pltpu.VMEM((pairs * tiles + 8, LANES), jnp.float32),
+            pltpu.VMEM((RUN * tiles + 8, LANES), jnp.float32),
         ],
         compiler_params=PARAMS,
     )(place_of * tiles, starts, bases, occ_sum, vir_sum, *blocks)
 
 
 def product(high, low, block):
-    dot = functools.partial(jnp.dot, preferred_element_type=jnp.float32)
     block_high, block_low = split(block)
-    return dot(high, block_high) + (dot(high, block_low) + dot(low, block_high))
+    return jnp.dot(
+        jnp.concatenate([high, low, high], axis=1),
+        jnp.concatenate([block_high, block_high, block_low], axis=0),
+        preferred_element_type=jnp.float32,
+    )
 
 
 def product_kernel(first, sizes, has_total, last, high, low, *refs):
@@ -154,8 +157,8 @@
     chip, core = row // 2, row % 2
     width, depth = raw_amps.shape[1], integrals.shape[0]
 
-    def other_chip(block, mask):
-        return lax.ppermute(block, "row", [(i, i ^ (2 * mask)) for i in range(8)])
+    def between_chips(block, pairs):
+        return lax.ppermute(block, "row", [(2 * a + c, 2 * b + c) for a, b in pairs for c in range(2)])
 
     def other_core(block):
         return lax.ppermute(block, "row", [(i, i ^ 1) for i in range(8)])
@@ -163,27 +166,31 @@
     def across(block, mask):
         return lax.ppermute(block, "col", [(i, i ^ mask) for i in range(4)])
 
-    next_chip, second_chip = other_chip(integrals, 1), other_chip(integrals, 2)
-    raw = [across(raw_amps, mask) for mask in (1, 2, 3)]
+    one = between_chips(integrals, [(0, 2), (3, 1), (1, 0), (2, 3)])
+    two = between_chips(integrals, [(1, 3), (2, 0), (0, 1), (3, 2)])
+    raw_x, raw_y = across(raw_amps, 1), across(raw_amps, 2)
+    at_end = (chip == 0) | (chip == 3)
 
     vir_sum = energy_sums(vir_energy, vir_pairs, "vir_sums")
     starts = (col ^ jnp.arange(4, dtype=jnp.int32)) * width
     place_of = ((pair_order // width) ^ col) * width + pair_order % width
-    blocks = ((0, 0), (1, 0), (2, 0), (0, 1), (1, 1), (2, 1), (3, 0), (3, 1))
-    runs = [(m, s, at) for m, s in blocks for at in range(0, depth, RUN)]
+    blocks = ((0, 0, 0), (1, 2, 0), (2, 1, 0), (0, 0, 1), (1, 2, 1), (2, 1, 1), (3, 3, 0), (3, 3, 1))
+    runs = [(jnp.where(at_end, end, inner), s, at) for end, inner, s in blocks for at in range(0, depth, RUN)]
     bases = jnp.stack([((chip ^ m) * 2 + (core ^ s)) * depth + at for m, s, at in runs])
 
-    second_chip, vir_sum, bases, place_of = lax.optimization_barrier((second_chip, vir_sum, bases, place_of))
-    third_chip = other_chip(second_chip, 1)
-    next_chip, occ_energy = lax.optimization_barrier((next_chip, occ_energy))
-    occ_sum = energy_sums(occ_energy, occ_pairs, "occ_sums", None)
-    *raw, occ_sum = lax.optimization_barrier((*raw, occ_sum))
-    high, low = ordered(place_of, starts, bases, occ_sum, vir_sum, raw_amps, *raw)
-    own = [integrals, next_chip, second_chip]
-    total = summed(high, low, 0, own)
-    third_chip, total = lax.optimization_barrier((third_chip, total))
-    total = summed(high, low, 3 * depth, [other_core(block) for block in own] + [third_chip], total)
-    return summed(high, low, 7 * depth, [other_core(third_chip)], total, last=True)
+    raw_d = across(raw_amps, 3)
+    one, vir_sum, bases, place_of = lax.optimization_barrier((one, vir_sum, bases, place_of))
+    far = between_chips(one, [(1, 0), (2, 3)])
+    raw_x, own = lax.optimization_barrier((raw_x, integrals))
+    middle = between_chips(own, [(1, 2), (2, 1)])
+    third = jnp.where(at_end, far, middle)
+    occ_sum = energy_sums(occ_energy, occ_pairs, "occ_sums")
+    high, low = ordered(place_of, starts, bases, occ_sum, vir_sum, raw_amps, raw_x, raw_y, raw_d)
+    total = summed(high, low, 0, [integrals, one, two])
+    third, total = lax.optimization_barrier((third, total))
+    crossed = [other_core(block) for block in (integrals, one, two)]
+    total = summed(high, low, 3 * depth, crossed + [third], total)
+    return summed(high, low, 7 * depth, [other_core(third)], total, last=True)
 
 
 def any_mesh(raw_amps, integrals, occ_energy, vir_energy, occ_pairs, vir_pairs, pair_order):

time: 61.4 us -> 60.7 us (0.989)
    ppermute x3 -> x4, waiting for transfers between devices: 24.2 us -> 9.47 us  [between_chips(): lax.ppermute(block, 'row', [(2 * a + c, 2 * b + c) for a, b in pairs for...]
    ppermute x3, waiting for transfers between devices: 1.01 us -> 15.4 us  [across(): return lax.ppermute(block, 'col', [(i, i ^ mask) for i in range(4)])]
    ppermute x3 -> x4, starting transfers between devices: 6.33 us -> 6.03 us  [between_chips(): lax.ppermute(block, 'row', [(2 * a + c, 2 * b + c) for a, b in pairs for...]
  transfers between devices with their start and end apart: 10 -> 11, of which waited for: 4 -> 5; matrix products, arithmetic and copies ran while one was open for 1% -> 2% of each run, Pallas kernels for 31% -> 30%
where the time goes in v5:
time: 60.7 us; the launch traced here: 60.3 us
  waiting for transfers between devices  25.6 us (42%)
  Pallas kernels  19.5 us (32%)
  starting transfers between devices  10.2 us (17%)
  local copies, waits for them, and re-layouts  4.04 us (7%)
  other arithmetic  0.88 us (1%)
    ppermute x3, waiting for transfers between devices, across(): return lax.ppermute(block, 'col', [(i, i ^ mask) for i in range(4)])  15.4 us
    ppermute x4, waiting for transfers between devices, between_chips(): lax.ppermute(block, 'row', [(2 * a + c, 2 * b + c) for a, b in pairs for...  9.47 us
    pallas_call x1, Pallas kernels, ordered(): pl.pallas_call(order_kernel, name='ordered', in_specs=[SMEM, SMEM, SMEM]...  7.21 us
    pallas_call x2, Pallas kernels, energy_sums(): pl.pallas_call(look_up, name=name, out_shape=jax.ShapeDtypeStruct((1, pai...  7.19 us
    ppermute x4, starting transfers between devices, between_chips(): lax.ppermute(block, 'row', [(2 * a + c, 2 * b + c) for a, b in pairs for...  6.03 us
    pallas_call x3, Pallas kernels, summed(): pl.pallas_call(functools.partial(product_kernel, first, sizes, total is n...  5.1 us
    unnamed x12, local copies, waits for them, and re-layouts  3.93 us
    ppermute x3, starting transfers between devices, across(): return lax.ppermute(block, 'col', [(i, i ^ mask) for i in range(4)])  3.49 us
  transfers between devices with their start and end apart: 11, of which 5 were waited for; matrix products, arithmetic and copies ran while one was open for 2% of the time, Pallas kernels for 30%

profile of v5, /device:TPU:0, one launch (start us, length us, event | category | flops | bytes accessed | tf_op | source)
XLA Modules:
  0.0 60.3 jit_solution(6799063813070721511)
XLA Ops:
  0.0 4.0 %collective-permute-start = (f32[384,512]{1,0:T(8,128)}, f32[384,512]{1,0:T(8,128)S(1)}, u32[]{:S(2)}, u32[]{:S(2)}) collective-permute-start(f32[384,512]{1,0:T(8,128)} %refs_0_.3), channel_id=1, source_target_pairs={{0,16},{4,20},{24,8},{28,12},{8,0},{12,4},{16,24},{20,28},{1,17},{... | collective-permute-start | bytes 2359304 | tf_op jit(solution)/shard_map/ppermute | solution.py:161
  4.0 1.5 %collective-permute-start.1 = (f32[256,768]{1,0:T(8,128)}, f32[256,768]{1,0:T(8,128)S(1)}, u32[]{:S(2)}, u32[]{:S(2)}) collective-permute-start(f32[256,768]{1,0:T(8,128)} %refs_0_.2), channel_id=1, source_target_pairs={{0,1},{1,0},{2,3},{3,2},{4,5},{5,4},{6,7},{7,6},{8,9},{9,8},{10,11... | collective-permute-start | bytes 2359304 | tf_op jit(solution)/shard_map/ppermute | solution.py:167
  5.5 1.5 %collective-permute-start.2 = (f32[256,768]{1,0:T(8,128)}, f32[256,768]{1,0:T(8,128)S(1)}, u32[]{:S(2)}, u32[]{:S(2)}) collective-permute-start(f32[256,768]{1,0:T(8,128)} %refs_0_.2), channel_id=1, source_target_pairs={{0,2},{1,3},{2,0},{3,1},{4,6},{5,7},{6,4},{7,5},{8,10},{9,11},{10,... | collective-permute-start | bytes 2359304 | tf_op jit(solution)/shard_map/ppermute | solution.py:167
  7.0 0.5 collective-permute-start.3
  7.5 0.7 %copy-done.2 = s32[3072,2]{0,1:T(2,128)S(1)} copy-done((s32[3072,2]{0,1:T(2,128)S(1)}, s32[3072,2]{0,1:T(2,128)}, u32[]{:S(2)}) %copy-start.2) | copy-done | bytes 24600
  8.3 0.7 %copy-done.3 = f32[2048]{0:T(1024)S(1)} copy-done((f32[2048]{0:T(1024)S(1)}, f32[2048]{0:T(1024)}, u32[]{:S(2)}) %copy-start.3) | copy-done | bytes 8216
  9.0 7.0 %vir_sums.1.vir_sum = f32[1,3072]{1,0:T(1,128)S(1)} custom-call(f32[16,128]{1,0:T(8,128)S(1)} %bitcast.29, s32[2,3072]{1,0:T(2,128)S(1)} %bitcast.28), custom_call_target="tpu_custom_call" | custom-call | tf_op jit(solution)/shard_map/vir_sums/pallas_call | solution.py:47
  16.0 0.7 %fusion.2 = s32[3072]{0:T(1024)S(1)} fusion(s32[3072]{0:T(1024)} %param.13, s32[]{:T(128)S(6)} %axis_index.25), kind=kLoop, calls=%fused_computation.5 | loop fusion | flops 46080 | bytes 24580 | tf_op jit(solution)/shard_map/add | solution.py:176
  16.7 0.1 stack.99.bases
  16.8 5.5 %collective-permute-done.refs_1_ = f32[384,512]{1,0:T(8,128)S(1)} collective-permute-done((f32[384,512]{1,0:T(8,128)}, f32[384,512]{1,0:T(8,128)S(1)}, u32[]{:S(2)}, u32[]{:S(2)}) %collective-permute-start) | collective-permute-done | bytes 786464 | tf_op jit(solution)/shard_map/ppermute | solution.py:161
  22.3 2.4 %collective-permute-done.1.refs_1_ = f32[256,768]{1,0:T(8,128)S(1)} collective-permute-done((f32[256,768]{1,0:T(8,128)}, f32[256,768]{1,0:T(8,128)S(1)}, u32[]{:S(2)}, u32[]{:S(2)}) %collective-permute-start.1) | collective-permute-done | bytes 786464 | tf_op jit(solution)/shard_map/ppermute | solution.py:167
  24.7 1.3 %collective-permute-start.4 = (f32[384,512]{1,0:T(8,128)S(1)}, f32[384,512]{1,0:T(8,128)S(1)}, u32[]{:S(2)}, u32[]{:S(2)}) collective-permute-start(f32[384,512]{1,0:T(8,128)S(1)} %collective-permute-done.refs_1_), channel_id=1, source_target_pairs={{8,0},{12,4},{16,24},{20,28},{9,1},{13,5},{17,25},{21,29},{10,2},{... | collective-permute-start | bytes 2359304 | tf_op jit(solution)/shard_map/ppermute | solution.py:161
  26.0 0.7 %collective-permute-start.5 = (f32[384,512]{1,0:T(8,128)}, f32[384,512]{1,0:T(8,128)S(1)}, u32[]{:S(2)}, u32[]{:S(2)}) collective-permute-start(f32[384,512]{1,0:T(8,128)} %refs_0_.3), channel_id=1, source_target_pairs={{8,16},{12,20},{16,8},{20,12},{9,17},{13,21},{17,9},{21,13},{10,18... | collective-permute-start | bytes 2359304 | tf_op jit(solution)/shard_map/ppermute | solution.py:161
  26.7 0.0 copy-start.4
  26.7 0.7 %copy-done.4 = s32[256,2]{0,1:T(2,128)S(1)} copy-done((s32[256,2]{0,1:T(2,128)S(1)}, s32[256,2]{0,1:T(2,128)}, u32[]{:S(2)}) %copy-start.4) | copy-done | bytes 2072
  27.4 0.7 %copy-done.5 = f32[256]{0:T(256)S(1)} copy-done((f32[256]{0:T(256)S(1)}, f32[256]{0:T(256)}, u32[]{:S(2)}) %copy-start.5) | copy-done | bytes 1048
  28.1 0.2 occ_sums.1.occ_sum
  28.3 13.0 %collective-permute-done.2.refs_2_ = f32[256,768]{1,0:T(8,128)S(1)} collective-permute-done((f32[256,768]{1,0:T(8,128)}, f32[256,768]{1,0:T(8,128)S(1)}, u32[]{:S(2)}, u32[]{:S(2)}) %collective-permute-start.2) | collective-permute-done | bytes 786464 | tf_op jit(solution)/shard_map/ppermute | solution.py:167
  41.3 0.0 collective-permute-start.8
  41.3 0.0 collective-permute-done.3.refs_3_
  41.3 0.5 collective-permute-start.9
  41.8 0.0 collective-permute-done.6.refs_2_
  41.8 0.1 collective-permute-start.10
  41.9 1.1 %copy-done = f32[256,768]{1,0:T(8,128)S(1)} copy-done((f32[256,768]{1,0:T(8,128)S(1)}, f32[256,768]{1,0:T(8,128)}, u32[]{:S(2)}) %copy-start) | copy-done | bytes 786456
  43.0 7.2 %ordered.1 = (bf16[256,3072]{1,0:T(8,128)(2,1)S(1)}, bf16[256,3072]{1,0:T(8,128)(2,1)S(1)}) custom-call(s32[3072]{0:T(1024)S(1)} %broadcast_multiply_fusion.row_of, s32[4]{0:T(128)S(1)} %xor_multiply_fusion.starts, s32[24]{0:T(128)S(1)} %stack.99.bases, f32[1,256]{1,0:T(1,128)S(1)} %occ_sums.1.occ_sum, f32[1,3072]{1,0:T(1,128)S(1)} %vir_sums.1.vir_sum, ...), custom_call_target="tpu_custom_call" | custom-call | tf_op jit(solution)/shard_map/ordered/pallas_call | solution.py:91
  50.3 2.3 %summed.3.refs_4_ = f32[256,512]{1,0:T(8,128)S(1)} custom-call(bf16[256,3072]{1,0:T(8,128)(2,1)S(1)} %get-tuple-element.19.high, bf16[256,3072]{1,0:T(8,128)(2,1)S(1)} %get-tuple-element.20.low, f32[384,512]{1,0:T(8,128)S(1)} %copy-done.1, f32[384,512]{1,0:T(8,128)S(1)} %collective-permute-done.refs_1_, f32[384,512]{1,0:T(8,128)} %collective-permute-done.6.refs_2_), custom_call_target="tpu_custom_call" | custom-call | tf_op jit(solution)/shard_map/summed/pallas_call | solution.py:144
  52.6 4.0 %collective-permute-done.4 = f32[384,512]{1,0:T(8,128)S(1)} collective-permute-done((f32[384,512]{1,0:T(8,128)S(1)}, f32[384,512]{1,0:T(8,128)S(1)}, u32[]{:S(2)}, u32[]{:S(2)}) %collective-permute-start.4) | collective-permute-done | bytes 786464 | tf_op jit(solution)/shard_map/ppermute | solution.py:161
  56.6 0.1 broadcast_select_fusion.refs_3_
  56.7 0.1 collective-permute-start.7
  56.8 1.5 %summed.4.refs_1_ = f32[256,512]{1,0:T(8,128)S(1)} custom-call(bf16[256,3072]{1,0:T(8,128)(2,1)S(1)} %get-tuple-element.19.high, bf16[256,3072]{1,0:T(8,128)(2,1)S(1)} %get-tuple-element.20.low, f32[384,512]{1,0:T(8,128)S(1)} %collective-permute-done.8.refs_0_, f32[384,512]{1,0:T(8,128)S(1)} %collective-permute-done.9.refs_1_, ...), custom_call_target="tpu_custom_call" | custom-call | tf_op jit(solution)/shard_map/summed/pallas_call | solution.py:144
  58.4 0.7 %collective-permute-done.7.refs_0_ = f32[384,512]{1,0:T(8,128)S(1)} collective-permute-done((f32[384,512]{1,0:T(8,128)S(1)}, f32[384,512]{1,0:T(8,128)S(1)}, u32[]{:S(2)}, u32[]{:S(2)}) %collective-permute-start.7) | collective-permute-done | bytes 786464 | tf_op jit(solution)/shard_map/ppermute | solution.py:164
  59.1 1.3 %summed.5 = f32[256,512]{1,0:T(8,128)} custom-call(bf16[256,3072]{1,0:T(8,128)(2,1)S(1)} %get-tuple-element.19.high, bf16[256,3072]{1,0:T(8,128)(2,1)S(1)} %get-tuple-element.20.low, f32[384,512]{1,0:T(8,128)S(1)} %collective-permute-done.7.refs_0_, f32[256,512]{1,0:T(8,128)S(1)} %summed.4.refs_1_), custom_call_target="tpu_custom_call" | custom-call | tf_op jit(solution)/shard_map/summed/pallas_call | solution.py:144
  (13 shorter events, 0.0 us)
Async XLA Ops:
  0.0 22.3 %collective-permute-start = (f32[384,512]{1,0:T(8,128)}, f32[384,512]{1,0:T(8,128)S(1)}, u32[]{:S(2)}, u32[]{:S(2)}) collective-permute-start(f32[384,512]{1,0:T(8,128)} %refs_0_.3), channel_id=1, source_target_pairs={{0,16},{4,20},{24,8},{28,12},{8,0},{12,4},{16,24},{20,28},{1,17},{... | collective-permute-start | bytes 2359304 | tf_op jit(solution)/shard_map/ppermute | solution.py:161
  4.0 20.7 %collective-permute-start.1 = (f32[256,768]{1,0:T(8,128)}, f32[256,768]{1,0:T(8,128)S(1)}, u32[]{:S(2)}, u32[]{:S(2)}) collective-permute-start(f32[256,768]{1,0:T(8,128)} %refs_0_.2), channel_id=1, source_target_pairs={{0,1},{1,0},{2,3},{3,2},{4,5},{5,4},{6,7},{7,6},{8,9},{9,8},{10,11... | collective-permute-start | bytes 2359304 | tf_op jit(solution)/shard_map/ppermute | solution.py:167
  5.5 35.8 %collective-permute-start.2 = (f32[256,768]{1,0:T(8,128)}, f32[256,768]{1,0:T(8,128)S(1)}, u32[]{:S(2)}, u32[]{:S(2)}) collective-permute-start(f32[256,768]{1,0:T(8,128)} %refs_0_.2), channel_id=1, source_target_pairs={{0,2},{1,3},{2,0},{3,1},{4,6},{5,7},{6,4},{7,5},{8,10},{9,11},{10,... | collective-permute-start | bytes 2359304 | tf_op jit(solution)/shard_map/ppermute | solution.py:167
  7.0 34.3 %collective-permute-start.3 = (f32[256,768]{1,0:T(8,128)}, f32[256,768]{1,0:T(8,128)S(1)}, u32[]{:S(2)}, u32[]{:S(2)}) collective-permute-start(f32[256,768]{1,0:T(8,128)} %refs_0_.2), channel_id=1, source_target_pairs={{0,3},{1,2},{2,1},{3,0},{4,7},{5,6},{6,5},{7,4},{8,11},{9,10},{10,... | collective-permute-start | bytes 2359304 | tf_op jit(solution)/shard_map/ppermute | solution.py:167
  7.5 34.3 %collective-permute-start.6 = (f32[384,512]{1,0:T(8,128)}, f32[384,512]{1,0:T(8,128)}, u32[]{:S(2)}, u32[]{:S(2)}) collective-permute-start(f32[384,512]{1,0:T(8,128)} %refs_0_.3), channel_id=1, source_target_pairs={{8,24},{12,28},{16,0},{20,4},{0,8},{4,12},{24,16},{28,20},{9,25},{... | collective-permute-start | bytes 2359304 | tf_op jit(solution)/shard_map/ppermute | solution.py:161
  7.5 0.7 %copy-start.2 = (s32[3072,2]{0,1:T(2,128)S(1)}, s32[3072,2]{0,1:T(2,128)}, u32[]{:S(2)}) copy-start(s32[3072,2]{0,1:T(2,128)} %param.12) | copy-start | bytes 73732
  8.3 0.7 %copy-start.3 = (f32[2048]{0:T(1024)S(1)}, f32[2048]{0:T(1024)}, u32[]{:S(2)}) copy-start(f32[2048]{0:T(1024)} %param.10) | copy-start | bytes 24580
  24.7 31.8 %collective-permute-start.4 = (f32[384,512]{1,0:T(8,128)S(1)}, f32[384,512]{1,0:T(8,128)S(1)}, u32[]{:S(2)}, u32[]{:S(2)}) collective-permute-start(f32[384,512]{1,0:T(8,128)S(1)} %collective-permute-done.refs_1_), channel_id=1, source_target_pairs={{8,0},{12,4},{16,24},{20,28},{9,1},{13,5},{17,25},{21,29},{10,2},{... | collective-permute-start | bytes 2359304 | tf_op jit(solution)/shard_map/ppermute | solution.py:161
  26.0 30.6 %collective-permute-start.5 = (f32[384,512]{1,0:T(8,128)}, f32[384,512]{1,0:T(8,128)S(1)}, u32[]{:S(2)}, u32[]{:S(2)}) collective-permute-start(f32[384,512]{1,0:T(8,128)} %refs_0_.3), channel_id=1, source_target_pairs={{8,16},{12,20},{16,8},{20,12},{9,17},{13,21},{17,9},{21,13},{10,18... | collective-permute-start | bytes 2359304 | tf_op jit(solution)/shard_map/ppermute | solution.py:161
  26.7 0.7 %copy-start.4 = (s32[256,2]{0,1:T(2,128)S(1)}, s32[256,2]{0,1:T(2,128)}, u32[]{:S(2)}) copy-start(s32[256,2]{0,1:T(2,128)} %param.11) | copy-start | bytes 6148
  27.4 0.7 %copy-start.5 = (f32[256]{0:T(256)S(1)}, f32[256]{0:T(256)}, u32[]{:S(2)}) copy-start(f32[256]{0:T(256)} %param.9) | copy-start | bytes 3076
  41.3 15.5 %collective-permute-start.8 = (f32[384,512]{1,0:T(8,128)}, f32[384,512]{1,0:T(8,128)S(1)}, u32[]{:S(2)}, u32[]{:S(2)}) collective-permute-start(f32[384,512]{1,0:T(8,128)} %refs_0_.3), channel_id=1, source_target_pairs={{0,4},{4,0},{8,12},{12,8},{16,20},{20,16},{24,28},{28,24},{1,5},{5... | collective-permute-start | bytes 2359304 | tf_op jit(solution)/shard_map/ppermute | solution.py:164
  41.3 15.5 %collective-permute-start.9 = (f32[384,512]{1,0:T(8,128)S(1)}, f32[384,512]{1,0:T(8,128)S(1)}, u32[]{:S(2)}, u32[]{:S(2)}) collective-permute-start(f32[384,512]{1,0:T(8,128)S(1)} %collective-permute-done.refs_1_), channel_id=1, source_target_pairs={{0,4},{4,0},{8,12},{12,8},{16,20},{20,16},{24,28},{28,24},{1,5},{5... | collective-permute-start | bytes 2359304 | tf_op jit(solution)/shard_map/ppermute | solution.py:164
  41.8 15.0 %collective-permute-start.10 = (f32[384,512]{1,0:T(8,128)}, f32[384,512]{1,0:T(8,128)S(1)}, u32[]{:S(2)}, u32[]{:S(2)}) collective-permute-start(f32[384,512]{1,0:T(8,128)} %collective-permute-done.6.refs_2_), channel_id=1, source_target_pairs={{0,4},{4,0},{8,12},{12,8},{16,20},{20,16},{24,28},{28,24},{1,5},{5... | collective-permute-start | bytes 2359304 | tf_op jit(solution)/shard_map/ppermute | solution.py:164
  41.9 1.1 %copy-start = (f32[256,768]{1,0:T(8,128)S(1)}, f32[256,768]{1,0:T(8,128)}, u32[]{:S(2)}) copy-start(f32[256,768]{1,0:T(8,128)} %refs_0_.2) | copy-start | bytes 2359300
  43.0 7.2 %copy-start.1 = (f32[384,512]{1,0:T(8,128)S(1)}, f32[384,512]{1,0:T(8,128)}, u32[]{:S(2)}) copy-start(f32[384,512]{1,0:T(8,128)} %refs_0_.3) | copy-start | bytes 2359300
  56.7 2.4 %collective-permute-start.7 = (f32[384,512]{1,0:T(8,128)S(1)}, f32[384,512]{1,0:T(8,128)S(1)}, u32[]{:S(2)}, u32[]{:S(2)}) collective-permute-start(f32[384,512]{1,0:T(8,128)S(1)} %broadcast_select_fusion.refs_3_), channel_id=1, source_target_pairs={{0,4},{4,0},{8,12},{12,8},{16,20},{20,16},{24,28},{28,24},{1,5},{5... | collective-permute-start | bytes 2359304 | tf_op jit(solution)/shard_map/ppermute | solution.py:164

commit v6 on v5

--- a/solution.py
+++ b/solution.py
@@ -168,29 +168,38 @@
 
     one = between_chips(integrals, [(0, 2), (3, 1), (1, 0), (2, 3)])
     two = between_chips(integrals, [(1, 3), (2, 0), (0, 1), (3, 2)])
-    raw_x, raw_y = across(raw_amps, 1), across(raw_amps, 2)
+    raw_x, raw_y, raw_d = [across(raw_amps, mask) for mask in (1, 2, 3)]
     at_end = (chip == 0) | (chip == 3)
-
+    cut = 256
+
+    crossed_own, vir_energy = lax.optimization_barrier((other_core(integrals), vir_energy))
     vir_sum = energy_sums(vir_energy, vir_pairs, "vir_sums")
     starts = (col ^ jnp.arange(4, dtype=jnp.int32)) * width
     place_of = ((pair_order // width) ^ col) * width + pair_order % width
-    blocks = ((0, 0, 0), (1, 2, 0), (2, 1, 0), (0, 0, 1), (1, 2, 1), (2, 1, 1), (3, 3, 0), (3, 3, 1))
-    runs = [(jnp.where(at_end, end, inner), s, at) for end, inner, s in blocks for at in range(0, depth, RUN)]
+    whole, first, second = range(0, depth, RUN), range(0, cut, RUN), range(cut, depth, RUN)
+    blocks = [(end, inner, s, whole) for s in range(2) for end, inner in ((0, 0), (1, 2), (2, 1))]
+    blocks += [(3, 3, s, part) for part in (first, second) for s in range(2)]
+    runs = [(jnp.where(at_end, end, inner), s, at) for end, inner, s, part in blocks for at in part]
     bases = jnp.stack([((chip ^ m) * 2 + (core ^ s)) * depth + at for m, s, at in runs])
 
-    raw_d = across(raw_amps, 3)
-    one, vir_sum, bases, place_of = lax.optimization_barrier((one, vir_sum, bases, place_of))
-    far = between_chips(one, [(1, 0), (2, 3)])
-    raw_x, own = lax.optimization_barrier((raw_x, integrals))
-    middle = between_chips(own, [(1, 2), (2, 1)])
-    third = jnp.where(at_end, far, middle)
     occ_sum = energy_sums(occ_energy, occ_pairs, "occ_sums")
+    one, vir_sum, occ_sum, starts, bases, place_of, mine = lax.optimization_barrier(
+        (one, vir_sum, occ_sum, starts, bases, place_of, integrals)
+    )
+    far_a = between_chips(one[:cut], [(1, 0), (2, 3)])
+    raw_x, mine = lax.optimization_barrier((raw_x, mine))
+    middle = between_chips(mine, [(1, 2), (2, 1)])
+    far_b = between_chips(one[cut:], [(1, 0), (2, 3)])
     high, low = ordered(place_of, starts, bases, occ_sum, vir_sum, raw_amps, raw_x, raw_y, raw_d)
-    total = summed(high, low, 0, [integrals, one, two])
-    third, total = lax.optimization_barrier((third, total))
-    crossed = [other_core(block) for block in (integrals, one, two)]
-    total = summed(high, low, 3 * depth, crossed + [third], total)
-    return summed(high, low, 7 * depth, [other_core(third)], total, last=True)
+    total = summed(high, low, 0, [integrals, one, two, crossed_own])
+    far_a, middle, total = lax.optimization_barrier((far_a, middle, total))
+    third_a = jnp.where(at_end, far_a, middle[:cut])
+    crossed_a = other_core(third_a)
+    total = summed(high, low, 4 * depth, [other_core(one), other_core(two)], total)
+    far_b, total = lax.optimization_barrier((far_b, total))
+    third_b = jnp.where(at_end, far_b, middle[cut:])
+    total = summed(high, low, 6 * depth, [third_a, crossed_a, third_b], total)
+    return summed(high, low, 7 * depth + cut, [other_core(third_b)], total, last=True)
 
 
 def any_mesh(raw_amps, integrals, occ_energy, vir_energy, occ_pairs, vir_pairs, pair_order):

time: 60.7 us -> 60.3 us (level)
  starting transfers between devices: 10.2 us -> 11.7 us
  waiting for transfers between devices: 25.6 us -> 24.2 us
  local copies, waits for them, and re-layouts: 4.04 us -> 2.97 us
    ppermute x4 -> x5, waiting for transfers between devices: 9.47 us -> 5.76 us  [between_chips(): lax.ppermute(block, 'row', [(2 * a + c, 2 * b + c) for a, b in pairs for...]
    ppermute x3, waiting for transfers between devices: 15.4 us -> 17.6 us  [across(): return lax.ppermute(block, 'col', [(i, i ^ mask) for i in range(4)])]
    unnamed x12, local copies, waits for them, and re-layouts: 3.93 us -> 2.8 us
    ppermute x4 -> x5, starting transfers between devices: 6.03 us -> 7.05 us  [between_chips(): lax.ppermute(block, 'row', [(2 * a + c, 2 * b + c) for a, b in pairs for...]
    pallas_call x3 -> x4, Pallas kernels: 5.1 us -> 5.57 us  [summed(): pl.pallas_call(functools.partial(product_kernel, first, sizes, total is n...]
  transfers between devices with their start and end apart: 11 -> 13, of which waited for: 5 -> 5; matrix products, arithmetic and copies ran while one was open for 2% -> 2% of each run, Pallas kernels for 30% -> 32%
where the time goes in v6:
time: 60.3 us; the launch traced here: 59.9 us
  waiting for transfers between devices  24.2 us (40%)
  Pallas kernels  20 us (33%)
  starting transfers between devices  11.7 us (19%)
  local copies, waits for them, and re-layouts  2.97 us (5%)
  other arithmetic  0.85 us (1%)
    ppermute x3, waiting for transfers between devices, across(): return lax.ppermute(block, 'col', [(i, i ^ mask) for i in range(4)])  17.6 us
    pallas_call x1, Pallas kernels, ordered(): pl.pallas_call(order_kernel, name='ordered', in_specs=[SMEM, SMEM, SMEM]...  7.22 us
    pallas_call x2, Pallas kernels, energy_sums(): pl.pallas_call(look_up, name=name, out_shape=jax.ShapeDtypeStruct((1, pai...  7.19 us
    ppermute x5, starting transfers between devices, between_chips(): lax.ppermute(block, 'row', [(2 * a + c, 2 * b + c) for a, b in pairs for...  7.05 us
    ppermute x5, waiting for transfers between devices, between_chips(): lax.ppermute(block, 'row', [(2 * a + c, 2 * b + c) for a, b in pairs for...  5.76 us
    pallas_call x4, Pallas kernels, summed(): pl.pallas_call(functools.partial(product_kernel, first, sizes, total is n...  5.57 us
    ppermute x3, starting transfers between devices, across(): return lax.ppermute(block, 'col', [(i, i ^ mask) for i in range(4)])  3.55 us
    unnamed x12, local copies, waits for them, and re-layouts  2.8 us
  transfers between devices with their start and end apart: 13, of which 5 were waited for; matrix products, arithmetic and copies ran while one was open for 2% of the time, Pallas kernels for 32%

profile of v6, /device:TPU:0, one launch (start us, length us, event | category | flops | bytes accessed | tf_op | source)
XLA Modules:
  0.0 59.9 jit_solution(415459058141792474)
XLA Ops:
  0.0 0.5 collective-permute-start.1
  0.5 3.6 %collective-permute-start = (f32[384,512]{1,0:T(8,128)}, f32[384,512]{1,0:T(8,128)S(1)}, u32[]{:S(2)}, u32[]{:S(2)}) collective-permute-start(f32[384,512]{1,0:T(8,128)} %refs_0_.3), channel_id=1, source_target_pairs={{0,16},{4,20},{24,8},{28,12},{8,0},{12,4},{16,24},{20,28},{1,17},{... | collective-permute-start | bytes 2359304 | tf_op jit(solution)/shard_map/ppermute | solution.py:161
  4.1 1.5 %collective-permute-start.2 = (f32[256,768]{1,0:T(8,128)}, f32[256,768]{1,0:T(8,128)S(1)}, u32[]{:S(2)}, u32[]{:S(2)}) collective-permute-start(f32[256,768]{1,0:T(8,128)} %refs_0_.2), channel_id=1, source_target_pairs={{0,1},{1,0},{2,3},{3,2},{4,5},{5,4},{6,7},{7,6},{8,9},{9,8},{10,11... | collective-permute-start | bytes 2359304 | tf_op jit(solution)/shard_map/ppermute | solution.py:167
  5.6 1.5 %collective-permute-start.3 = (f32[256,768]{1,0:T(8,128)}, f32[256,768]{1,0:T(8,128)S(1)}, u32[]{:S(2)}, u32[]{:S(2)}) collective-permute-start(f32[256,768]{1,0:T(8,128)} %refs_0_.2), channel_id=1, source_target_pairs={{0,2},{1,3},{2,0},{3,1},{4,6},{5,7},{6,4},{7,5},{8,10},{9,11},{10,... | collective-permute-start | bytes 2359304 | tf_op jit(solution)/shard_map/ppermute | solution.py:167
  7.1 0.0 collective-permute-start.7
  7.1 0.7 %copy-done.4 = s32[256,2]{0,1:T(2,128)S(1)} copy-done((s32[256,2]{0,1:T(2,128)S(1)}, s32[256,2]{0,1:T(2,128)}, u32[]{:S(2)}) %copy-start.4) | copy-done | bytes 2072
  7.8 0.7 %copy-done.5 = f32[256]{0:T(256)S(1)} copy-done((f32[256]{0:T(256)S(1)}, f32[256]{0:T(256)}, u32[]{:S(2)}) %copy-start.5) | copy-done | bytes 1048
  8.5 0.2 occ_sums.1.occ_sum
  8.6 0.1 stack.99.bases
  8.8 0.7 %fusion.2 = s32[3072]{0:T(1024)S(1)} fusion(s32[3072]{0:T(1024)} %param.13, s32[]{:T(128)S(6)} %axis_index.22), kind=kLoop, calls=%fused_computation.6 | loop fusion | flops 46080 | bytes 24580 | tf_op jit(solution)/shard_map/add | solution.py:178
  9.5 0.5 collective-permute-start.4
  10.1 0.7 %copy-done.2 = s32[3072,2]{0,1:T(2,128)S(1)} copy-done((s32[3072,2]{0,1:T(2,128)S(1)}, s32[3072,2]{0,1:T(2,128)}, u32[]{:S(2)}) %copy-start.2) | copy-done | bytes 24600
  10.8 0.7 %copy-done.3 = f32[2048]{0:T(1024)S(1)} copy-done((f32[2048]{0:T(1024)S(1)}, f32[2048]{0:T(1024)}, u32[]{:S(2)}) %copy-start.3) | copy-done | bytes 8216
  11.5 7.0 %vir_sums.1.vir_sum = f32[1,3072]{1,0:T(1,128)S(1)} custom-call(f32[16,128]{1,0:T(8,128)S(1)} %bitcast.29, s32[2,3072]{1,0:T(2,128)S(1)} %bitcast.28), custom_call_target="tpu_custom_call" | custom-call | tf_op jit(solution)/shard_map/vir_sums/pallas_call | solution.py:47
  18.5 3.8 %collective-permute-done.refs_1_ = f32[384,512]{1,0:T(8,128)S(1)} collective-permute-done((f32[384,512]{1,0:T(8,128)}, f32[384,512]{1,0:T(8,128)S(1)}, u32[]{:S(2)}, u32[]{:S(2)}) %collective-permute-start) | collective-permute-done | bytes 786464 | tf_op jit(solution)/shard_map/ppermute | solution.py:161
  22.3 2.4 %collective-permute-done.2.refs_1_ = f32[256,768]{1,0:T(8,128)S(1)} collective-permute-done((f32[256,768]{1,0:T(8,128)}, f32[256,768]{1,0:T(8,128)S(1)}, u32[]{:S(2)}, u32[]{:S(2)}) %collective-permute-start.2) | collective-permute-done | bytes 786464 | tf_op jit(solution)/shard_map/ppermute | solution.py:167
  24.7 0.7 %collective-permute-start.10 = (f32[384,512]{1,0:T(8,128)}, f32[384,512]{1,0:T(8,128)S(1)}, u32[]{:S(2)}, u32[]{:S(2)}) collective-permute-start(f32[384,512]{1,0:T(8,128)} %refs_0_.3), channel_id=1, source_target_pairs={{8,16},{12,20},{16,8},{20,12},{9,17},{13,21},{17,9},{21,13},{10,18... | collective-permute-start | bytes 2359304 | tf_op jit(solution)/shard_map/ppermute | solution.py:161
  25.4 1.3 %collective-permute-start.9 = (f32[256,512]{1,0:T(8,128)S(1)}, f32[256,512]{1,0:T(8,128)S(1)}, u32[]{:S(2)}, u32[]{:S(2)}) collective-permute-start(f32[256,512]{1,0:T(8,128)S(1)} %slice.13), channel_id=1, source_target_pairs={{8,0},{12,4},{16,24},{20,28},{9,1},{13,5},{17,25},{21,29},{10,2},{... | collective-permute-start | bytes 1572872 | tf_op jit(solution)/shard_map/ppermute | solution.py:161
  26.7 15.3 %collective-permute-done.3.refs_2_ = f32[256,768]{1,0:T(8,128)S(1)} collective-permute-done((f32[256,768]{1,0:T(8,128)}, f32[256,768]{1,0:T(8,128)S(1)}, u32[]{:S(2)}, u32[]{:S(2)}) %collective-permute-start.3) | collective-permute-done | bytes 786464 | tf_op jit(solution)/shard_map/ppermute | solution.py:167
  42.0 0.5 collective-permute-start.8
  42.5 0.0 copy-start.1
  42.6 1.4 %collective-permute-start.5 = (f32[128,512]{1,0:T(8,128)S(1)}, f32[128,512]{1,0:T(8,128)S(1)}, u32[]{:S(2)}, u32[]{:S(2)}) collective-permute-start(f32[128,512]{1,0:T(8,128)S(1)} %slice.12), channel_id=1, source_target_pairs={{8,0},{12,4},{16,24},{20,28},{9,1},{13,5},{17,25},{21,29},{10,2},{... | collective-permute-start | bytes 786440 | tf_op jit(solution)/shard_map/ppermute | solution.py:161
  44.0 7.2 %ordered.1 = (bf16[256,3072]{1,0:T(8,128)(2,1)S(1)}, bf16[256,3072]{1,0:T(8,128)(2,1)S(1)}) custom-call(s32[3072]{0:T(1024)S(1)} %broadcast_multiply_fusion.row_of, s32[4]{0:T(128)S(1)} %xor_multiply_fusion.starts, s32[24]{0:T(128)S(1)} %stack.99.bases, f32[1,256]{1,0:T(1,128)S(1)} %occ_sums.1.occ_sum, f32[1,3072]{1,0:T(1,128)S(1)} %vir_sums.1.vir_sum, ...), custom_call_target="tpu_custom_call" | custom-call | tf_op jit(solution)/shard_map/ordered/pallas_call | solution.py:91
  51.2 2.9 %summed.4.refs_2_ = f32[256,512]{1,0:T(8,128)S(1)} custom-call(bf16[256,3072]{1,0:T(8,128)(2,1)S(1)} %get-tuple-element.31.high, bf16[256,3072]{1,0:T(8,128)(2,1)S(1)} %get-tuple-element.32.low, f32[384,512]{1,0:T(8,128)S(1)} %copy-done.1, f32[384,512]{1,0:T(8,128)S(1)} %collective-permute-done.refs_1_, f32[384,512]{1,0:T(8,128)} %collective-permute-done.7.refs_2_, ...), custom_call_target="tpu_custom_call" | custom-call | tf_op jit(solution)/shard_map/summed/pallas_call | solution.py:144
  54.2 0.1 slice_select_fusion.refs_0_
  54.3 0.1 collective-permute-start.12
  54.4 0.9 %summed.5.refs_3_ = f32[256,512]{1,0:T(8,128)S(1)} custom-call(bf16[256,3072]{1,0:T(8,128)(2,1)S(1)} %get-tuple-element.31.high, bf16[256,3072]{1,0:T(8,128)(2,1)S(1)} %get-tuple-element.32.low, f32[384,512]{1,0:T(8,128)S(1)} %collective-permute-done.6.refs_0_, f32[384,512]{1,0:T(8,128)S(1)} %collective-permute-done.8.refs_1_, f32[256,512]{1,0:T(8,128)S(1)} %summed.4.refs_2_), custom_call_target="tpu_custom_call" | custom-call | tf_op jit(solution)/shard_map/summed/pallas_call | solution.py:144
  55.3 2.0 %collective-permute-done.5 = f32[128,512]{1,0:T(8,128)S(1)} collective-permute-done((f32[128,512]{1,0:T(8,128)S(1)}, f32[128,512]{1,0:T(8,128)S(1)}, u32[]{:S(2)}, u32[]{:S(2)}) %collective-permute-start.5) | collective-permute-done | bytes 262176 | tf_op jit(solution)/shard_map/ppermute | solution.py:161
  57.3 0.1 collective-permute-start.11
  57.4 0.7 %summed.6.refs_1_ = f32[256,512]{1,0:T(8,128)S(1)} custom-call(bf16[256,3072]{1,0:T(8,128)(2,1)S(1)} %get-tuple-element.31.high, bf16[256,3072]{1,0:T(8,128)(2,1)S(1)} %get-tuple-element.32.low, f32[256,512]{1,0:T(8,128)S(1)} %slice_select_fusion.refs_0_, f32[256,512]{1,0:T(8,128)S(1)} %collective-permute-done.12.refs_1_, ...), custom_call_target="tpu_custom_call" | custom-call | tf_op jit(solution)/shard_map/summed/pallas_call | solution.py:144
  58.1 0.8 %collective-permute-done.11.refs_0_ = f32[128,512]{1,0:T(8,128)S(1)} collective-permute-done((f32[128,512]{1,0:T(8,128)S(1)}, f32[128,512]{1,0:T(8,128)S(1)}, u32[]{:S(2)}, u32[]{:S(2)}) %collective-permute-start.11) | collective-permute-done | bytes 262176 | tf_op jit(solution)/shard_map/ppermute | solution.py:164
  58.9 1.0 %summed.7 = f32[256,512]{1,0:T(8,128)} custom-call(bf16[256,3072]{1,0:T(8,128)(2,1)S(1)} %get-tuple-element.31.high, bf16[256,3072]{1,0:T(8,128)(2,1)S(1)} %get-tuple-element.32.low, f32[128,512]{1,0:T(8,128)S(1)} %collective-permute-done.11.refs_0_, f32[256,512]{1,0:T(8,128)S(1)} %summed.6.refs_1_), custom_call_target="tpu_custom_call" | custom-call | tf_op jit(solution)/shard_map/summed/pallas_call | solution.py:144
  (21 shorter events, 0.1 us)
Async XLA Ops:
  0.0 44.0 %copy-start = (f32[256,768]{1,0:T(8,128)S(1)}, f32[256,768]{1,0:T(8,128)}, u32[]{:S(2)}) copy-start(f32[256,768]{1,0:T(8,128)} %refs_0_.2) | copy-start | bytes 2359300
  0.0 9.5 %collective-permute-start.1 = (f32[384,512]{1,0:T(8,128)}, f32[384,512]{1,0:T(8,128)}, u32[]{:S(2)}, u32[]{:S(2)}) collective-permute-start(f32[384,512]{1,0:T(8,128)} %refs_0_.3), channel_id=1, source_target_pairs={{0,4},{4,0},{8,12},{12,8},{16,20},{20,16},{24,28},{28,24},{1,5},{5... | collective-permute-start | bytes 2359304 | tf_op jit(solution)/shard_map/ppermute | solution.py:164
  0.5 21.9 %collective-permute-start = (f32[384,512]{1,0:T(8,128)}, f32[384,512]{1,0:T(8,128)S(1)}, u32[]{:S(2)}, u32[]{:S(2)}) collective-permute-start(f32[384,512]{1,0:T(8,128)} %refs_0_.3), channel_id=1, source_target_pairs={{0,16},{4,20},{24,8},{28,12},{8,0},{12,4},{16,24},{20,28},{1,17},{... | collective-permute-start | bytes 2359304 | tf_op jit(solution)/shard_map/ppermute | solution.py:161
  4.1 20.6 %collective-permute-start.2 = (f32[256,768]{1,0:T(8,128)}, f32[256,768]{1,0:T(8,128)S(1)}, u32[]{:S(2)}, u32[]{:S(2)}) collective-permute-start(f32[256,768]{1,0:T(8,128)} %refs_0_.2), channel_id=1, source_target_pairs={{0,1},{1,0},{2,3},{3,2},{4,5},{5,4},{6,7},{7,6},{8,9},{9,8},{10,11... | collective-permute-start | bytes 2359304 | tf_op jit(solution)/shard_map/ppermute | solution.py:167
  5.6 36.4 %collective-permute-start.3 = (f32[256,768]{1,0:T(8,128)}, f32[256,768]{1,0:T(8,128)S(1)}, u32[]{:S(2)}, u32[]{:S(2)}) collective-permute-start(f32[256,768]{1,0:T(8,128)} %refs_0_.2), channel_id=1, source_target_pairs={{0,2},{1,3},{2,0},{3,1},{4,6},{5,7},{6,4},{7,5},{8,10},{9,11},{10,... | collective-permute-start | bytes 2359304 | tf_op jit(solution)/shard_map/ppermute | solution.py:167
  7.1 34.9 %collective-permute-start.7 = (f32[384,512]{1,0:T(8,128)}, f32[384,512]{1,0:T(8,128)}, u32[]{:S(2)}, u32[]{:S(2)}) collective-permute-start(f32[384,512]{1,0:T(8,128)} %refs_0_.3), channel_id=1, source_target_pairs={{8,24},{12,28},{16,0},{20,4},{0,8},{4,12},{24,16},{28,20},{9,25},{... | collective-permute-start | bytes 2359304 | tf_op jit(solution)/shard_map/ppermute | solution.py:161
  7.1 0.7 %copy-start.4 = (s32[256,2]{0,1:T(2,128)S(1)}, s32[256,2]{0,1:T(2,128)}, u32[]{:S(2)}) copy-start(s32[256,2]{0,1:T(2,128)} %param.11) | copy-start | bytes 6148
  7.8 0.7 %copy-start.5 = (f32[256]{0:T(256)S(1)}, f32[256]{0:T(256)}, u32[]{:S(2)}) copy-start(f32[256]{0:T(256)} %param.9) | copy-start | bytes 3076
  9.5 33.0 %collective-permute-start.4 = (f32[256,768]{1,0:T(8,128)}, f32[256,768]{1,0:T(8,128)S(1)}, u32[]{:S(2)}, u32[]{:S(2)}) collective-permute-start(f32[256,768]{1,0:T(8,128)} %refs_0_.2), channel_id=1, source_target_pairs={{0,3},{1,2},{2,1},{3,0},{4,7},{5,6},{6,5},{7,4},{8,11},{9,10},{10,... | collective-permute-start | bytes 2359304 | tf_op jit(solution)/shard_map/ppermute | solution.py:167
  10.1 0.7 %copy-start.2 = (s32[3072,2]{0,1:T(2,128)S(1)}, s32[3072,2]{0,1:T(2,128)}, u32[]{:S(2)}) copy-start(s32[3072,2]{0,1:T(2,128)} %param.12) | copy-start | bytes 73732
  10.8 0.7 %copy-start.3 = (f32[2048]{0:T(1024)S(1)}, f32[2048]{0:T(1024)}, u32[]{:S(2)}) copy-start(f32[2048]{0:T(1024)} %param.10) | copy-start | bytes 24580
  24.7 29.5 %collective-permute-start.10 = (f32[384,512]{1,0:T(8,128)}, f32[384,512]{1,0:T(8,128)S(1)}, u32[]{:S(2)}, u32[]{:S(2)}) collective-permute-start(f32[384,512]{1,0:T(8,128)} %refs_0_.3), channel_id=1, source_target_pairs={{8,16},{12,20},{16,8},{20,12},{9,17},{13,21},{17,9},{21,13},{10,18... | collective-permute-start | bytes 2359304 | tf_op jit(solution)/shard_map/ppermute | solution.py:161
  25.4 28.7 %collective-permute-start.9 = (f32[256,512]{1,0:T(8,128)S(1)}, f32[256,512]{1,0:T(8,128)S(1)}, u32[]{:S(2)}, u32[]{:S(2)}) collective-permute-start(f32[256,512]{1,0:T(8,128)S(1)} %slice.13), channel_id=1, source_target_pairs={{8,0},{12,4},{16,24},{20,28},{9,1},{13,5},{17,25},{21,29},{10,2},{... | collective-permute-start | bytes 1572872 | tf_op jit(solution)/shard_map/ppermute | solution.py:161
  42.0 12.4 %collective-permute-start.6 = (f32[384,512]{1,0:T(8,128)S(1)}, f32[384,512]{1,0:T(8,128)S(1)}, u32[]{:S(2)}, u32[]{:S(2)}) collective-permute-start(f32[384,512]{1,0:T(8,128)S(1)} %collective-permute-done.refs_1_), channel_id=1, source_target_pairs={{0,4},{4,0},{8,12},{12,8},{16,20},{20,16},{24,28},{28,24},{1,5},{5... | collective-permute-start | bytes 2359304 | tf_op jit(solution)/shard_map/ppermute | solution.py:164
  42.0 12.4 %collective-permute-start.8 = (f32[384,512]{1,0:T(8,128)}, f32[384,512]{1,0:T(8,128)S(1)}, u32[]{:S(2)}, u32[]{:S(2)}) collective-permute-start(f32[384,512]{1,0:T(8,128)} %collective-permute-done.7.refs_2_), channel_id=1, source_target_pairs={{0,4},{4,0},{8,12},{12,8},{16,20},{20,16},{24,28},{28,24},{1,5},{5... | collective-permute-start | bytes 2359304 | tf_op jit(solution)/shard_map/ppermute | solution.py:164
  42.5 8.7 %copy-start.1 = (f32[384,512]{1,0:T(8,128)S(1)}, f32[384,512]{1,0:T(8,128)}, u32[]{:S(2)}) copy-start(f32[384,512]{1,0:T(8,128)} %refs_0_.3) | copy-start | bytes 2359300
  42.6 14.7 %collective-permute-start.5 = (f32[128,512]{1,0:T(8,128)S(1)}, f32[128,512]{1,0:T(8,128)S(1)}, u32[]{:S(2)}, u32[]{:S(2)}) collective-permute-start(f32[128,512]{1,0:T(8,128)S(1)} %slice.12), channel_id=1, source_target_pairs={{8,0},{12,4},{16,24},{20,28},{9,1},{13,5},{17,25},{21,29},{10,2},{... | collective-permute-start | bytes 786440 | tf_op jit(solution)/shard_map/ppermute | solution.py:161
  54.3 3.1 %collective-permute-start.12 = (f32[256,512]{1,0:T(8,128)S(1)}, f32[256,512]{1,0:T(8,128)S(1)}, u32[]{:S(2)}, u32[]{:S(2)}) collective-permute-start(f32[256,512]{1,0:T(8,128)S(1)} %slice_select_fusion.refs_0_), channel_id=1, source_target_pairs={{0,4},{4,0},{8,12},{12,8},{16,20},{20,16},{24,28},{28,24},{1,5},{5... | collective-permute-start | bytes 1572872 | tf_op jit(solution)/shard_map/ppermute | solution.py:164
  57.3 1.6 %collective-permute-start.11 = (f32[128,512]{1,0:T(8,128)S(1)}, f32[128,512]{1,0:T(8,128)S(1)}, u32[]{:S(2)}, u32[]{:S(2)}) collective-permute-start(f32[128,512]{1,0:T(8,128)S(1)} %slice_select_fusion.1.refs_2_), channel_id=1, source_target_pairs={{0,4},{4,0},{8,12},{12,8},{16,20},{20,16},{24,28},{28,24},{1,5},{5... | collective-permute-start | bytes 786440 | tf_op jit(solution)/shard_map/ppermute | solution.py:164

commit v7 on v6

--- a/solution.py
+++ b/solution.py
@@ -172,7 +172,6 @@
     at_end = (chip == 0) | (chip == 3)
     cut = 256
 
-    crossed_own, vir_energy = lax.optimization_barrier((other_core(integrals), vir_energy))
     vir_sum = energy_sums(vir_energy, vir_pairs, "vir_sums")
     starts = (col ^ jnp.arange(4, dtype=jnp.int32)) * width
     place_of = ((pair_order // width) ^ col) * width + pair_order % width
@@ -187,15 +186,16 @@
         (one, vir_sum, occ_sum, starts, bases, place_of, integrals)
     )
     far_a = between_chips(one[:cut], [(1, 0), (2, 3)])
+    crossed = other_core(jnp.concatenate([mine, one]))
     raw_x, mine = lax.optimization_barrier((raw_x, mine))
     middle = between_chips(mine, [(1, 2), (2, 1)])
     far_b = between_chips(one[cut:], [(1, 0), (2, 3)])
     high, low = ordered(place_of, starts, bases, occ_sum, vir_sum, raw_amps, raw_x, raw_y, raw_d)
-    total = summed(high, low, 0, [integrals, one, two, crossed_own])
+    total = summed(high, low, 0, [integrals, one, two])
     far_a, middle, total = lax.optimization_barrier((far_a, middle, total))
     third_a = jnp.where(at_end, far_a, middle[:cut])
     crossed_a = other_core(third_a)
-    total = summed(high, low, 4 * depth, [other_core(one), other_core(two)], total)
+    total = summed(high, low, 3 * depth, [crossed, other_core(two)], total)
     far_b, total = lax.optimization_barrier((far_b, total))
     third_b = jnp.where(at_end, far_b, middle[cut:])
     total = summed(high, low, 6 * depth, [third_a, crossed_a, third_b], total)

time: 60.3 us -> 59.6 us (0.988)
  waiting for transfers between devices: 24.2 us -> 22.3 us
  Pallas kernels: 20 us -> 18.5 us
  starting transfers between devices: 11.7 us -> 13.1 us
  other arithmetic: 0.85 us -> 2.11 us
    ppermute x3, waiting for transfers between devices: 17.6 us -> 4.66 us  [across(): return lax.ppermute(block, 'col', [(i, i ^ mask) for i in range(4)])]
    ppermute x5, waiting for transfers between devices: 5.76 us -> 16.9 us  [between_chips(): lax.ppermute(block, 'row', [(2 * a + c, 2 * b + c) for a, b in pairs for...]
    ppermute x3, starting transfers between devices: 3.55 us -> 5.52 us  [across(): return lax.ppermute(block, 'col', [(i, i ^ mask) for i in range(4)])]
    pallas_call x4, Pallas kernels: 5.57 us -> 4.06 us  [summed(): pl.pallas_call(functools.partial(product_kernel, first, sizes, total is n...]
    concatenate x0 -> x1, other arithmetic: none -> 1.25 us  [four_chips_each(): crossed = other_core(jnp.concatenate([mine, one]))]
    ppermute x5 -> x4, starting transfers between devices: 1.12 us -> 0.25 us  [other_core(): return lax.ppermute(block, 'row', [(i, i ^ 1) for i in range(8)])]
  transfers between devices with their start and end apart: 13 -> 12, of which waited for: 5 -> 5; matrix products, arithmetic and copies ran while one was open for 2% -> 4% of each run, Pallas kernels for 32% -> 29%
where the time goes in v7:
time: 59.6 us; the launch traced here: 59.2 us
  waiting for transfers between devices  22.3 us (37%)
  Pallas kernels  18.5 us (31%)
  starting transfers between devices  13.1 us (22%)
  local copies, waits for them, and re-layouts  2.96 us (5%)
  other arithmetic  2.11 us (4%)
    ppermute x5, waiting for transfers between devices, between_chips(): lax.ppermute(block, 'row', [(2 * a + c, 2 * b + c) for a, b in pairs for...  16.9 us
    ppermute x5, starting transfers between devices, between_chips(): lax.ppermute(block, 'row', [(2 * a + c, 2 * b + c) for a, b in pairs for...  7.31 us
    pallas_call x1, Pallas kernels, ordered(): pl.pallas_call(order_kernel, name='ordered', in_specs=[SMEM, SMEM, SMEM]...  7.22 us
    pallas_call x2, Pallas kernels, energy_sums(): pl.pallas_call(look_up, name=name, out_shape=jax.ShapeDtypeStruct((1, pai...  7.19 us
    ppermute x3, starting transfers between devices, across(): return lax.ppermute(block, 'col', [(i, i ^ mask) for i in range(4)])  5.52 us
    ppermute x3, waiting for transfers between devices, across(): return lax.ppermute(block, 'col', [(i, i ^ mask) for i in range(4)])  4.66 us
    pallas_call x4, Pallas kernels, summed(): pl.pallas_call(functools.partial(product_kernel, first, sizes, total is n...  4.06 us
    unnamed x12, local copies, waits for them, and re-layouts  2.8 us
  transfers between devices with their start and end apart: 12, of which 5 were waited for; matrix products, arithmetic and copies ran while one was open for 4% of the time, Pallas kernels for 29%

profile of v7, /device:TPU:0, one launch (start us, length us, event | category | flops | bytes accessed | tf_op | source)
XLA Modules:
  0.0 59.2 jit_solution(7132387046374110023)
XLA Ops:
  0.0 4.0 %collective-permute-start = (f32[384,512]{1,0:T(8,128)}, f32[384,512]{1,0:T(8,128)S(1)}, u32[]{:S(2)}, u32[]{:S(2)}) collective-permute-start(f32[384,512]{1,0:T(8,128)} %refs_0_.3), channel_id=1, source_target_pairs={{0,16},{4,20},{24,8},{28,12},{8,0},{12,4},{16,24},{20,28},{1,17},{... | collective-permute-start | bytes 2359304 | tf_op jit(solution)/shard_map/ppermute | solution.py:161
  4.0 1.5 %collective-permute-start.1 = (f32[256,768]{1,0:T(8,128)}, f32[256,768]{1,0:T(8,128)S(1)}, u32[]{:S(2)}, u32[]{:S(2)}) collective-permute-start(f32[256,768]{1,0:T(8,128)} %refs_0_.2), channel_id=1, source_target_pairs={{0,1},{1,0},{2,3},{3,2},{4,5},{5,4},{6,7},{7,6},{8,9},{9,8},{10,11... | collective-permute-start | bytes 2359304 | tf_op jit(solution)/shard_map/ppermute | solution.py:167
  5.5 1.5 %collective-permute-start.2 = (f32[256,768]{1,0:T(8,128)}, f32[256,768]{1,0:T(8,128)S(1)}, u32[]{:S(2)}, u32[]{:S(2)}) collective-permute-start(f32[256,768]{1,0:T(8,128)} %refs_0_.2), channel_id=1, source_target_pairs={{0,2},{1,3},{2,0},{3,1},{4,6},{5,7},{6,4},{7,5},{8,10},{9,11},{10,... | collective-permute-start | bytes 2359304 | tf_op jit(solution)/shard_map/ppermute | solution.py:167
  7.1 0.7 %fusion.2 = s32[3072]{0:T(1024)S(1)} fusion(s32[3072]{0:T(1024)} %param.13, s32[]{:T(128)S(6)} %axis_index.22), kind=kLoop, calls=%fused_computation.7 | loop fusion | flops 46080 | bytes 24580 | tf_op jit(solution)/shard_map/add | solution.py:177
  7.8 0.0 copy-start.2
  7.8 0.7 %copy-done.2 = s32[3072,2]{0,1:T(2,128)S(1)} copy-done((s32[3072,2]{0,1:T(2,128)S(1)}, s32[3072,2]{0,1:T(2,128)}, u32[]{:S(2)}) %copy-start.2) | copy-done | bytes 24600
  8.6 0.7 %copy-done.3 = f32[2048]{0:T(1024)S(1)} copy-done((f32[2048]{0:T(1024)S(1)}, f32[2048]{0:T(1024)}, u32[]{:S(2)}) %copy-start.3) | copy-done | bytes 8216
  9.3 7.0 %vir_sums.1.vir_sum = f32[1,3072]{1,0:T(1,128)S(1)} custom-call(f32[16,128]{1,0:T(8,128)S(1)} %bitcast.29, s32[2,3072]{1,0:T(2,128)S(1)} %bitcast.28), custom_call_target="tpu_custom_call" | custom-call | tf_op jit(solution)/shard_map/vir_sums/pallas_call | solution.py:47
  16.3 0.7 %copy-done.4 = s32[256,2]{0,1:T(2,128)S(1)} copy-done((s32[256,2]{0,1:T(2,128)S(1)}, s32[256,2]{0,1:T(2,128)}, u32[]{:S(2)}) %copy-start.4) | copy-done | bytes 2072
  17.0 0.7 %copy-done.5 = f32[256]{0:T(256)S(1)} copy-done((f32[256]{0:T(256)S(1)}, f32[256]{0:T(256)}, u32[]{:S(2)}) %copy-start.5) | copy-done | bytes 1048
  17.7 0.2 occ_sums.1.occ_sum
  17.8 0.1 stack.99.bases
  18.0 0.0 copy-start.1
  18.0 4.4 %collective-permute-done.refs_1_ = f32[384,512]{1,0:T(8,128)S(1)} collective-permute-done((f32[384,512]{1,0:T(8,128)}, f32[384,512]{1,0:T(8,128)S(1)}, u32[]{:S(2)}, u32[]{:S(2)}) %collective-permute-start) | collective-permute-done | bytes 786464 | tf_op jit(solution)/shard_map/ppermute | solution.py:161
  22.3 1.3 %pad_maximum_fusion = f32[768,512]{1,0:T(8,128)S(1)} fusion(f32[384,512]{1,0:T(8,128)S(1)} %collective-permute-done.refs_1_, f32[384,512]{1,0:T(8,128)} %refs_0_.3), kind=kLoop, calls=%fused_computation | loop fusion | flops 393216 | bytes 3145728 | tf_op jit(solution)/shard_map/concatenate | solution.py:189
  23.6 0.1 collective-permute-start.5
  23.7 2.5 %collective-permute-start.3 = (f32[256,768]{1,0:T(8,128)S(1)}, f32[256,768]{1,0:T(8,128)S(1)}, u32[]{:S(2)}, u32[]{:S(2)}) collective-permute-start(f32[256,768]{1,0:T(8,128)S(1)} %copy-done.1), channel_id=1, source_target_pairs={{0,3},{1,2},{2,1},{3,0},{4,7},{5,6},{6,5},{7,4},{8,11},{9,10},{10,... | collective-permute-start | bytes 2359304 | tf_op jit(solution)/shard_map/ppermute | solution.py:167
  26.2 0.7 %collective-permute-start.9 = (f32[384,512]{1,0:T(8,128)S(1)}, f32[384,512]{1,0:T(8,128)S(1)}, u32[]{:S(2)}, u32[]{:S(2)}) collective-permute-start(f32[384,512]{1,0:T(8,128)S(1)} %copy-done), channel_id=1, source_target_pairs={{8,16},{12,20},{16,8},{20,12},{9,17},{13,21},{17,9},{21,13},{10,18... | collective-permute-start | bytes 2359304 | tf_op jit(solution)/shard_map/ppermute | solution.py:161
  27.0 1.3 %collective-permute-start.8 = (f32[256,512]{1,0:T(8,128)S(1)}, f32[256,512]{1,0:T(8,128)S(1)}, u32[]{:S(2)}, u32[]{:S(2)}) collective-permute-start(f32[256,512]{1,0:T(8,128)S(1)} %slice.13), channel_id=1, source_target_pairs={{8,0},{12,4},{16,24},{20,28},{9,1},{13,5},{17,25},{21,29},{10,2},{... | collective-permute-start | bytes 1572872 | tf_op jit(solution)/shard_map/ppermute | solution.py:161
  28.3 11.6 %collective-permute-done.6.refs_2_ = f32[384,512]{1,0:T(8,128)S(1)} collective-permute-done((f32[384,512]{1,0:T(8,128)}, f32[384,512]{1,0:T(8,128)S(1)}, u32[]{:S(2)}, u32[]{:S(2)}) %collective-permute-start.6) | collective-permute-done | bytes 786464 | tf_op jit(solution)/shard_map/ppermute | solution.py:161
  39.9 4.7 %collective-permute-done.3.refs_3_ = f32[256,768]{1,0:T(8,128)S(1)} collective-permute-done((f32[256,768]{1,0:T(8,128)S(1)}, f32[256,768]{1,0:T(8,128)S(1)}, u32[]{:S(2)}, u32[]{:S(2)}) %collective-permute-start.3) | collective-permute-done | bytes 786464 | tf_op jit(solution)/shard_map/ppermute | solution.py:167
  44.5 1.3 %collective-permute-start.4 = (f32[128,512]{1,0:T(8,128)S(1)}, f32[128,512]{1,0:T(8,128)S(1)}, u32[]{:S(2)}, u32[]{:S(2)}) collective-permute-start(f32[128,512]{1,0:T(8,128)S(1)} %slice.12), channel_id=1, source_target_pairs={{8,0},{12,4},{16,24},{20,28},{9,1},{13,5},{17,25},{21,29},{10,2},{... | collective-permute-start | bytes 786440 | tf_op jit(solution)/shard_map/ppermute | solution.py:161
  45.8 7.2 %ordered.1 = (bf16[256,3072]{1,0:T(8,128)(2,1)S(1)}, bf16[256,3072]{1,0:T(8,128)(2,1)S(1)}) custom-call(s32[3072]{0:T(1024)S(1)} %broadcast_multiply_fusion.row_of, s32[4]{0:T(128)S(1)} %xor_multiply_fusion.starts, s32[24]{0:T(128)S(1)} %stack.99.bases, f32[1,256]{1,0:T(1,128)S(1)} %occ_sums.1.occ_sum, f32[1,3072]{1,0:T(1,128)S(1)} %vir_sums.1.vir_sum, ...), custom_call_target="tpu_custom_call" | custom-call | tf_op jit(solution)/shard_map/ordered/pallas_call | solution.py:91
  53.0 1.2 %summed.4.refs_2_ = f32[256,512]{1,0:T(8,128)S(1)} custom-call(bf16[256,3072]{1,0:T(8,128)(2,1)S(1)} %get-tuple-element.28.high, bf16[256,3072]{1,0:T(8,128)(2,1)S(1)} %get-tuple-element.29.low, f32[384,512]{1,0:T(8,128)S(1)} %copy-done, f32[384,512]{1,0:T(8,128)S(1)} %collective-permute-done.refs_1_, f32[384,512]{1,0:T(8,128)S(1)} %collective-permute-done.6.refs_2_), custom_call_target="tpu_custom_call" | custom-call | tf_op jit(solution)/shard_map/summed/pallas_call | solution.py:144
  54.3 0.1 slice_select_fusion.refs_0_
  54.4 0.1 collective-permute-start.11
  54.5 1.1 %summed.5.refs_3_ = f32[256,512]{1,0:T(8,128)S(1)} custom-call(bf16[256,3072]{1,0:T(8,128)(2,1)S(1)} %get-tuple-element.28.high, bf16[256,3072]{1,0:T(8,128)(2,1)S(1)} %get-tuple-element.29.low, f32[768,512]{1,0:T(8,128)S(1)} %collective-permute-done.5.refs_0_, f32[384,512]{1,0:T(8,128)S(1)} %collective-permute-done.7.refs_1_, f32[256,512]{1,0:T(8,128)S(1)} %summed.4.refs_2_), custom_call_target="tpu_custom_call" | custom-call | tf_op jit(solution)/shard_map/summed/pallas_call | solution.py:144
  55.6 1.0 %collective-permute-done.4 = f32[128,512]{1,0:T(8,128)S(1)} collective-permute-done((f32[128,512]{1,0:T(8,128)S(1)}, f32[128,512]{1,0:T(8,128)S(1)}, u32[]{:S(2)}, u32[]{:S(2)}) %collective-permute-start.4) | collective-permute-done | bytes 262176 | tf_op jit(solution)/shard_map/ppermute | solution.py:161
  56.6 0.1 collective-permute-start.10
  56.7 0.7 %summed.6.refs_1_ = f32[256,512]{1,0:T(8,128)S(1)} custom-call(bf16[256,3072]{1,0:T(8,128)(2,1)S(1)} %get-tuple-element.28.high, bf16[256,3072]{1,0:T(8,128)(2,1)S(1)} %get-tuple-element.29.low, f32[256,512]{1,0:T(8,128)S(1)} %slice_select_fusion.refs_0_, f32[256,512]{1,0:T(8,128)S(1)} %collective-permute-done.11.refs_1_, ...), custom_call_target="tpu_custom_call" | custom-call | tf_op jit(solution)/shard_map/summed/pallas_call | solution.py:144
  57.4 0.8 %collective-permute-done.10.refs_0_ = f32[128,512]{1,0:T(8,128)S(1)} collective-permute-done((f32[128,512]{1,0:T(8,128)S(1)}, f32[128,512]{1,0:T(8,128)S(1)}, u32[]{:S(2)}, u32[]{:S(2)}) %collective-permute-start.10) | collective-permute-done | bytes 262176 | tf_op jit(solution)/shard_map/ppermute | solution.py:164
  58.2 1.0 %summed.7 = f32[256,512]{1,0:T(8,128)} custom-call(bf16[256,3072]{1,0:T(8,128)(2,1)S(1)} %get-tuple-element.28.high, bf16[256,3072]{1,0:T(8,128)(2,1)S(1)} %get-tuple-element.29.low, f32[128,512]{1,0:T(8,128)S(1)} %collective-permute-done.10.refs_0_, f32[256,512]{1,0:T(8,128)S(1)} %summed.6.refs_1_), custom_call_target="tpu_custom_call" | custom-call | tf_op jit(solution)/shard_map/summed/pallas_call | solution.py:144
  (20 shorter events, 0.1 us)
Async XLA Ops:
  0.0 22.3 %collective-permute-start = (f32[384,512]{1,0:T(8,128)}, f32[384,512]{1,0:T(8,128)S(1)}, u32[]{:S(2)}, u32[]{:S(2)}) collective-permute-start(f32[384,512]{1,0:T(8,128)} %refs_0_.3), channel_id=1, source_target_pairs={{0,16},{4,20},{24,8},{28,12},{8,0},{12,4},{16,24},{20,28},{1,17},{... | collective-permute-start | bytes 2359304 | tf_op jit(solution)/shard_map/ppermute | solution.py:161
  4.0 22.2 %collective-permute-start.1 = (f32[256,768]{1,0:T(8,128)}, f32[256,768]{1,0:T(8,128)S(1)}, u32[]{:S(2)}, u32[]{:S(2)}) collective-permute-start(f32[256,768]{1,0:T(8,128)} %refs_0_.2), channel_id=1, source_target_pairs={{0,1},{1,0},{2,3},{3,2},{4,5},{5,4},{6,7},{7,6},{8,9},{9,8},{10,11... | collective-permute-start | bytes 2359304 | tf_op jit(solution)/shard_map/ppermute | solution.py:167
  5.5 21.4 %collective-permute-start.2 = (f32[256,768]{1,0:T(8,128)}, f32[256,768]{1,0:T(8,128)S(1)}, u32[]{:S(2)}, u32[]{:S(2)}) collective-permute-start(f32[256,768]{1,0:T(8,128)} %refs_0_.2), channel_id=1, source_target_pairs={{0,2},{1,3},{2,0},{3,1},{4,6},{5,7},{6,4},{7,5},{8,10},{9,11},{10,... | collective-permute-start | bytes 2359304 | tf_op jit(solution)/shard_map/ppermute | solution.py:167
  7.0 32.8 %collective-permute-start.6 = (f32[384,512]{1,0:T(8,128)}, f32[384,512]{1,0:T(8,128)S(1)}, u32[]{:S(2)}, u32[]{:S(2)}) collective-permute-start(f32[384,512]{1,0:T(8,128)} %refs_0_.3), channel_id=1, source_target_pairs={{8,24},{12,28},{16,0},{20,4},{0,8},{4,12},{24,16},{28,20},{9,25},{... | collective-permute-start | bytes 2359304 | tf_op jit(solution)/shard_map/ppermute | solution.py:161
  7.8 0.7 %copy-start.2 = (s32[3072,2]{0,1:T(2,128)S(1)}, s32[3072,2]{0,1:T(2,128)}, u32[]{:S(2)}) copy-start(s32[3072,2]{0,1:T(2,128)} %param.12) | copy-start | bytes 73732
  8.6 0.7 %copy-start.3 = (f32[2048]{0:T(1024)S(1)}, f32[2048]{0:T(1024)}, u32[]{:S(2)}) copy-start(f32[2048]{0:T(1024)} %param.10) | copy-start | bytes 24580
  16.3 0.7 %copy-start.4 = (s32[256,2]{0,1:T(2,128)S(1)}, s32[256,2]{0,1:T(2,128)}, u32[]{:S(2)}) copy-start(s32[256,2]{0,1:T(2,128)} %param.11) | copy-start | bytes 6148
  17.0 0.7 %copy-start.5 = (f32[256]{0:T(256)S(1)}, f32[256]{0:T(256)}, u32[]{:S(2)}) copy-start(f32[256]{0:T(256)} %param.9) | copy-start | bytes 3076
  18.0 5.7 %copy-start.1 = (f32[256,768]{1,0:T(8,128)S(1)}, f32[256,768]{1,0:T(8,128)}, u32[]{:S(2)}) copy-start(f32[256,768]{1,0:T(8,128)} %refs_0_.2) | copy-start | bytes 2359300
  18.0 8.2 %copy-start = (f32[384,512]{1,0:T(8,128)S(1)}, f32[384,512]{1,0:T(8,128)}, u32[]{:S(2)}) copy-start(f32[384,512]{1,0:T(8,128)} %refs_0_.3) | copy-start | bytes 2359300
  23.6 30.8 %collective-permute-start.5 = (f32[768,512]{1,0:T(8,128)S(1)}, f32[768,512]{1,0:T(8,128)S(1)}, u32[]{:S(2)}, u32[]{:S(2)}) collective-permute-start(f32[768,512]{1,0:T(8,128)S(1)} %pad_maximum_fusion), channel_id=1, source_target_pairs={{0,4},{4,0},{8,12},{12,8},{16,20},{20,16},{24,28},{28,24},{1,5},{5... | collective-permute-start | bytes 4718600 | tf_op jit(solution)/shard_map/ppermute | solution.py:164
  23.7 20.8 %collective-permute-start.3 = (f32[256,768]{1,0:T(8,128)S(1)}, f32[256,768]{1,0:T(8,128)S(1)}, u32[]{:S(2)}, u32[]{:S(2)}) collective-permute-start(f32[256,768]{1,0:T(8,128)S(1)} %copy-done.1), channel_id=1, source_target_pairs={{0,3},{1,2},{2,1},{3,0},{4,7},{5,6},{6,5},{7,4},{8,11},{9,10},{10,... | collective-permute-start | bytes 2359304 | tf_op jit(solution)/shard_map/ppermute | solution.py:167
  26.2 28.0 %collective-permute-start.9 = (f32[384,512]{1,0:T(8,128)S(1)}, f32[384,512]{1,0:T(8,128)S(1)}, u32[]{:S(2)}, u32[]{:S(2)}) collective-permute-start(f32[384,512]{1,0:T(8,128)S(1)} %copy-done), channel_id=1, source_target_pairs={{8,16},{12,20},{16,8},{20,12},{9,17},{13,21},{17,9},{21,13},{10,18... | collective-permute-start | bytes 2359304 | tf_op jit(solution)/shard_map/ppermute | solution.py:161
  27.0 27.3 %collective-permute-start.8 = (f32[256,512]{1,0:T(8,128)S(1)}, f32[256,512]{1,0:T(8,128)S(1)}, u32[]{:S(2)}, u32[]{:S(2)}) collective-permute-start(f32[256,512]{1,0:T(8,128)S(1)} %slice.13), channel_id=1, source_target_pairs={{8,0},{12,4},{16,24},{20,28},{9,1},{13,5},{17,25},{21,29},{10,2},{... | collective-permute-start | bytes 1572872 | tf_op jit(solution)/shard_map/ppermute | solution.py:161
  39.8 14.6 %collective-permute-start.7 = (f32[384,512]{1,0:T(8,128)S(1)}, f32[384,512]{1,0:T(8,128)S(1)}, u32[]{:S(2)}, u32[]{:S(2)}) collective-permute-start(f32[384,512]{1,0:T(8,128)S(1)} %collective-permute-done.6.refs_2_), channel_id=1, source_target_pairs={{0,4},{4,0},{8,12},{12,8},{16,20},{20,16},{24,28},{28,24},{1,5},{5... | collective-permute-start | bytes 2359304 | tf_op jit(solution)/shard_map/ppermute | solution.py:164
  44.5 12.0 %collective-permute-start.4 = (f32[128,512]{1,0:T(8,128)S(1)}, f32[128,512]{1,0:T(8,128)S(1)}, u32[]{:S(2)}, u32[]{:S(2)}) collective-permute-start(f32[128,512]{1,0:T(8,128)S(1)} %slice.12), channel_id=1, source_target_pairs={{8,0},{12,4},{16,24},{20,28},{9,1},{13,5},{17,25},{21,29},{10,2},{... | collective-permute-start | bytes 786440 | tf_op jit(solution)/shard_map/ppermute | solution.py:161
  54.4 2.4 %collective-permute-start.11 = (f32[256,512]{1,0:T(8,128)S(1)}, f32[256,512]{1,0:T(8,128)S(1)}, u32[]{:S(2)}, u32[]{:S(2)}) collective-permute-start(f32[256,512]{1,0:T(8,128)S(1)} %slice_select_fusion.refs_0_), channel_id=1, source_target_pairs={{0,4},{4,0},{8,12},{12,8},{16,20},{20,16},{24,28},{28,24},{1,5},{5... | collective-permute-start | bytes 1572872 | tf_op jit(solution)/shard_map/ppermute | solution.py:164
  56.6 1.6 %collective-permute-start.10 = (f32[128,512]{1,0:T(8,128)S(1)}, f32[128,512]{1,0:T(8,128)S(1)}, u32[]{:S(2)}, u32[]{:S(2)}) collective-permute-start(f32[128,512]{1,0:T(8,128)S(1)} %slice_select_fusion.1.refs_2_), channel_id=1, source_target_pairs={{0,4},{4,0},{8,12},{12,8},{16,20},{20,16},{24,28},{28,24},{1,5},{5... | collective-permute-start | bytes 786440 | tf_op jit(solution)/shard_map/ppermute | solution.py:164

commit v8 on v7

--- a/solution.py
+++ b/solution.py
@@ -186,7 +186,7 @@
         (one, vir_sum, occ_sum, starts, bases, place_of, integrals)
     )
     far_a = between_chips(one[:cut], [(1, 0), (2, 3)])
-    crossed = other_core(jnp.concatenate([mine, one]))
+    crossed = other_core(jnp.concatenate([integrals, one]))
     raw_x, mine = lax.optimization_barrier((raw_x, mine))
     middle = between_chips(mine, [(1, 2), (2, 1)])
     far_b = between_chips(one[cut:], [(1, 0), (2, 3)])

time: 59.6 us -> 59.6 us (level)
  no operation moved by 1% of the time
where the time goes in v8:
time: 59.6 us; the launch traced here: 59.2 us
  waiting for transfers between devices  22.3 us (37%)
  Pallas kernels  18.5 us (31%)
  starting transfers between devices  13.1 us (22%)
  local copies, waits for them, and re-layouts  2.96 us (5%)
  other arithmetic  2.11 us (4%)
    ppermute x5, waiting for transfers between devices, between_chips(): lax.ppermute(block, 'row', [(2 * a + c, 2 * b + c) for a, b in pairs for...  16.9 us
    ppermute x5, starting transfers between devices, between_chips(): lax.ppermute(block, 'row', [(2 * a + c, 2 * b + c) for a, b in pairs for...  7.31 us
    pallas_call x1, Pallas kernels, ordered(): pl.pallas_call(order_kernel, name='ordered', in_specs=[SMEM, SMEM, SMEM]...  7.22 us
    pallas_call x2, Pallas kernels, energy_sums(): pl.pallas_call(look_up, name=name, out_shape=jax.ShapeDtypeStruct((1, pai...  7.19 us
    ppermute x3, starting transfers between devices, across(): return lax.ppermute(block, 'col', [(i, i ^ mask) for i in range(4)])  5.52 us
    ppermute x3, waiting for transfers between devices, across(): return lax.ppermute(block, 'col', [(i, i ^ mask) for i in range(4)])  4.66 us
    pallas_call x4, Pallas kernels, summed(): pl.pallas_call(functools.partial(product_kernel, first, sizes, total is n...  4.06 us
    unnamed x12, local copies, waits for them, and re-layouts  2.8 us
  transfers between devices with their start and end apart: 12, of which 5 were waited for; matrix products, arithmetic and copies ran while one was open for 4% of the time, Pallas kernels for 29%

profile of v8, /device:TPU:0, one launch (start us, length us, event | category | flops | bytes accessed | tf_op | source)
XLA Modules:
  0.0 59.2 jit_solution(7132387046374110023)
XLA Ops:
  0.0 4.0 %collective-permute-start = (f32[384,512]{1,0:T(8,128)}, f32[384,512]{1,0:T(8,128)S(1)}, u32[]{:S(2)}, u32[]{:S(2)}) collective-permute-start(f32[384,512]{1,0:T(8,128)} %refs_0_.3), channel_id=1, source_target_pairs={{0,16},{4,20},{24,8},{28,12},{8,0},{12,4},{16,24},{20,28},{1,17},{... | collective-permute-start | bytes 2359304 | tf_op jit(solution)/shard_map/ppermute | solution.py:161
  4.0 1.5 %collective-permute-start.1 = (f32[256,768]{1,0:T(8,128)}, f32[256,768]{1,0:T(8,128)S(1)}, u32[]{:S(2)}, u32[]{:S(2)}) collective-permute-start(f32[256,768]{1,0:T(8,128)} %refs_0_.2), channel_id=1, source_target_pairs={{0,1},{1,0},{2,3},{3,2},{4,5},{5,4},{6,7},{7,6},{8,9},{9,8},{10,11... | collective-permute-start | bytes 2359304 | tf_op jit(solution)/shard_map/ppermute | solution.py:167
  5.5 1.5 %collective-permute-start.2 = (f32[256,768]{1,0:T(8,128)}, f32[256,768]{1,0:T(8,128)S(1)}, u32[]{:S(2)}, u32[]{:S(2)}) collective-permute-start(f32[256,768]{1,0:T(8,128)} %refs_0_.2), channel_id=1, source_target_pairs={{0,2},{1,3},{2,0},{3,1},{4,6},{5,7},{6,4},{7,5},{8,10},{9,11},{10,... | collective-permute-start | bytes 2359304 | tf_op jit(solution)/shard_map/ppermute | solution.py:167
  7.1 0.7 %fusion.2 = s32[3072]{0:T(1024)S(1)} fusion(s32[3072]{0:T(1024)} %param.13, s32[]{:T(128)S(6)} %axis_index.22), kind=kLoop, calls=%fused_computation.7 | loop fusion | flops 46080 | bytes 24580 | tf_op jit(solution)/shard_map/add | solution.py:177
  7.8 0.0 copy-start.2
  7.8 0.7 %copy-done.2 = s32[3072,2]{0,1:T(2,128)S(1)} copy-done((s32[3072,2]{0,1:T(2,128)S(1)}, s32[3072,2]{0,1:T(2,128)}, u32[]{:S(2)}) %copy-start.2) | copy-done | bytes 24600
  8.6 0.7 %copy-done.3 = f32[2048]{0:T(1024)S(1)} copy-done((f32[2048]{0:T(1024)S(1)}, f32[2048]{0:T(1024)}, u32[]{:S(2)}) %copy-start.3) | copy-done | bytes 8216
  9.3 7.0 %vir_sums.1.vir_sum = f32[1,3072]{1,0:T(1,128)S(1)} custom-call(f32[16,128]{1,0:T(8,128)S(1)} %bitcast.29, s32[2,3072]{1,0:T(2,128)S(1)} %bitcast.28), custom_call_target="tpu_custom_call" | custom-call | tf_op jit(solution)/shard_map/vir_sums/pallas_call | solution.py:47
  16.3 0.7 %copy-done.4 = s32[256,2]{0,1:T(2,128)S(1)} copy-done((s32[256,2]{0,1:T(2,128)S(1)}, s32[256,2]{0,1:T(2,128)}, u32[]{:S(2)}) %copy-start.4) | copy-done | bytes 2072
  17.0 0.7 %copy-done.5 = f32[256]{0:T(256)S(1)} copy-done((f32[256]{0:T(256)S(1)}, f32[256]{0:T(256)}, u32[]{:S(2)}) %copy-start.5) | copy-done | bytes 1048
  17.7 0.2 occ_sums.1.occ_sum
  17.8 0.1 stack.99.bases
  18.0 0.0 copy-start.1
  18.0 4.4 %collective-permute-done.refs_1_ = f32[384,512]{1,0:T(8,128)S(1)} collective-permute-done((f32[384,512]{1,0:T(8,128)}, f32[384,512]{1,0:T(8,128)S(1)}, u32[]{:S(2)}, u32[]{:S(2)}) %collective-permute-start) | collective-permute-done | bytes 786464 | tf_op jit(solution)/shard_map/ppermute | solution.py:161
  22.3 1.3 %pad_maximum_fusion = f32[768,512]{1,0:T(8,128)S(1)} fusion(f32[384,512]{1,0:T(8,128)S(1)} %collective-permute-done.refs_1_, f32[384,512]{1,0:T(8,128)} %refs_0_.3), kind=kLoop, calls=%fused_computation | loop fusion | flops 393216 | bytes 3145728 | tf_op jit(solution)/shard_map/concatenate | solution.py:189
  23.6 0.1 collective-permute-start.5
  23.7 2.5 %collective-permute-start.3 = (f32[256,768]{1,0:T(8,128)S(1)}, f32[256,768]{1,0:T(8,128)S(1)}, u32[]{:S(2)}, u32[]{:S(2)}) collective-permute-start(f32[256,768]{1,0:T(8,128)S(1)} %copy-done.1), channel_id=1, source_target_pairs={{0,3},{1,2},{2,1},{3,0},{4,7},{5,6},{6,5},{7,4},{8,11},{9,10},{10,... | collective-permute-start | bytes 2359304 | tf_op jit(solution)/shard_map/ppermute | solution.py:167
  26.2 0.7 %collective-permute-start.9 = (f32[384,512]{1,0:T(8,128)S(1)}, f32[384,512]{1,0:T(8,128)S(1)}, u32[]{:S(2)}, u32[]{:S(2)}) collective-permute-start(f32[384,512]{1,0:T(8,128)S(1)} %copy-done), channel_id=1, source_target_pairs={{8,16},{12,20},{16,8},{20,12},{9,17},{13,21},{17,9},{21,13},{10,18... | collective-permute-start | bytes 2359304 | tf_op jit(solution)/shard_map/ppermute | solution.py:161
  27.0 1.3 %collective-permute-start.8 = (f32[256,512]{1,0:T(8,128)S(1)}, f32[256,512]{1,0:T(8,128)S(1)}, u32[]{:S(2)}, u32[]{:S(2)}) collective-permute-start(f32[256,512]{1,0:T(8,128)S(1)} %slice.13), channel_id=1, source_target_pairs={{8,0},{12,4},{16,24},{20,28},{9,1},{13,5},{17,25},{21,29},{10,2},{... | collective-permute-start | bytes 1572872 | tf_op jit(solution)/shard_map/ppermute | solution.py:161
  28.3 11.6 %collective-permute-done.6.refs_2_ = f32[384,512]{1,0:T(8,128)S(1)} collective-permute-done((f32[384,512]{1,0:T(8,128)}, f32[384,512]{1,0:T(8,128)S(1)}, u32[]{:S(2)}, u32[]{:S(2)}) %collective-permute-start.6) | collective-permute-done | bytes 786464 | tf_op jit(solution)/shard_map/ppermute | solution.py:161
  39.9 4.7 %collective-permute-done.3.refs_3_ = f32[256,768]{1,0:T(8,128)S(1)} collective-permute-done((f32[256,768]{1,0:T(8,128)S(1)}, f32[256,768]{1,0:T(8,128)S(1)}, u32[]{:S(2)}, u32[]{:S(2)}) %collective-permute-start.3) | collective-permute-done | bytes 786464 | tf_op jit(solution)/shard_map/ppermute | solution.py:167
  44.5 1.3 %collective-permute-start.4 = (f32[128,512]{1,0:T(8,128)S(1)}, f32[128,512]{1,0:T(8,128)S(1)}, u32[]{:S(2)}, u32[]{:S(2)}) collective-permute-start(f32[128,512]{1,0:T(8,128)S(1)} %slice.12), channel_id=1, source_target_pairs={{8,0},{12,4},{16,24},{20,28},{9,1},{13,5},{17,25},{21,29},{10,2},{... | collective-permute-start | bytes 786440 | tf_op jit(solution)/shard_map/ppermute | solution.py:161
  45.8 7.2 %ordered.1 = (bf16[256,3072]{1,0:T(8,128)(2,1)S(1)}, bf16[256,3072]{1,0:T(8,128)(2,1)S(1)}) custom-call(s32[3072]{0:T(1024)S(1)} %broadcast_multiply_fusion.row_of, s32[4]{0:T(128)S(1)} %xor_multiply_fusion.starts, s32[24]{0:T(128)S(1)} %stack.99.bases, f32[1,256]{1,0:T(1,128)S(1)} %occ_sums.1.occ_sum, f32[1,3072]{1,0:T(1,128)S(1)} %vir_sums.1.vir_sum, ...), custom_call_target="tpu_custom_call" | custom-call | tf_op jit(solution)/shard_map/ordered/pallas_call | solution.py:91
  53.0 1.2 %summed.4.refs_2_ = f32[256,512]{1,0:T(8,128)S(1)} custom-call(bf16[256,3072]{1,0:T(8,128)(2,1)S(1)} %get-tuple-element.28.high, bf16[256,3072]{1,0:T(8,128)(2,1)S(1)} %get-tuple-element.29.low, f32[384,512]{1,0:T(8,128)S(1)} %copy-done, f32[384,512]{1,0:T(8,128)S(1)} %collective-permute-done.refs_1_, f32[384,512]{1,0:T(8,128)S(1)} %collective-permute-done.6.refs_2_), custom_call_target="tpu_custom_call" | custom-call | tf_op jit(solution)/shard_map/summed/pallas_call | solution.py:144
  54.3 0.1 slice_select_fusion.refs_0_
  54.4 0.1 collective-permute-start.11
  54.5 1.1 %summed.5.refs_3_ = f32[256,512]{1,0:T(8,128)S(1)} custom-call(bf16[256,3072]{1,0:T(8,128)(2,1)S(1)} %get-tuple-element.28.high, bf16[256,3072]{1,0:T(8,128)(2,1)S(1)} %get-tuple-element.29.low, f32[768,512]{1,0:T(8,128)S(1)} %collective-permute-done.5.refs_0_, f32[384,512]{1,0:T(8,128)S(1)} %collective-permute-done.7.refs_1_, f32[256,512]{1,0:T(8,128)S(1)} %summed.4.refs_2_), custom_call_target="tpu_custom_call" | custom-call | tf_op jit(solution)/shard_map/summed/pallas_call | solution.py:144
  55.6 1.0 %collective-permute-done.4 = f32[128,512]{1,0:T(8,128)S(1)} collective-permute-done((f32[128,512]{1,0:T(8,128)S(1)}, f32[128,512]{1,0:T(8,128)S(1)}, u32[]{:S(2)}, u32[]{:S(2)}) %collective-permute-start.4) | collective-permute-done | bytes 262176 | tf_op jit(solution)/shard_map/ppermute | solution.py:161
  56.6 0.1 collective-permute-start.10
  56.7 0.7 %summed.6.refs_1_ = f32[256,512]{1,0:T(8,128)S(1)} custom-call(bf16[256,3072]{1,0:T(8,128)(2,1)S(1)} %get-tuple-element.28.high, bf16[256,3072]{1,0:T(8,128)(2,1)S(1)} %get-tuple-element.29.low, f32[256,512]{1,0:T(8,128)S(1)} %slice_select_fusion.refs_0_, f32[256,512]{1,0:T(8,128)S(1)} %collective-permute-done.11.refs_1_, ...), custom_call_target="tpu_custom_call" | custom-call | tf_op jit(solution)/shard_map/summed/pallas_call | solution.py:144
  57.4 0.8 %collective-permute-done.10.refs_0_ = f32[128,512]{1,0:T(8,128)S(1)} collective-permute-done((f32[128,512]{1,0:T(8,128)S(1)}, f32[128,512]{1,0:T(8,128)S(1)}, u32[]{:S(2)}, u32[]{:S(2)}) %collective-permute-start.10) | collective-permute-done | bytes 262176 | tf_op jit(solution)/shard_map/ppermute | solution.py:164
  58.2 1.0 %summed.7 = f32[256,512]{1,0:T(8,128)} custom-call(bf16[256,3072]{1,0:T(8,128)(2,1)S(1)} %get-tuple-element.28.high, bf16[256,3072]{1,0:T(8,128)(2,1)S(1)} %get-tuple-element.29.low, f32[128,512]{1,0:T(8,128)S(1)} %collective-permute-done.10.refs_0_, f32[256,512]{1,0:T(8,128)S(1)} %summed.6.refs_1_), custom_call_target="tpu_custom_call" | custom-call | tf_op jit(solution)/shard_map/summed/pallas_call | solution.py:144
  (20 shorter events, 0.1 us)
Async XLA Ops:
  0.0 22.3 %collective-permute-start = (f32[384,512]{1,0:T(8,128)}, f32[384,512]{1,0:T(8,128)S(1)}, u32[]{:S(2)}, u32[]{:S(2)}) collective-permute-start(f32[384,512]{1,0:T(8,128)} %refs_0_.3), channel_id=1, source_target_pairs={{0,16},{4,20},{24,8},{28,12},{8,0},{12,4},{16,24},{20,28},{1,17},{... | collective-permute-start | bytes 2359304 | tf_op jit(solution)/shard_map/ppermute | solution.py:161
  4.0 22.2 %collective-permute-start.1 = (f32[256,768]{1,0:T(8,128)}, f32[256,768]{1,0:T(8,128)S(1)}, u32[]{:S(2)}, u32[]{:S(2)}) collective-permute-start(f32[256,768]{1,0:T(8,128)} %refs_0_.2), channel_id=1, source_target_pairs={{0,1},{1,0},{2,3},{3,2},{4,5},{5,4},{6,7},{7,6},{8,9},{9,8},{10,11... | collective-permute-start | bytes 2359304 | tf_op jit(solution)/shard_map/ppermute | solution.py:167
  5.5 21.4 %collective-permute-start.2 = (f32[256,768]{1,0:T(8,128)}, f32[256,768]{1,0:T(8,128)S(1)}, u32[]{:S(2)}, u32[]{:S(2)}) collective-permute-start(f32[256,768]{1,0:T(8,128)} %refs_0_.2), channel_id=1, source_target_pairs={{0,2},{1,3},{2,0},{3,1},{4,6},{5,7},{6,4},{7,5},{8,10},{9,11},{10,... | collective-permute-start | bytes 2359304 | tf_op jit(solution)/shard_map/ppermute | solution.py:167
  7.0 32.8 %collective-permute-start.6 = (f32[384,512]{1,0:T(8,128)}, f32[384,512]{1,0:T(8,128)S(1)}, u32[]{:S(2)}, u32[]{:S(2)}) collective-permute-start(f32[384,512]{1,0:T(8,128)} %refs_0_.3), channel_id=1, source_target_pairs={{8,24},{12,28},{16,0},{20,4},{0,8},{4,12},{24,16},{28,20},{9,25},{... | collective-permute-start | bytes 2359304 | tf_op jit(solution)/shard_map/ppermute | solution.py:161
  7.8 0.7 %copy-start.2 = (s32[3072,2]{0,1:T(2,128)S(1)}, s32[3072,2]{0,1:T(2,128)}, u32[]{:S(2)}) copy-start(s32[3072,2]{0,1:T(2,128)} %param.12) | copy-start | bytes 73732
  8.6 0.7 %copy-start.3 = (f32[2048]{0:T(1024)S(1)}, f32[2048]{0:T(1024)}, u32[]{:S(2)}) copy-start(f32[2048]{0:T(1024)} %param.10) | copy-start | bytes 24580
  16.3 0.7 %copy-start.4 = (s32[256,2]{0,1:T(2,128)S(1)}, s32[256,2]{0,1:T(2,128)}, u32[]{:S(2)}) copy-start(s32[256,2]{0,1:T(2,128)} %param.11) | copy-start | bytes 6148
  17.0 0.7 %copy-start.5 = (f32[256]{0:T(256)S(1)}, f32[256]{0:T(256)}, u32[]{:S(2)}) copy-start(f32[256]{0:T(256)} %param.9) | copy-start | bytes 3076
  18.0 5.7 %copy-start.1 = (f32[256,768]{1,0:T(8,128)S(1)}, f32[256,768]{1,0:T(8,128)}, u32[]{:S(2)}) copy-start(f32[256,768]{1,0:T(8,128)} %refs_0_.2) | copy-start | bytes 2359300
  18.0 8.2 %copy-start = (f32[384,512]{1,0:T(8,128)S(1)}, f32[384,512]{1,0:T(8,128)}, u32[]{:S(2)}) copy-start(f32[384,512]{1,0:T(8,128)} %refs_0_.3) | copy-start | bytes 2359300
  23.6 30.8 %collective-permute-start.5 = (f32[768,512]{1,0:T(8,128)S(1)}, f32[768,512]{1,0:T(8,128)S(1)}, u32[]{:S(2)}, u32[]{:S(2)}) collective-permute-start(f32[768,512]{1,0:T(8,128)S(1)} %pad_maximum_fusion), channel_id=1, source_target_pairs={{0,4},{4,0},{8,12},{12,8},{16,20},{20,16},{24,28},{28,24},{1,5},{5... | collective-permute-start | bytes 4718600 | tf_op jit(solution)/shard_map/ppermute | solution.py:164
  23.7 20.8 %collective-permute-start.3 = (f32[256,768]{1,0:T(8,128)S(1)}, f32[256,768]{1,0:T(8,128)S(1)}, u32[]{:S(2)}, u32[]{:S(2)}) collective-permute-start(f32[256,768]{1,0:T(8,128)S(1)} %copy-done.1), channel_id=1, source_target_pairs={{0,3},{1,2},{2,1},{3,0},{4,7},{5,6},{6,5},{7,4},{8,11},{9,10},{10,... | collective-permute-start | bytes 2359304 | tf_op jit(solution)/shard_map/ppermute | solution.py:167
  26.2 28.0 %collective-permute-start.9 = (f32[384,512]{1,0:T(8,128)S(1)}, f32[384,512]{1,0:T(8,128)S(1)}, u32[]{:S(2)}, u32[]{:S(2)}) collective-permute-start(f32[384,512]{1,0:T(8,128)S(1)} %copy-done), channel_id=1, source_target_pairs={{8,16},{12,20},{16,8},{20,12},{9,17},{13,21},{17,9},{21,13},{10,18... | collective-permute-start | bytes 2359304 | tf_op jit(solution)/shard_map/ppermute | solution.py:161
  27.0 27.3 %collective-permute-start.8 = (f32[256,512]{1,0:T(8,128)S(1)}, f32[256,512]{1,0:T(8,128)S(1)}, u32[]{:S(2)}, u32[]{:S(2)}) collective-permute-start(f32[256,512]{1,0:T(8,128)S(1)} %slice.13), channel_id=1, source_target_pairs={{8,0},{12,4},{16,24},{20,28},{9,1},{13,5},{17,25},{21,29},{10,2},{... | collective-permute-start | bytes 1572872 | tf_op jit(solution)/shard_map/ppermute | solution.py:161
  39.8 14.6 %collective-permute-start.7 = (f32[384,512]{1,0:T(8,128)S(1)}, f32[384,512]{1,0:T(8,128)S(1)}, u32[]{:S(2)}, u32[]{:S(2)}) collective-permute-start(f32[384,512]{1,0:T(8,128)S(1)} %collective-permute-done.6.refs_2_), channel_id=1, source_target_pairs={{0,4},{4,0},{8,12},{12,8},{16,20},{20,16},{24,28},{28,24},{1,5},{5... | collective-permute-start | bytes 2359304 | tf_op jit(solution)/shard_map/ppermute | solution.py:164
  44.5 12.0 %collective-permute-start.4 = (f32[128,512]{1,0:T(8,128)S(1)}, f32[128,512]{1,0:T(8,128)S(1)}, u32[]{:S(2)}, u32[]{:S(2)}) collective-permute-start(f32[128,512]{1,0:T(8,128)S(1)} %slice.12), channel_id=1, source_target_pairs={{8,0},{12,4},{16,24},{20,28},{9,1},{13,5},{17,25},{21,29},{10,2},{... | collective-permute-start | bytes 786440 | tf_op jit(solution)/shard_map/ppermute | solution.py:161
  54.4 2.4 %collective-permute-start.11 = (f32[256,512]{1,0:T(8,128)S(1)}, f32[256,512]{1,0:T(8,128)S(1)}, u32[]{:S(2)}, u32[]{:S(2)}) collective-permute-start(f32[256,512]{1,0:T(8,128)S(1)} %slice_select_fusion.refs_0_), channel_id=1, source_target_pairs={{0,4},{4,0},{8,12},{12,8},{16,20},{20,16},{24,28},{28,24},{1,5},{5... | collective-permute-start | bytes 1572872 | tf_op jit(solution)/shard_map/ppermute | solution.py:164
  56.6 1.6 %collective-permute-start.10 = (f32[128,512]{1,0:T(8,128)S(1)}, f32[128,512]{1,0:T(8,128)S(1)}, u32[]{:S(2)}, u32[]{:S(2)}) collective-permute-start(f32[128,512]{1,0:T(8,128)S(1)} %slice_select_fusion.1.refs_2_), channel_id=1, source_target_pairs={{0,4},{4,0},{8,12},{12,8},{16,20},{20,16},{24,28},{28,24},{1,5},{5... | collective-permute-start | bytes 786440 | tf_op jit(solution)/shard_map/ppermute | solution.py:164
